TPU v7x, 128 devices: a whole 4x4x4 slice. The times are simulated.
128 devices in a mesh: section: 8 (over z, y_lo), ctx: 16 (over y_hi, x, core).
Axes of the slice: x: 4, y: 4 (y_hi: 2, y_lo: 2; y = y_hi * 2 + y_lo), z: 4, core: 2. Of those that a mesh axis runs over, the one named last changes fastest.
Arguments:
- query: bfloat16 [8, 6144, 3072], P('section', 'ctx'), may hold values from -200 to 200
- key: bfloat16 [8, 6144, 3072], P('section', 'ctx'), may hold values from -6 to 6
- value: bfloat16 [8, 6144, 3072], P('section', 'ctx'), may hold values from -6 to 6
- out_grad: bfloat16 [8, 6144, 3072], P('section', 'ctx'), may hold values from -6 to 6
- tile_mask: int32 [32, 16], P('ctx'), may hold values from 0 to 1, as said below
Outputs:
- key_grad: bfloat16 [8, 6144, 3072], P('section', 'ctx')
- value_grad: bfloat16 [8, 6144, 3072], P('section', 'ctx')
- upstream: bfloat16 [8, 6144, 3072], P('section', 'ctx')
Inputs may be any that keep to these rules, and one draw needn't show every extreme that they name: `tile_mask`: every query tile a reads the key tile a // 2 of its own image rows; the share of ones differs from one pair of query tiles to the next.
All inputs are finite; a program needn't handle non-finite values.
Results may differ from a plain program's by a relative error of at most 0.014.
The roundings to bfloat16 on the way count: a program that leaves them out, or rounds other values in their place, can miss the bound.
Values may be sent and summed in bfloat16 or wider, within the bound.
No kernel may reach another device: no remote copies, remote signals or barrier semaphores. Data moves between devices by JAX's collectives and lax.ppermute only.
A program may use at most 256 MiB of HBM per device.

v0:
```python
import jax
import jax.numpy as jnp
from jax import lax
from jax.sharding import PartitionSpec as P

HD = 128


def side_by_side(arrays, axis, dim, along):
    widths = [a.shape[along] for a in arrays]
    both = jnp.concatenate(arrays, axis=along)
    result = lax.all_gather(both, axis, axis=dim, tiled=True)
    return tuple(jnp.split(result, [sum(widths[:k]) for k in range(1, len(widths))], axis=along))


def from_behind(value, axis, steps):
    count = lax.axis_size(axis)
    first, last = (max(0, -steps), min(count, count - steps))
    return lax.ppermute(value, axis, [(source, source + steps) for source in range(first, last)])


def pool_band(data, width):
    count = data.shape[0] // (2 * width)
    grid = data.astype(jnp.float32).reshape(count, 2, width // 2, 2, data.shape[1])
    return grid.mean(axis=(1, 3)).reshape(-1, data.shape[1]).astype(jnp.bfloat16)


def unpool_band(pooled, width):
    grid = (pooled / 4.0).reshape(1, 1, width // 2, 1, pooled.shape[1])
    grid = jnp.broadcast_to(grid, (1, 2, width // 2, 2, pooled.shape[1]))
    return grid.reshape(-1, pooled.shape[1]).astype(jnp.bfloat16)


def head_core(qhead, khead, vhead, dhead, allowed):
    scale = 1.0 / HD**0.5
    scores = jnp.dot(qhead, khead.T, preferred_element_type=jnp.float32) * scale
    scores = jnp.where(allowed, scores, -1e30)
    top = jnp.max(scores, axis=1, keepdims=True)
    expo = jnp.exp(scores - top)
    probs = expo / jnp.sum(expo, axis=1, keepdims=True)
    probs_low = probs.astype(jnp.bfloat16)
    attended = jnp.dot(probs_low, vhead, preferred_element_type=jnp.float32)
    delta = jnp.sum(dhead.astype(jnp.float32) * attended, axis=1, keepdims=True)
    dprob = jnp.dot(dhead, vhead.T, preferred_element_type=jnp.float32)
    score_grad = (probs * (dprob - delta) * scale).astype(jnp.bfloat16)
    qgrad = jnp.dot(score_grad, khead, preferred_element_type=jnp.float32).astype(jnp.bfloat16)
    return (qgrad, score_grad, probs_low)


def shards(query, key, value, out_grad, tile_mask):
    local_q = query[0]
    local_k = key[0]
    local_v = value[0]
    local_d = out_grad[0]
    tokens, width_all = local_q.shape
    row_len = tokens // 2
    pooled_key, pooled_value = side_by_side(
        (pool_band(local_k, row_len), pool_band(local_v, row_len)), "ctx", 0, 1
    )
    rows_mask = jnp.repeat(tile_mask, row_len, axis=0)
    allowed = jnp.repeat(rows_mask, row_len // 2, axis=1) > 0
    heads = width_all // HD

    def head_slices(index):
        start = index * HD
        qh = lax.dynamic_slice_in_dim(local_q, start, HD, 1)
        kh = lax.dynamic_slice_in_dim(pooled_key, start, HD, 1)
        vh = lax.dynamic_slice_in_dim(pooled_value, start, HD, 1)
        dh = lax.dynamic_slice_in_dim(local_d, start, HD, 1)
        return (qh, kh, vh, dh)

    def per_head_kept(index):
        qh, kh, vh, dh = head_slices(index)
        return head_core(qh, kh, vh, dh, allowed)

    qgrad, score_all, probs_all = lax.map(per_head_kept, jnp.arange(heads, dtype=jnp.int32))
    qgrad = jnp.transpose(qgrad, (1, 0, 2)).reshape(tokens, width_all)
    query_heads = local_q.reshape(tokens, heads, HD)
    grad_heads = local_d.reshape(tokens, heads, HD)
    kpart = jnp.einsum("htk,thd->khd", score_all, query_heads, preferred_element_type=jnp.float32)
    vpart = jnp.einsum("htk,thd->khd", probs_all, grad_heads, preferred_element_type=jnp.float32)
    summed = lax.psum_scatter(
        jnp.concatenate(
            [
                kpart.reshape(row_len // 2 * lax.axis_size("ctx"), width_all),
                vpart.reshape(row_len // 2 * lax.axis_size("ctx"), width_all),
            ],
            axis=1,
        ).astype(jnp.bfloat16),
        "ctx",
        scatter_dimension=0,
        tiled=True,
    ).astype(jnp.float32)
    kgrad = summed[:, :width_all]
    vgrad = summed[:, width_all:]
    upstream = from_behind(qgrad, "section", -1)
    key_grad = unpool_band(kgrad, row_len)
    value_grad = unpool_band(vgrad, row_len)
    return (key_grad[None], value_grad[None], upstream[None])


def solution(mesh):
    return jax.shard_map(
        shards,
        mesh=mesh,
        in_specs=(
            P("section", "ctx", None),
            P("section", "ctx", None),
            P("section", "ctx", None),
            P("section", "ctx", None),
            P("ctx", None),
        ),
        out_specs=(P("section", "ctx", None), P("section", "ctx", None), P("section", "ctx", None)),
        check_vma=False,
    )
```

profile of v0, /device:TPU:56, one launch (start us, length us, event | category | flops | bytes accessed | tf_op | source)
XLA Modules:
  0.0 725.7 jit_solution(3157595229878676443)
XLA Ops:
  7.2 6.3 reshape.109
  13.5 4.2 reshape.110
  17.8 5.7 reduce_sum.36
  23.5 5.7 reduce_sum.37
  30.8 3.0 copy.23
  34.1 4.3 copy.30
  38.4 112.3 %all-gather.2.cloned.1.call-done = bf16[1536,6144]{1,0:T(8,128)(2,1)} async-done(((bf16[96,6144]{1,0:T(8,128)(2,1)}), bf16[1536,6144]{1,0:T(8,128)(2,1)}) %all-gather.2.cloned.1.call-update) | async-done | bytes 18874384 | tf_op jit(solution)/shard_map/all_gather | solution.py:12
  150.7 14.4 %fusion.26 = (bf16[1536,3072]{1,0:T(8,128)(2,1)}, bf16[1536,3072]{1,0:T(8,128)(2,1)}) fusion(bf16[1536,6144]{1,0:T(8,128)(2,1)} %all-gather.2.cloned.1.call-done), kind=kLoop, calls=%fused_computation.41 | loop fusion | bytes 37748736 | tf_op jit(solution)/shard_map/split | solution.py:13
  165.1 300.6 %while.15 = (s32[]{:T(128)}, bf16[24,384,128]{2,1,0:T(8,128)(2,1)}, bf16[24,384,1536]{2,1,0:T(8,128)(2,1)}, bf16[24,384,1536]{2,1,0:T(8,128)(2,1)}, s32[24]{0:T(...) while((s32[]{:T(128)}, bf16[24,384,128]{2,1,0:T(8,128)(2,1)}, ...), condition=%wide.region_6.7_spmd.clone, body=%wide.region_2.6_spmd.clone.sunk | while | flops 614202240 | bytes 20869828 | solution.py:76
  172.6 2.9 bitcast_dynamic-update-slice_fusion.4
  175.5 2.1 fusion.48
  185.1 2.9 bitcast_dynamic-update-slice_fusion.4
  188.1 2.1 fusion.48
  197.7 2.9 bitcast_dynamic-update-slice_fusion.4
  200.6 2.1 fusion.48
  210.2 2.9 bitcast_dynamic-update-slice_fusion.4
  213.1 2.1 fusion.48
  222.7 3.0 bitcast_dynamic-update-slice_fusion.4
  225.7 2.1 fusion.48
  235.2 2.9 bitcast_dynamic-update-slice_fusion.4
  238.2 2.1 fusion.48
  247.7 2.9 bitcast_dynamic-update-slice_fusion.4
  250.6 2.1 fusion.48
  260.2 3.0 bitcast_dynamic-update-slice_fusion.4
  263.3 2.1 fusion.48
  272.8 2.9 bitcast_dynamic-update-slice_fusion.4
  275.7 2.1 fusion.48
  285.3 2.9 bitcast_dynamic-update-slice_fusion.4
  288.2 2.1 fusion.48
  297.8 3.0 bitcast_dynamic-update-slice_fusion.4
  300.7 2.1 fusion.48
  310.4 3.0 bitcast_dynamic-update-slice_fusion.4
  313.3 2.1 fusion.48
  322.9 2.9 bitcast_dynamic-update-slice_fusion.4
  335.4 2.9 bitcast_dynamic-update-slice_fusion.4
  347.9 2.9 bitcast_dynamic-update-slice_fusion.4
  360.5 3.0 bitcast_dynamic-update-slice_fusion.4
  363.4 2.1 fusion.48
  373.0 2.9 bitcast_dynamic-update-slice_fusion.4
  376.0 2.1 fusion.48
  385.6 2.9 bitcast_dynamic-update-slice_fusion.4
  388.5 2.1 fusion.48
  398.1 2.9 bitcast_dynamic-update-slice_fusion.4
  410.6 2.9 bitcast_dynamic-update-slice_fusion.4
  413.6 2.1 fusion.48
  423.1 2.9 bitcast_dynamic-update-slice_fusion.4
  426.0 2.1 fusion.48
  435.6 3.0 bitcast_dynamic-update-slice_fusion.4
  438.6 2.1 fusion.48
  448.2 2.9 bitcast_dynamic-update-slice_fusion.4
  451.1 2.1 fusion.48
  460.7 2.9 bitcast_dynamic-update-slice_fusion.4
  463.6 2.1 fusion.48
  465.7 14.9 %convolution_convert_fusion.1 = bf16[24,1536,128]{1,2,0:T(8,128)(2,1)} fusion(bf16[384,24,128]{0,2,1:T(8,128)(2,1)S(1)} %bitcast.50, bf16[24,384,1536]{2,1,0:T(8,128)(2,1)} %get-tuple-element.58), kind=kOutput, calls=%fused_computation.29 | convolution fusion | flops 3628597248 | bytes 40108032 | tf_op jit(solution)/shard_map/htk,thd->khd/dot_general | solution.py:81
  480.5 12.8 %copy.28 = bf16[1536,3072]{1,0:T(8,128)(2,1)} copy(bf16[1536,3072]{0,1:T(8,128)(2,1)} %bitcast.47) | data formatting | bytes 18874368 | tf_op jit(solution)/shard_map/reshape | solution.py:86
  493.4 14.8 %convolution_convert_fusion.2 = bf16[24,1536,128]{1,2,0:T(8,128)(2,1)} fusion(bf16[384,24,128]{0,2,1:T(8,128)(2,1)S(1)} %bitcast.51, bf16[24,384,1536]{2,1,0:T(8,128)(2,1)} %get-tuple-element.57), kind=kOutput, calls=%fused_computation.30 | convolution fusion | flops 3628597248 | bytes 40108032 | tf_op jit(solution)/shard_map/htk,thd->khd/dot_general | solution.py:80
  508.2 12.7 %copy.27 = bf16[1536,3072]{1,0:T(8,128)(2,1)} copy(bf16[1536,3072]{0,1:T(8,128)(2,1)} %bitcast.48) | data formatting | bytes 18874368 | tf_op jit(solution)/shard_map/reshape | solution.py:85
  520.9 16.5 %pad_maximum_fusion = bf16[1536,6144]{1,0:T(8,128)(2,1)} fusion(bf16[1536,3072]{1,0:T(8,128)(2,1)} %copy.28, bf16[1536,3072]{1,0:T(8,128)(2,1)} %copy.27), kind=kLoop, calls=%fused_computation.28 | loop fusion | flops 37748736 | bytes 37748736 | tf_op jit(solution)/shard_map/concatenate | solution.py:83
  539.5 2.1 collective-permute-start
  541.6 66.8 %collective-permute-done = bf16[384,3072]{1,0:T(8,128)(2,1)} collective-permute-done((bf16[384,3072]{1,0:T(8,128)(2,1)S(1)}, bf16[384,3072]{1,0:T(8,128)(2,1)}, u32[]{:S(2)}, u32[]{:S(2)}) %collective-permute-start) | collective-permute-done | bytes 2359328 | tf_op jit(solution)/shard_map/ppermute | solution.py:19
  608.4 98.5 %reduce-scatter.2.cloned.1.call-done = bf16[96,6144]{1,0:T(8,128)(2,1)} async-done(((bf16[1536,6144]{1,0:T(8,128)(2,1)}), bf16[96,6144]{1,0:T(8,128)(2,1)}) %reduce-scatter.2.cloned.1.call-update) | async-done | bytes 1179664 | tf_op jit(solution)/shard_map/reduce_scatter | solution.py:82
  709.8 2.3 convert_element_type.90
  713.3 2.3 convert_element_type.92
  715.7 3.2 copy.53
  (199 shorter events, 179.5 us)
Async XLA Ops:
  7.2 6.3 copy-start.1
  7.2 143.5 %all-gather.2.cloned.1.call-start = ((), (), s32[]{:S(2)}) async-start(), calls=%async_computation.1 | async-start | bytes 20054016 | tf_op jit(solution)/shard_map/all_gather | solution.py:12
  30.5 676.4 %reduce-scatter.2.cloned.1.call-start = ((), (), s32[]{:S(2)}) async-start(), calls=%async_computation.2 | async-start | bytes 20054016 | tf_op jit(solution)/shard_map/reduce_scatter | solution.py:82
  30.8 3.0 copy-start.3
  480.5 12.8 %copy-start = (bf16[1,384,3072]{1,2,0:T(8,128)(2,1)S(1)}, bf16[1,384,3072]{1,2,0:T(8,128)(2,1)}, u32[]{:S(2)}) copy-start(bf16[1,384,3072]{1,2,0:T(8,128)(2,1)} %copy.30) | copy-start | bytes 7077892
  537.4 1.7 copy-start.2
  539.5 68.9 %collective-permute-start = (bf16[384,3072]{1,0:T(8,128)(2,1)S(1)}, bf16[384,3072]{1,0:T(8,128)(2,1)}, u32[]{:S(2)}, u32[]{:S(2)}) collective-permute-start(bf16[384,3072]{1,0:T(8,128)(2,1)S(1)} %copy_bitcast_fusion), channel_id=1, source_target_pairs={{16,0},{32,16},{48,32},{64,48},{80,64},{96,80},{112,96},{17,1},{33... | collective-permute-start | bytes 7077896 | tf_op jit(solution)/shard_map/ppermute | solution.py:19
Sparse Core Ops, SparseCore 0:
  30.6 120.0 all-gather.1
  537.6 169.2 reduce-scatter.1
where the time goes:
time: 733 us; the launch traced here: 726 us
  waiting for transfers between devices  278 us (38%)
  matrix products  233 us (32%)
  local copies, waits for them, and re-layouts  104 us (14%)
  other arithmetic  78.2 us (11%)
  loops' own time  16.2 us (2%)
  between operations  14.2 us (2%)
    all_gather x1, waiting for transfers between devices, side_by_side(): result = lax.all_gather(both, axis, axis=dim, tiled=True)  112 us
    reduce_scatter x1, waiting for transfers between devices, shards(): lax.psum_scatter(jnp.concatenate([kpart.reshape(row_len // 2 * lax.axis_s...  98.5 us
    dot_general x24, matrix products, head_core(): dprob = jnp.dot(dhead, vhead.T, preferred_element_type=jnp.float32)  70.5 us
    ppermute x1, waiting for transfers between devices, from_behind(): lax.ppermute(value, axis, [(source, source + steps) for source in range(f...  66.8 us
    dot_general x24, matrix products, head_core(): jnp.dot(score_grad, khead, preferred_element_type=jnp.float32)  50.7 us
    dot_general x24, matrix products, head_core(): attended = jnp.dot(probs_low, vhead, preferred_element_type=jnp.float32)  40.8 us
    dot_general x24, matrix products, head_core(): scores = jnp.dot(qhead, khead.T, preferred_element_type=jnp.float32) * scale  40.8 us
    dynamic_update_slice x24, other arithmetic, shards(): lax.map(per_head_kept, jnp.arange(heads, dtype=jnp.int32))  36.1 us
  transfers between devices with their start and end apart: 3, of which 3 were waited for; matrix products, arithmetic and copies ran while one was open for 1% of the time, Pallas kernels for 0%

commit v1 on v0

v1 whole, which is shorter than its diff:
```python
import functools

import jax
import jax.numpy as jnp
from jax import lax
from jax.experimental import pallas as pl
from jax.experimental.pallas import tpu as pltpu
from jax.sharding import PartitionSpec as P

HD = 128
CHIPS = 8
CORES = 2
HEADS_CHIP = 3
TOK = 384
POOL = 96
ROW = 192
WIDE = HEADS_CHIP * HD
KTILES = CHIPS * CORES
KEYS = KTILES * POOL
SCALE = 1.0 / HD**0.5
LOG2E = 1.4426950408889634
BLOCKED = -1e30
NN = (((1,), (0,)), ((), ()))
NT = (((1,), (1,)), ((), ()))
TN = (((0,), (0,)), ((), ()))


def dot(a, b, dims):
    return lax.dot_general(a, b, dims, preferred_element_type=jnp.float32)


def pool_matrix(shape, token_dim):
    token = lax.broadcasted_iota(jnp.int32, shape, token_dim)
    pooled = lax.broadcasted_iota(jnp.int32, shape, 1 - token_dim)
    column = jnp.where(token >= ROW, token - ROW, token)
    return jnp.where(column // 2 == pooled, 1.0, 0.0).astype(jnp.bfloat16)


def pack_kernel(q_ref, k_ref, v_ref, d_ref, bias_ref, kv_out, qd_out):
    pool = pool_matrix((POOL, TOK), 1)
    kv_out[0, :POOL] = (dot(pool, k_ref[0], NN) * 0.25).astype(jnp.bfloat16)
    kv_out[0, POOL : 2 * POOL] = (dot(pool, v_ref[0], NN) * 0.25).astype(jnp.bfloat16)
    kv_out[0, 2 * POOL :] = bias_ref[...]
    qd_out[0, :TOK] = q_ref[0]
    qd_out[0, TOK:] = d_ref[0]


def pack(query, key, value, out_grad, bias):
    column = pl.BlockSpec((1, TOK, WIDE), lambda j: (0, 0, j))
    return pl.pallas_call(
        pack_kernel,
        grid=(CHIPS,),
        in_specs=[column] * 4 + [pl.BlockSpec((KTILES, TOK), lambda j: (0, 0))],
        out_specs=[
            pl.BlockSpec((1, 2 * POOL + KTILES, WIDE), lambda j: (j, 0, 0)),
            pl.BlockSpec((1, 2 * TOK, WIDE), lambda j: (j, 0, 0)),
        ],
        out_shape=[
            jax.ShapeDtypeStruct((CHIPS, 2 * POOL + KTILES, WIDE), jnp.bfloat16),
            jax.ShapeDtypeStruct((CHIPS, 2 * TOK, WIDE), jnp.bfloat16),
        ],
        name="pack",
    )(query, key, value, out_grad, bias)


def attend_kernel(order_ref, q_ref, d_ref, own_ref, other_ref, bias_ref, *rest):
    dq_refs = rest[:CHIPS]
    dkv_own, dkv_other, keys, values, dkeys, dvalues, expo, dprob = rest[CHIPS:]
    step = pl.program_id(0)

    @pl.when(step == 0)
    def _():
        for s in range(CHIPS):
            for half, ref in enumerate((own_ref, other_ref)):
                at = (half * CHIPS + s) * POOL
                keys[at : at + POOL] = ref[s, :POOL]
                values[at : at + POOL] = ref[s, POOL:]
        dkeys[...] = jnp.zeros_like(dkeys)
        dvalues[...] = jnp.zeros_like(dvalues)

    q = q_ref[0]
    d = d_ref[0]
    part = 4 * POOL
    top = jnp.full((8, TOK), -3e38, jnp.float32)
    for at in range(0, KEYS, part):
        scores = dot(keys[at : at + part], q, NT)
        for tile in range(part // POOL):
            row = at // POOL + tile
            bias = bias_ref[0, row : row + 1].astype(jnp.float32)
            one = scores[tile * POOL : (tile + 1) * POOL] + bias
            expo[at + tile * POOL : at + (tile + 1) * POOL] = one
            top = jnp.maximum(top, jnp.max(one.reshape(POOL // 8, 8, TOK), axis=0))
    top = jnp.max(top, axis=0, keepdims=True)
    total = jnp.zeros((8, TOK), jnp.float32)
    weighted = jnp.zeros((8, TOK), jnp.float32)
    for at in range(0, KEYS, part):
        grad = dot(values[at : at + part], d, NT)
        e = jnp.exp2((expo[at : at + part] - top) * (SCALE * LOG2E))
        expo[at : at + part] = e
        dprob[at : at + part] = grad
        total = total + jnp.sum(e.reshape(part // 8, 8, TOK), axis=0)
        weighted = weighted + jnp.sum((e * grad).reshape(part // 8, 8, TOK), axis=0)
    inverse = 1.0 / jnp.sum(total, axis=0, keepdims=True)
    delta = jnp.sum(weighted, axis=0, keepdims=True) * inverse
    scaled = inverse * SCALE
    dq = jnp.zeros((TOK, HD), jnp.float32)
    for at in range(0, KEYS, part):
        e = expo[at : at + part]
        probs = (e * inverse).astype(jnp.bfloat16)
        sgrad = ((e * scaled) * (dprob[at : at + part] - delta)).astype(jnp.bfloat16)
        dvalues[at : at + part] += dot(probs, d, NN)
        dkeys[at : at + part] += dot(sgrad, q, NN)
        dq = dq + dot(sgrad, keys[at : at + part], TN)
    for k in range(CHIPS):

        @pl.when(step == k)
        def _():
            dq_refs[k][...] = dq.astype(jnp.bfloat16)

    @pl.when(step == CHIPS - 1)
    def _():
        for s in range(CHIPS):
            at = s * POOL
            dkv_own[s, :POOL] = dkeys[at : at + POOL]
            dkv_own[s, POOL:] = dvalues[at : at + POOL]
            at = (CHIPS + s) * POOL
            dkv_other[s, :POOL] = dkeys[at : at + POOL].astype(jnp.bfloat16)
            dkv_other[s, POOL:] = dvalues[at : at + POOL].astype(jnp.bfloat16)


def attend(order, qd, kv_own, kv_other, head):
    whole = lambda k, order: (0, 0, 0)
    return pl.pallas_call(
        attend_kernel,
        grid_spec=pltpu.PrefetchScalarGridSpec(
            num_scalar_prefetch=1,
            grid=(CHIPS,),
            in_specs=[
                pl.BlockSpec((1, TOK, HD), lambda k, order: (order[k], 0, head)),
                pl.BlockSpec((1, TOK, HD), lambda k, order: (order[k], 1, head)),
                pl.BlockSpec((CHIPS, 2 * POOL, HD), lambda k, order: (0, 0, head)),
                pl.BlockSpec((CHIPS, 2 * POOL, HD), lambda k, order: (0, 0, head)),
                pl.BlockSpec((1, KTILES, TOK), lambda k, order: (order[k], 2 * POOL // KTILES, 0)),
            ],
            out_specs=[pl.BlockSpec((TOK, HD), lambda k, order: (0, 0))] * CHIPS
            + [pl.BlockSpec((CHIPS, 2 * POOL, HD), whole)] * 2,
            scratch_shapes=[
                pltpu.VMEM((KEYS, HD), jnp.bfloat16),
                pltpu.VMEM((KEYS, HD), jnp.bfloat16),
                pltpu.VMEM((KEYS, HD), jnp.float32),
                pltpu.VMEM((KEYS, HD), jnp.float32),
                pltpu.VMEM((KEYS, TOK), jnp.float32),
                pltpu.VMEM((KEYS, TOK), jnp.float32),
            ],
        ),
        out_shape=[jax.ShapeDtypeStruct((TOK, HD), jnp.bfloat16)] * CHIPS
        + [
            jax.ShapeDtypeStruct((CHIPS, 2 * POOL, HD), jnp.float32),
            jax.ShapeDtypeStruct((CHIPS, 2 * POOL, HD), jnp.bfloat16),
        ],
        compiler_params=pltpu.CompilerParams(vmem_limit_bytes=40 * 2**20),
        cost_estimate=pl.CostEstimate(
            flops=10 * CHIPS * TOK * KEYS * HD,
            bytes_accessed=6 * 2**20,
            transcendentals=CHIPS * TOK * KEYS,
        ),
        name="attend",
    )(order, qd, qd, kv_own, kv_other, kv_own)


def unpool_kernel(dkv_ref, dk_ref, dv_ref):
    spread = pool_matrix((TOK, POOL), 0)
    dk_ref[0] = (dot(spread, dkv_ref[0, :POOL], NN) * 0.25).astype(jnp.bfloat16)
    dv_ref[0] = (dot(spread, dkv_ref[0, POOL:], NN) * 0.25).astype(jnp.bfloat16)


def unpool(dkv):
    column = pl.BlockSpec((1, TOK, WIDE), lambda j: (0, 0, j))
    whole = jax.ShapeDtypeStruct((1, TOK, CHIPS * WIDE), jnp.bfloat16)
    return pl.pallas_call(
        unpool_kernel,
        grid=(CHIPS,),
        in_specs=[pl.BlockSpec((1, 2 * POOL, WIDE), lambda j: (j, 0, 0))],
        out_specs=[column, column],
        out_shape=[whole, whole],
        name="unpool",
    )(dkv)


def place_kernel(order_ref, *refs):
    pieces, out_ref = refs[:-1], refs[-1]
    step = pl.program_id(0)
    for k in range(CHIPS):

        @pl.when(step == k)
        def _():
            for head in range(HEADS_CHIP):
                out_ref[0, :, head * HD : (head + 1) * HD] = pieces[head * CHIPS + k][...]


def place(order, pieces):
    return pl.pallas_call(
        place_kernel,
        grid_spec=pltpu.PrefetchScalarGridSpec(
            num_scalar_prefetch=1,
            grid=(CHIPS,),
            in_specs=[pl.BlockSpec((TOK, HD), lambda k, order: (0, 0))] * len(pieces),
            out_specs=pl.BlockSpec((1, TOK, WIDE), lambda k, order: (0, 0, order[k])),
        ),
        out_shape=jax.ShapeDtypeStruct((1, TOK, CHIPS * WIDE), jnp.bfloat16),
        compiler_params=pltpu.CompilerParams(vmem_limit_bytes=24 * 2**20),
        name="place",
    )(order, *pieces)


def turned(chip, k, sign):
    outer, inner = k // 4, k % 4
    return (chip // 4 + sign * outer) % 2 * 4 + (chip % 4 + sign * inner) % 4


def shards(query, key, value, out_grad, tile_mask, sections):
    here = lax.axis_index("ctx")
    chip, core = here // CORES, here % CORES
    by_core = tile_mask.reshape(2, CHIPS, CORES)
    own_first = jnp.where(core == 0, by_core, by_core[:, :, ::-1])
    own_first = own_first.transpose(2, 1, 0).reshape(KTILES, 2)
    bias = jnp.where(jnp.repeat(own_first, ROW, axis=1) > 0, 0.0, BLOCKED).astype(jnp.bfloat16)
    kv, qd = pack(query, key, value, out_grad, bias)
    groups = [list(range(c, CHIPS * CORES, CORES)) for c in range(CORES)]
    trade = functools.partial(
        lax.all_to_all, axis_name="ctx", split_axis=0, concat_axis=0, axis_index_groups=groups, tiled=True
    )
    swap = functools.partial(
        lax.ppermute, axis_name="ctx", perm=[(i, i ^ 1) for i in range(CHIPS * CORES)]
    )
    kv_own = trade(kv)
    kv_other = swap(kv_own)
    qd = trade(qd)
    ahead = jnp.stack([turned(chip, k, 1) for k in range(CHIPS)]).astype(jnp.int32)
    behind = jnp.stack([turned(chip, k, -1) for k in range(CHIPS)]).astype(jnp.int32)
    pieces, own_terms, other_terms = [], [], []
    for head in range(HEADS_CHIP):
        *dq, dkv_own, dkv_other = attend(ahead, qd, kv_own, kv_other, head)
        for k in range(CHIPS):
            pairs = [
                (
                    section * KTILES + s * CORES + c,
                    (section - 1) * KTILES + turned(s, k, 1) * CORES + c,
                )
                for section in range(1, sections)
                for s in range(CHIPS)
                for c in range(CORES)
            ]
            pieces.append(lax.ppermute(dq[k], ("section", "ctx"), pairs))
        own_terms.append(dkv_own)
        other_terms.append(swap(dkv_other))
    dkv = [(a + b.astype(jnp.float32)).astype(jnp.bfloat16) for a, b in zip(own_terms, other_terms)]
    dkv = trade(jnp.concatenate(dkv, axis=2))
    key_grad, value_grad = unpool(dkv)
    upstream = place(behind, pieces)
    return key_grad, value_grad, upstream


def solution(mesh):
    spec = P("section", "ctx", None)
    return jax.shard_map(
        functools.partial(shards, sections=mesh.shape["section"]),
        mesh=mesh,
        in_specs=(spec, spec, spec, spec, P("ctx", None)),
        out_specs=(spec, spec, spec),
        check_vma=False,
    )
```

time: 733 us -> 290 us (0.40)
  matrix products: 233 us -> 0 us
  waiting for transfers between devices: 278 us -> 62.7 us
  starting transfers between devices: 2.4 us -> 108 us
  local copies, waits for them, and re-layouts: 104 us -> 2.05 us
  Pallas kernels: 0 us -> 84.8 us
  other arithmetic: 78.2 us -> 1.43 us
  blocking collectives: 0 us -> 24 us
  loops' own time: 16.2 us -> 0 us
  between operations: 14.2 us -> 1.52 us
    dot_general x98 -> x0, matrix products: 233 us -> none  [the longest x24 70.5 us: head_core(): dprob = jnp.dot(dhead, vhead.T, preferred_element_type=jnp.float32)]
    all_gather x1 -> x0, waiting for transfers between devices: 112 us -> none  [side_by_side(): result = lax.all_gather(both, axis, axis=dim, tiled=True)]
    reduce_scatter x1 -> x0, waiting for transfers between devices: 98.5 us -> none  [shards(): lax.psum_scatter(jnp.concatenate([kpart.reshape(row_len // 2 * lax.axis_s...]
    pallas_call x0 -> x6, Pallas kernels: none -> 84.8 us  [the longest x3 65.2 us: attend(): pl.pallas_call(attend_kernel, grid_spec=pltpu.PrefetchScalarGridSpec(num_...]
    ppermute x1 -> x28, starting transfers between devices: 2.14 us -> 79.6 us  [the longest x24 78.8 us: shards(): pieces.append(lax.ppermute(dq[k], ('section', 'ctx'), pairs))]
    ppermute x1 -> x28, waiting for transfers between devices: 66.8 us -> 12.8 us  [the longest x24 8.4 us: shards(): pieces.append(lax.ppermute(dq[k], ('section', 'ctx'), pairs))]
    all_to_all x0 -> x2, waiting for transfers between devices: none -> 49.9 us  [the longest x1 49.9 us: shards(): qd = trade(qd)]
    dynamic_update_slice x24 -> x0, other arithmetic: 36.1 us -> none  [shards(): lax.map(per_head_kept, jnp.arange(heads, dtype=jnp.int32))]
  transfers between devices with their start and end apart: 3 -> 30, of which waited for: 3 -> 9; matrix products, arithmetic and copies ran while one was open for 1% -> 0% of each run, Pallas kernels for 0% -> 17%
where the time goes in v1:
time: 290 us; the launch traced here: 284 us
  starting transfers between devices  108 us (37%)
  Pallas kernels  84.8 us (29%)
  waiting for transfers between devices  62.7 us (22%)
  blocking collectives  24 us (8%)
    ppermute x24, starting transfers between devices, shards(): pieces.append(lax.ppermute(dq[k], ('section', 'ctx'), pairs))  78.8 us
    pallas_call x3, Pallas kernels, attend(): pl.pallas_call(attend_kernel, grid_spec=pltpu.PrefetchScalarGridSpec(num_...  65.2 us
    all_to_all x1, waiting for transfers between devices, shards(): qd = trade(qd)  49.9 us
    all_to_all x1, blocking collectives, shards(): kv_own = trade(kv)  24 us
    all_to_all x1, starting transfers between devices, shards(): dkv = trade(jnp.concatenate(dkv, axis=2))  20.7 us
    pallas_call x1, Pallas kernels, pack(): pl.pallas_call(pack_kernel, grid=(CHIPS,), in_specs=[column] * 4 + [pl.Bl...  8.95 us
    ppermute x24, waiting for transfers between devices, shards(): pieces.append(lax.ppermute(dq[k], ('section', 'ctx'), pairs))  8.4 us
    all_to_all x1, starting transfers between devices, shards(): qd = trade(qd)  7.48 us
  transfers between devices with their start and end apart: 30, of which 9 were waited for; matrix products, arithmetic and copies ran while one was open for 0% of the time, Pallas kernels for 17%

profile of v1, /device:TPU:56, one launch (start us, length us, event | category | flops | bytes accessed | tf_op | source)
XLA Modules:
  0.0 284.1 jit_solution(12192055406869509896)
XLA Ops:
  0.6 0.8 reshape.23
  1.4 0.1 rev.3
  1.5 0.1 copy.12
  1.6 0.1 broadcast_in_dim.13
  1.7 0.7 convert_element_type.24.bias_ref
  2.4 9.0 %pack.1 = (bf16[8,208,384]{2,1,0:T(8,128)(2,1)}, bf16[8,768,384]{2,1,0:T(8,128)(2,1)}) custom-call(bf16[1,384,3072]{2,1,0:T(8,128)(2,1)} %q_ref.1, bf16[1,384,3072]{2,1,0:T(8,128)(2,1)} %k_ref.1, bf16[1,384,3072]{2,1,0:T(8,128)(2,1)} %v_ref.1, bf16[1,384,3072]{2,1,0:T(8,128)(2,1)} %d_ref.1, bf16[16,384]{1,0:T(8,128)(2,1)} %convert_element_type.24.bias_ref), custom_call_target="tpu_custom_call" | custom-call | tf_op jit(solution)/shard_map/pack/pallas_call | solution.py:50
  11.4 24.0 %all_to_all.15.own_ref.bias_ref = bf16[8,208,384]{2,1,0:T(8,128)(2,1)S(1)} all-to-all(bf16[8,208,384]{2,1,0:T(8,128)(2,1)} %get-tuple-element.38), channel_id=1, replica_groups={{0,2,4,6,8,10,12,14},{1,3,5,7,9,11,13,15},{16,18,20,22,24,26,28,30},{17..., dimensions={0} | all-to-all | bytes 2555904 | tf_op jit(solution)/shard_map/all_to_all | solution.py:236
  35.3 7.5 %all-to-all-start = ((bf16[8,768,384]{2,1,0:T(8,128)(2,1)}), bf16[8,768,384]{2,1,0:T(8,128)(2,1)}, u32[]{:S(2)}, u32[]{:S(2)}) async-start(bf16[8,768,384]{2,1,0:T(8,128)(2,1)} %get-tuple-element.37), calls=%async_computation | async-start | bytes 9437184 | tf_op jit(solution)/shard_map/all_to_all | solution.py:238
  42.8 0.1 stack.60.order_ref
  42.9 2.9 %collective-permute-done.other_ref = bf16[8,208,384]{2,1,0:T(8,128)(2,1)S(1)} collective-permute-done((bf16[8,208,384]{2,1,0:T(8,128)(2,1)S(1)}, bf16[8,208,384]{2,1,0:T(8,128)(2,1)S(1)}, u32[]{:S(2)}, u32[]{:S(2)}) %collective-permute-start) | collective-permute-done | bytes 1277984 | tf_op jit(solution)/shard_map/ppermute | solution.py:237
  45.8 49.9 %all-to-all-done.q_ref.d_ref = bf16[8,768,384]{2,1,0:T(8,128)(2,1)} async-done(((bf16[8,768,384]{2,1,0:T(8,128)(2,1)}), bf16[8,768,384]{2,1,0:T(8,128)(2,1)}, u32[]{:S(2)}, u32[]{:S(2)}) %all-to-all-start) | async-done | bytes 4718624 | tf_op jit(solution)/shard_map/all_to_all | solution.py:238
  95.6 21.7 %attend.5 = (bf16[384,128]{1,0:T(8,128)(2,1)S(1)}, bf16[384,128]{1,0:T(8,128)(2,1)S(1)}, bf16[384,128]{1,0:T(8,128)(2,1)S(1)}, bf16[384,128]{1,0:T(8,128)(2,1)S(...) custom-call(s32[8]{0:T(128)S(1)} %stack.60.order_ref, ...), custom_call_target="tpu_custom_call" | custom-call | flops 6039797760 | bytes 6291456 | tf_op jit(solution)/shard_map/attend/pallas_call | solution.py:133
  117.4 0.1 collective-permute-start.3
  117.5 21.8 %attend.4 = (bf16[384,128]{1,0:T(8,128)(2,1)S(1)}, bf16[384,128]{1,0:T(8,128)(2,1)S(1)}, bf16[384,128]{1,0:T(8,128)(2,1)S(1)}, bf16[384,128]{1,0:T(8,128)(2,1)S(...) custom-call(s32[8]{0:T(128)S(1)} %stack.60.order_ref, ...), custom_call_target="tpu_custom_call" | custom-call | flops 6039797760 | bytes 6291456 | tf_op jit(solution)/shard_map/attend/pallas_call | solution.py:133
  139.3 0.6 collective-permute-start.2
  139.9 21.7 %attend.3 = (bf16[384,128]{1,0:T(8,128)(2,1)S(1)}, bf16[384,128]{1,0:T(8,128)(2,1)S(1)}, bf16[384,128]{1,0:T(8,128)(2,1)S(1)}, bf16[384,128]{1,0:T(8,128)(2,1)S(...) custom-call(s32[8]{0:T(128)S(1)} %stack.60.order_ref, ...), custom_call_target="tpu_custom_call" | custom-call | flops 6039797760 | bytes 6291456 | tf_op jit(solution)/shard_map/attend/pallas_call | solution.py:133
  161.7 0.0 copy-start.24
  161.7 0.0 copy-start.26
  161.8 0.1 collective-permute-start.1
  161.9 0.0 collective-permute-done.3
  161.9 0.1 add_convert_fusion
  162.0 0.1 add_convert_fusion.1
  162.1 1.5 collective-permute-done.1
  163.6 0.1 add_convert_fusion.2
  163.8 1.2 pad_maximum_fusion
  165.0 20.7 %all-to-all-start.2 = ((bf16[8,192,384]{2,1,0:T(8,128)(2,1)}), bf16[8,192,384]{2,1,0:T(8,128)(2,1)}, u32[]{:S(2)}, u32[]{:S(2)}) async-start(bf16[8,192,384]{2,1,0:T(8,128)(2,1)} %pad_maximum_fusion), calls=%async_computation.2 | async-start | bytes 2359296 | tf_op jit(solution)/shard_map/all_to_all | solution.py:258
  185.7 2.6 collective-permute-start.4
  188.3 3.6 %collective-permute-start.5 = (bf16[384,128]{1,0:T(8,128)(2,1)S(1)}, bf16[384,128]{1,0:T(8,128)(2,1)S(1)}, u32[]{:S(2)}, u32[]{:S(2)}) collective-permute-start(bf16[384,128]{1,0:T(8,128)(2,1)S(1)} %copy-done.25), channel_id=1, source_target_pairs={{16,2},{17,3},{18,4},{19,5},{20,6},{21,7},{22,0},{23,1},{24,10},{2... | collective-permute-start | bytes 294920 | tf_op jit(solution)/shard_map/ppermute | solution.py:254
  192.0 4.8 %collective-permute-start.6 = (bf16[384,128]{1,0:T(8,128)(2,1)S(1)}, bf16[384,128]{1,0:T(8,128)(2,1)S(1)}, u32[]{:S(2)}, u32[]{:S(2)}) collective-permute-start(bf16[384,128]{1,0:T(8,128)(2,1)S(1)} %copy-done.23), channel_id=1, source_target_pairs={{16,4},{17,5},{18,6},{19,7},{20,0},{21,1},{22,2},{23,3},{24,12},{2... | collective-permute-start | bytes 294920 | tf_op jit(solution)/shard_map/ppermute | solution.py:254
  196.8 2.4 collective-permute-start.7
  199.1 1.9 collective-permute-start.8
  201.1 0.0 collective-permute-done.4.refs_0_
  201.1 10.8 %collective-permute-start.9 = (bf16[384,128]{1,0:T(8,128)(2,1)S(1)}, bf16[384,128]{1,0:T(8,128)(2,1)S(1)}, u32[]{:S(2)}, u32[]{:S(2)}) collective-permute-start(bf16[384,128]{1,0:T(8,128)(2,1)S(1)} %copy-done.17), channel_id=1, source_target_pairs={{16,10},{17,11},{18,12},{19,13},{20,14},{21,15},{22,8},{23,9},{24,... | collective-permute-start | bytes 294920 | tf_op jit(solution)/shard_map/ppermute | solution.py:254
  211.9 0.0 collective-permute-done.5.refs_1_
  211.9 8.7 %collective-permute-start.10 = (bf16[384,128]{1,0:T(8,128)(2,1)S(1)}, bf16[384,128]{1,0:T(8,128)(2,1)S(1)}, u32[]{:S(2)}, u32[]{:S(2)}) collective-permute-start(bf16[384,128]{1,0:T(8,128)(2,1)S(1)} %copy-done.15), channel_id=1, source_target_pairs={{16,12},{17,13},{18,14},{19,15},{20,8},{21,9},{22,10},{23,11},{24,... | collective-permute-start | bytes 294920 | tf_op jit(solution)/shard_map/ppermute | solution.py:254
  220.7 0.0 collective-permute-done.6.refs_2_
  220.7 2.0 collective-permute-start.11
  222.7 0.0 collective-permute-done.7.refs_3_
  222.7 1.9 collective-permute-start.12
  224.7 1.9 collective-permute-start.13
  226.6 0.0 collective-permute-done.9.refs_5_
  226.6 1.9 collective-permute-start.14
  228.6 1.9 collective-permute-start.15
  230.5 1.0 collective-permute-done.11.refs_7_
  231.5 1.9 collective-permute-start.16
  233.5 2.5 collective-permute-start.17
  236.0 7.2 %collective-permute-start.18 = (bf16[384,128]{1,0:T(8,128)(2,1)S(1)}, bf16[384,128]{1,0:T(8,128)(2,1)S(1)}, u32[]{:S(2)}, u32[]{:S(2)}) collective-permute-start(bf16[384,128]{1,0:T(8,128)(2,1)S(1)} %get-tuple-element.61), channel_id=1, source_target_pairs={{16,12},{17,13},{18,14},{19,15},{20,8},{21,9},{22,10},{23,11},{24,... | collective-permute-start | bytes 294920 | tf_op jit(solution)/shard_map/ppermute | solution.py:254
  243.2 3.9 %collective-permute-start.19 = (bf16[384,128]{1,0:T(8,128)(2,1)S(1)}, bf16[384,128]{1,0:T(8,128)(2,1)S(1)}, u32[]{:S(2)}, u32[]{:S(2)}) collective-permute-start(bf16[384,128]{1,0:T(8,128)(2,1)S(1)} %get-tuple-element.62), channel_id=1, source_target_pairs={{16,14},{17,15},{18,8},{19,9},{20,10},{21,11},{22,12},{23,13},{24,... | collective-permute-start | bytes 294920 | tf_op jit(solution)/shard_map/ppermute | solution.py:254
  247.1 1.9 collective-permute-start.20
  249.1 1.9 collective-permute-start.21
  251.0 1.9 collective-permute-start.22
  252.9 1.9 collective-permute-start.23
  254.9 1.9 collective-permute-start.24
  256.8 0.2 collective-permute-done.20.refs_16_
  257.0 3.4 %collective-permute-start.25 = (bf16[384,128]{1,0:T(8,128)(2,1)S(1)}, bf16[384,128]{1,0:T(8,128)(2,1)S(1)}, u32[]{:S(2)}, u32[]{:S(2)}) collective-permute-start(bf16[384,128]{1,0:T(8,128)(2,1)S(1)} %get-tuple-element.68), channel_id=1, source_target_pairs={{16,10},{17,11},{18,12},{19,13},{20,14},{21,15},{22,8},{23,9},{24,... | collective-permute-start | bytes 294920 | tf_op jit(solution)/shard_map/ppermute | solution.py:254
  260.4 1.9 collective-permute-start.26
  262.4 0.3 collective-permute-done.22.refs_18_
  262.6 3.9 %collective-permute-start.27 = (bf16[384,128]{1,0:T(8,128)(2,1)S(1)}, bf16[384,128]{1,0:T(8,128)(2,1)S(1)}, u32[]{:S(2)}, u32[]{:S(2)}) collective-permute-start(bf16[384,128]{1,0:T(8,128)(2,1)S(1)} %get-tuple-element.70), channel_id=1, source_target_pairs={{16,14},{17,15},{18,8},{19,9},{20,10},{21,11},{22,12},{23,13},{24,... | collective-permute-start | bytes 294920 | tf_op jit(solution)/shard_map/ppermute | solution.py:254
  266.6 0.1 stack.68.order_ref
  266.7 1.1 collective-permute-done.25.refs_21_
  267.8 3.7 %collective-permute-done.26.refs_22_ = bf16[384,128]{1,0:T(8,128)(2,1)S(1)} collective-permute-done((bf16[384,128]{1,0:T(8,128)(2,1)S(1)}, bf16[384,128]{1,0:T(8,128)(2,1)S(1)}, u32[]{:S(2)}, u32[]{:S(2)}) %collective-permute-start.26) | collective-permute-done | bytes 98336 | tf_op jit(solution)/shard_map/ppermute | solution.py:254
  271.5 2.0 collective-permute-done.27.refs_23_
  273.5 3.8 %place.1 = bf16[1,384,3072]{2,1,0:T(8,128)(2,1)} custom-call(s32[8]{0:T(128)S(1)} %stack.68.order_ref, bf16[384,128]{1,0:T(8,128)(2,1)S(1)} %collective-permute-done.4.refs_0_, bf16[384,128]{1,0:T(8,128)(2,1)S(1)} %collective-permute-done.5.refs_1_, bf16[384,128]{1,0:T(8,128)(2,1)S(1)} %collective-permute-done.6.refs_2_, ...), custom_call_target="tpu_custom_call" | custom-call | tf_op jit(solution)/shard_map/place/pallas_call | solution.py:202
  277.3 6.7 %unpool.1 = (bf16[1,384,3072]{2,1,0:T(8,128)(2,1)}, bf16[1,384,3072]{2,1,0:T(8,128)(2,1)}) custom-call(bf16[8,192,384]{2,1,0:T(8,128)(2,1)} %all-to-all-done.2.dkv_ref), custom_call_target="tpu_custom_call" | custom-call | tf_op jit(solution)/shard_map/unpool/pallas_call | solution.py:180
  (71 shorter events, 0.2 us)
Async XLA Ops:
  35.3 60.3 %all-to-all-start = ((bf16[8,768,384]{2,1,0:T(8,128)(2,1)}), bf16[8,768,384]{2,1,0:T(8,128)(2,1)}, u32[]{:S(2)}, u32[]{:S(2)}) async-start(bf16[8,768,384]{2,1,0:T(8,128)(2,1)} %get-tuple-element.37), calls=%async_computation | async-start | bytes 9437184 | tf_op jit(solution)/shard_map/all_to_all | solution.py:238
  42.8 3.0 %collective-permute-start = (bf16[8,208,384]{2,1,0:T(8,128)(2,1)S(1)}, bf16[8,208,384]{2,1,0:T(8,128)(2,1)S(1)}, u32[]{:S(2)}, u32[]{:S(2)}) collective-permute-start(bf16[8,208,384]{2,1,0:T(8,128)(2,1)S(1)} %all_to_all.15.own_ref.bias_ref), channel_id=1, source_target_pairs={{0,1},{1,0},{2,3},{3,2},{4,5},{5,4},{6,7},{7,6},{8,9},{9,8},{10,11... | collective-permute-start | bytes 3833864 | tf_op jit(solution)/shard_map/ppermute | solution.py:237
  117.4 44.5 %collective-permute-start.3 = (bf16[8,192,128]{2,1,0:T(8,128)(2,1)S(1)}, bf16[8,192,128]{2,1,0:T(8,128)(2,1)S(1)}, u32[]{:S(2)}, u32[]{:S(2)}) collective-permute-start(bf16[8,192,128]{2,1,0:T(8,128)(2,1)S(1)} %get-tuple-element.44), channel_id=1, source_target_pairs={{0,1},{1,0},{2,3},{3,2},{4,5},{5,4},{6,7},{7,6},{8,9},{9,8},{10,11... | collective-permute-start | bytes 1179656 | tf_op jit(solution)/shard_map/ppermute | solution.py:256
  139.2 22.4 %copy-start = (bf16[384,128]{1,0:T(8,128)(2,1)}, bf16[384,128]{1,0:T(8,128)(2,1)S(1)}, u32[]{:S(2)}) copy-start(bf16[384,128]{1,0:T(8,128)(2,1)S(1)} %get-tuple-element.60) | copy-start | bytes 294916
  139.3 22.4 %copy-start.2 = (bf16[384,128]{1,0:T(8,128)(2,1)}, bf16[384,128]{1,0:T(8,128)(2,1)S(1)}, u32[]{:S(2)}) copy-start(bf16[384,128]{1,0:T(8,128)(2,1)S(1)} %get-tuple-element.59) | copy-start | bytes 294916
  139.3 22.4 %copy-start.4 = (bf16[384,128]{1,0:T(8,128)(2,1)}, bf16[384,128]{1,0:T(8,128)(2,1)S(1)}, u32[]{:S(2)}) copy-start(bf16[384,128]{1,0:T(8,128)(2,1)S(1)} %get-tuple-element.58) | copy-start | bytes 294916
  139.3 22.4 %copy-start.6 = (bf16[384,128]{1,0:T(8,128)(2,1)}, bf16[384,128]{1,0:T(8,128)(2,1)S(1)}, u32[]{:S(2)}) copy-start(bf16[384,128]{1,0:T(8,128)(2,1)S(1)} %get-tuple-element.57) | copy-start | bytes 294916
  139.3 22.4 %copy-start.8 = (bf16[384,128]{1,0:T(8,128)(2,1)}, bf16[384,128]{1,0:T(8,128)(2,1)S(1)}, u32[]{:S(2)}) copy-start(bf16[384,128]{1,0:T(8,128)(2,1)S(1)} %get-tuple-element.56) | copy-start | bytes 294916
  139.3 22.4 %copy-start.10 = (bf16[384,128]{1,0:T(8,128)(2,1)}, bf16[384,128]{1,0:T(8,128)(2,1)S(1)}, u32[]{:S(2)}) copy-start(bf16[384,128]{1,0:T(8,128)(2,1)S(1)} %get-tuple-element.55) | copy-start | bytes 294916
  139.3 22.7 %collective-permute-start.2 = (bf16[8,192,128]{2,1,0:T(8,128)(2,1)S(1)}, bf16[8,192,128]{2,1,0:T(8,128)(2,1)S(1)}, u32[]{:S(2)}, u32[]{:S(2)}) collective-permute-start(bf16[8,192,128]{2,1,0:T(8,128)(2,1)S(1)} %get-tuple-element.42), channel_id=1, source_target_pairs={{0,1},{1,0},{2,3},{3,2},{4,5},{5,4},{6,7},{7,6},{8,9},{9,8},{10,11... | collective-permute-start | bytes 1179656 | tf_op jit(solution)/shard_map/ppermute | solution.py:256
  161.7 2.0 copy-start.12
  161.7 2.0 copy-start.14
  161.7 2.0 copy-start.16
  161.7 2.0 copy-start.18
  161.7 2.0 copy-start.20
  161.7 2.0 copy-start.22
  161.7 2.0 copy-start.24
  161.7 2.0 copy-start.26
  161.8 1.8 collective-permute-start.1
  163.7 59.0 %copy-start.11 = (bf16[384,128]{1,0:T(8,128)(2,1)S(1)}, bf16[384,128]{1,0:T(8,128)(2,1)}, u32[]{:S(2)}) copy-start(bf16[384,128]{1,0:T(8,128)(2,1)} %copy-done.10) | copy-start | bytes 294916
  163.7 60.9 %copy-start.9 = (bf16[384,128]{1,0:T(8,128)(2,1)S(1)}, bf16[384,128]{1,0:T(8,128)(2,1)}, u32[]{:S(2)}) copy-start(bf16[384,128]{1,0:T(8,128)(2,1)} %copy-done.8) | copy-start | bytes 294916
  163.7 62.9 %copy-start.7 = (bf16[384,128]{1,0:T(8,128)(2,1)S(1)}, bf16[384,128]{1,0:T(8,128)(2,1)}, u32[]{:S(2)}) copy-start(bf16[384,128]{1,0:T(8,128)(2,1)} %copy-done.6) | copy-start | bytes 294916
  163.8 64.8 %copy-start.5 = (bf16[384,128]{1,0:T(8,128)(2,1)S(1)}, bf16[384,128]{1,0:T(8,128)(2,1)}, u32[]{:S(2)}) copy-start(bf16[384,128]{1,0:T(8,128)(2,1)} %copy-done.4) | copy-start | bytes 294916
  163.8 67.8 %copy-start.3 = (bf16[384,128]{1,0:T(8,128)(2,1)S(1)}, bf16[384,128]{1,0:T(8,128)(2,1)}, u32[]{:S(2)}) copy-start(bf16[384,128]{1,0:T(8,128)(2,1)} %copy-done.2) | copy-start | bytes 294916
  163.8 69.7 %copy-start.1 = (bf16[384,128]{1,0:T(8,128)(2,1)S(1)}, bf16[384,128]{1,0:T(8,128)(2,1)}, u32[]{:S(2)}) copy-start(bf16[384,128]{1,0:T(8,128)(2,1)} %copy-done) | copy-start | bytes 294916
  165.0 20.7 %copy-start.27 = (bf16[384,128]{1,0:T(8,128)(2,1)S(1)}, bf16[384,128]{1,0:T(8,128)(2,1)}, u32[]{:S(2)}) copy-start(bf16[384,128]{1,0:T(8,128)(2,1)} %copy-done.26) | copy-start | bytes 294916
  165.0 23.4 %copy-start.25 = (bf16[384,128]{1,0:T(8,128)(2,1)S(1)}, bf16[384,128]{1,0:T(8,128)(2,1)}, u32[]{:S(2)}) copy-start(bf16[384,128]{1,0:T(8,128)(2,1)} %copy-done.24) | copy-start | bytes 294916
  165.0 27.0 %copy-start.23 = (bf16[384,128]{1,0:T(8,128)(2,1)S(1)}, bf16[384,128]{1,0:T(8,128)(2,1)}, u32[]{:S(2)}) copy-start(bf16[384,128]{1,0:T(8,128)(2,1)} %copy-done.22) | copy-start | bytes 294916
  165.0 31.8 %copy-start.21 = (bf16[384,128]{1,0:T(8,128)(2,1)S(1)}, bf16[384,128]{1,0:T(8,128)(2,1)}, u32[]{:S(2)}) copy-start(bf16[384,128]{1,0:T(8,128)(2,1)} %copy-done.20) | copy-start | bytes 294916
  165.0 34.2 %copy-start.19 = (bf16[384,128]{1,0:T(8,128)(2,1)S(1)}, bf16[384,128]{1,0:T(8,128)(2,1)}, u32[]{:S(2)}) copy-start(bf16[384,128]{1,0:T(8,128)(2,1)} %copy-done.18) | copy-start | bytes 294916
  165.0 36.1 %copy-start.17 = (bf16[384,128]{1,0:T(8,128)(2,1)S(1)}, bf16[384,128]{1,0:T(8,128)(2,1)}, u32[]{:S(2)}) copy-start(bf16[384,128]{1,0:T(8,128)(2,1)} %copy-done.16) | copy-start | bytes 294916
  165.0 46.9 %copy-start.15 = (bf16[384,128]{1,0:T(8,128)(2,1)S(1)}, bf16[384,128]{1,0:T(8,128)(2,1)}, u32[]{:S(2)}) copy-start(bf16[384,128]{1,0:T(8,128)(2,1)} %copy-done.14) | copy-start | bytes 294916
  165.0 55.7 %copy-start.13 = (bf16[384,128]{1,0:T(8,128)(2,1)S(1)}, bf16[384,128]{1,0:T(8,128)(2,1)}, u32[]{:S(2)}) copy-start(bf16[384,128]{1,0:T(8,128)(2,1)} %copy-done.12) | copy-start | bytes 294916
  165.0 112.3 %all-to-all-start.2 = ((bf16[8,192,384]{2,1,0:T(8,128)(2,1)}), bf16[8,192,384]{2,1,0:T(8,128)(2,1)}, u32[]{:S(2)}, u32[]{:S(2)}) async-start(bf16[8,192,384]{2,1,0:T(8,128)(2,1)} %pad_maximum_fusion), calls=%async_computation.2 | async-start | bytes 2359296 | tf_op jit(solution)/shard_map/all_to_all | solution.py:258
  185.7 15.4 %collective-permute-start.4 = (bf16[384,128]{1,0:T(8,128)(2,1)S(1)}, bf16[384,128]{1,0:T(8,128)(2,1)S(1)}, u32[]{:S(2)}, u32[]{:S(2)}) collective-permute-start(bf16[384,128]{1,0:T(8,128)(2,1)S(1)} %copy-done.27), channel_id=1, source_target_pairs={{16,0},{17,1},{18,2},{19,3},{20,4},{21,5},{22,6},{23,7},{24,8},{25... | collective-permute-start | bytes 294920 | tf_op jit(solution)/shard_map/ppermute | solution.py:254
  188.3 23.6 %collective-permute-start.5 = (bf16[384,128]{1,0:T(8,128)(2,1)S(1)}, bf16[384,128]{1,0:T(8,128)(2,1)S(1)}, u32[]{:S(2)}, u32[]{:S(2)}) collective-permute-start(bf16[384,128]{1,0:T(8,128)(2,1)S(1)} %copy-done.25), channel_id=1, source_target_pairs={{16,2},{17,3},{18,4},{19,5},{20,6},{21,7},{22,0},{23,1},{24,10},{2... | collective-permute-start | bytes 294920 | tf_op jit(solution)/shard_map/ppermute | solution.py:254
  192.0 28.7 %collective-permute-start.6 = (bf16[384,128]{1,0:T(8,128)(2,1)S(1)}, bf16[384,128]{1,0:T(8,128)(2,1)S(1)}, u32[]{:S(2)}, u32[]{:S(2)}) collective-permute-start(bf16[384,128]{1,0:T(8,128)(2,1)S(1)} %copy-done.23), channel_id=1, source_target_pairs={{16,4},{17,5},{18,6},{19,7},{20,0},{21,1},{22,2},{23,3},{24,12},{2... | collective-permute-start | bytes 294920 | tf_op jit(solution)/shard_map/ppermute | solution.py:254
  196.8 25.9 %collective-permute-start.7 = (bf16[384,128]{1,0:T(8,128)(2,1)S(1)}, bf16[384,128]{1,0:T(8,128)(2,1)S(1)}, u32[]{:S(2)}, u32[]{:S(2)}) collective-permute-start(bf16[384,128]{1,0:T(8,128)(2,1)S(1)} %copy-done.21), channel_id=1, source_target_pairs={{16,6},{17,7},{18,0},{19,1},{20,2},{21,3},{22,4},{23,5},{24,14},{2... | collective-permute-start | bytes 294920 | tf_op jit(solution)/shard_map/ppermute | solution.py:254
  199.1 25.5 %collective-permute-start.8 = (bf16[384,128]{1,0:T(8,128)(2,1)S(1)}, bf16[384,128]{1,0:T(8,128)(2,1)S(1)}, u32[]{:S(2)}, u32[]{:S(2)}) collective-permute-start(bf16[384,128]{1,0:T(8,128)(2,1)S(1)} %copy-done.19), channel_id=1, source_target_pairs={{16,8},{17,9},{18,10},{19,11},{20,12},{21,13},{22,14},{23,15},{24,... | collective-permute-start | bytes 294920 | tf_op jit(solution)/shard_map/ppermute | solution.py:254
  201.1 25.5 %collective-permute-start.9 = (bf16[384,128]{1,0:T(8,128)(2,1)S(1)}, bf16[384,128]{1,0:T(8,128)(2,1)S(1)}, u32[]{:S(2)}, u32[]{:S(2)}) collective-permute-start(bf16[384,128]{1,0:T(8,128)(2,1)S(1)} %copy-done.17), channel_id=1, source_target_pairs={{16,10},{17,11},{18,12},{19,13},{20,14},{21,15},{22,8},{23,9},{24,... | collective-permute-start | bytes 294920 | tf_op jit(solution)/shard_map/ppermute | solution.py:254
  211.9 16.6 %collective-permute-start.10 = (bf16[384,128]{1,0:T(8,128)(2,1)S(1)}, bf16[384,128]{1,0:T(8,128)(2,1)S(1)}, u32[]{:S(2)}, u32[]{:S(2)}) collective-permute-start(bf16[384,128]{1,0:T(8,128)(2,1)S(1)} %copy-done.15), channel_id=1, source_target_pairs={{16,12},{17,13},{18,14},{19,15},{20,8},{21,9},{22,10},{23,11},{24,... | collective-permute-start | bytes 294920 | tf_op jit(solution)/shard_map/ppermute | solution.py:254
  220.7 10.8 %collective-permute-start.11 = (bf16[384,128]{1,0:T(8,128)(2,1)S(1)}, bf16[384,128]{1,0:T(8,128)(2,1)S(1)}, u32[]{:S(2)}, u32[]{:S(2)}) collective-permute-start(bf16[384,128]{1,0:T(8,128)(2,1)S(1)} %copy-done.13), channel_id=1, source_target_pairs={{16,14},{17,15},{18,8},{19,9},{20,10},{21,11},{22,12},{23,13},{24,... | collective-permute-start | bytes 294920 | tf_op jit(solution)/shard_map/ppermute | solution.py:254
  222.7 10.7 %collective-permute-start.12 = (bf16[384,128]{1,0:T(8,128)(2,1)S(1)}, bf16[384,128]{1,0:T(8,128)(2,1)S(1)}, u32[]{:S(2)}, u32[]{:S(2)}) collective-permute-start(bf16[384,128]{1,0:T(8,128)(2,1)S(1)} %copy-done.11), channel_id=1, source_target_pairs={{16,0},{17,1},{18,2},{19,3},{20,4},{21,5},{22,6},{23,7},{24,8},{25... | collective-permute-start | bytes 294920 | tf_op jit(solution)/shard_map/ppermute | solution.py:254
  224.7 11.4 %collective-permute-start.13 = (bf16[384,128]{1,0:T(8,128)(2,1)S(1)}, bf16[384,128]{1,0:T(8,128)(2,1)S(1)}, u32[]{:S(2)}, u32[]{:S(2)}) collective-permute-start(bf16[384,128]{1,0:T(8,128)(2,1)S(1)} %copy-done.9), channel_id=1, source_target_pairs={{16,2},{17,3},{18,4},{19,5},{20,6},{21,7},{22,0},{23,1},{24,10},{2... | collective-permute-start | bytes 294920 | tf_op jit(solution)/shard_map/ppermute | solution.py:254
  226.6 16.6 %collective-permute-start.14 = (bf16[384,128]{1,0:T(8,128)(2,1)S(1)}, bf16[384,128]{1,0:T(8,128)(2,1)S(1)}, u32[]{:S(2)}, u32[]{:S(2)}) collective-permute-start(bf16[384,128]{1,0:T(8,128)(2,1)S(1)} %copy-done.7), channel_id=1, source_target_pairs={{16,4},{17,5},{18,6},{19,7},{20,0},{21,1},{22,2},{23,3},{24,12},{2... | collective-permute-start | bytes 294920 | tf_op jit(solution)/shard_map/ppermute | solution.py:254
  228.6 18.5 %collective-permute-start.15 = (bf16[384,128]{1,0:T(8,128)(2,1)S(1)}, bf16[384,128]{1,0:T(8,128)(2,1)S(1)}, u32[]{:S(2)}, u32[]{:S(2)}) collective-permute-start(bf16[384,128]{1,0:T(8,128)(2,1)S(1)} %copy-done.5), channel_id=1, source_target_pairs={{16,6},{17,7},{18,0},{19,1},{20,2},{21,3},{22,4},{23,5},{24,14},{2... | collective-permute-start | bytes 294920 | tf_op jit(solution)/shard_map/ppermute | solution.py:254
  231.5 17.5 %collective-permute-start.16 = (bf16[384,128]{1,0:T(8,128)(2,1)S(1)}, bf16[384,128]{1,0:T(8,128)(2,1)S(1)}, u32[]{:S(2)}, u32[]{:S(2)}) collective-permute-start(bf16[384,128]{1,0:T(8,128)(2,1)S(1)} %copy-done.3), channel_id=1, source_target_pairs={{16,8},{17,9},{18,10},{19,11},{20,12},{21,13},{22,14},{23,15},{24,... | collective-permute-start | bytes 294920 | tf_op jit(solution)/shard_map/ppermute | solution.py:254
  233.5 17.5 %collective-permute-start.17 = (bf16[384,128]{1,0:T(8,128)(2,1)S(1)}, bf16[384,128]{1,0:T(8,128)(2,1)S(1)}, u32[]{:S(2)}, u32[]{:S(2)}) collective-permute-start(bf16[384,128]{1,0:T(8,128)(2,1)S(1)} %copy-done.1), channel_id=1, source_target_pairs={{16,10},{17,11},{18,12},{19,13},{20,14},{21,15},{22,8},{23,9},{24,... | collective-permute-start | bytes 294920 | tf_op jit(solution)/shard_map/ppermute | solution.py:254
  236.0 16.9 %collective-permute-start.18 = (bf16[384,128]{1,0:T(8,128)(2,1)S(1)}, bf16[384,128]{1,0:T(8,128)(2,1)S(1)}, u32[]{:S(2)}, u32[]{:S(2)}) collective-permute-start(bf16[384,128]{1,0:T(8,128)(2,1)S(1)} %get-tuple-element.61), channel_id=1, source_target_pairs={{16,12},{17,13},{18,14},{19,15},{20,8},{21,9},{22,10},{23,11},{24,... | collective-permute-start | bytes 294920 | tf_op jit(solution)/shard_map/ppermute | solution.py:254
  243.2 11.7 %collective-permute-start.19 = (bf16[384,128]{1,0:T(8,128)(2,1)S(1)}, bf16[384,128]{1,0:T(8,128)(2,1)S(1)}, u32[]{:S(2)}, u32[]{:S(2)}) collective-permute-start(bf16[384,128]{1,0:T(8,128)(2,1)S(1)} %get-tuple-element.62), channel_id=1, source_target_pairs={{16,14},{17,15},{18,8},{19,9},{20,10},{21,11},{22,12},{23,13},{24,... | collective-permute-start | bytes 294920 | tf_op jit(solution)/shard_map/ppermute | solution.py:254
  247.1 9.9 %collective-permute-start.20 = (bf16[384,128]{1,0:T(8,128)(2,1)S(1)}, bf16[384,128]{1,0:T(8,128)(2,1)S(1)}, u32[]{:S(2)}, u32[]{:S(2)}) collective-permute-start(bf16[384,128]{1,0:T(8,128)(2,1)S(1)} %get-tuple-element.63), channel_id=1, source_target_pairs={{16,0},{17,1},{18,2},{19,3},{20,4},{21,5},{22,6},{23,7},{24,8},{25... | collective-permute-start | bytes 294920 | tf_op jit(solution)/shard_map/ppermute | solution.py:254
  249.1 11.4 %collective-permute-start.21 = (bf16[384,128]{1,0:T(8,128)(2,1)S(1)}, bf16[384,128]{1,0:T(8,128)(2,1)S(1)}, u32[]{:S(2)}, u32[]{:S(2)}) collective-permute-start(bf16[384,128]{1,0:T(8,128)(2,1)S(1)} %get-tuple-element.64), channel_id=1, source_target_pairs={{16,2},{17,3},{18,4},{19,5},{20,6},{21,7},{22,0},{23,1},{24,10},{2... | collective-permute-start | bytes 294920 | tf_op jit(solution)/shard_map/ppermute | solution.py:254
  251.0 11.6 %collective-permute-start.22 = (bf16[384,128]{1,0:T(8,128)(2,1)S(1)}, bf16[384,128]{1,0:T(8,128)(2,1)S(1)}, u32[]{:S(2)}, u32[]{:S(2)}) collective-permute-start(bf16[384,128]{1,0:T(8,128)(2,1)S(1)} %get-tuple-element.65), channel_id=1, source_target_pairs={{16,4},{17,5},{18,6},{19,7},{20,0},{21,1},{22,2},{23,3},{24,12},{2... | collective-permute-start | bytes 294920 | tf_op jit(solution)/shard_map/ppermute | solution.py:254
  252.9 13.7 %collective-permute-start.23 = (bf16[384,128]{1,0:T(8,128)(2,1)S(1)}, bf16[384,128]{1,0:T(8,128)(2,1)S(1)}, u32[]{:S(2)}, u32[]{:S(2)}) collective-permute-start(bf16[384,128]{1,0:T(8,128)(2,1)S(1)} %get-tuple-element.66), channel_id=1, source_target_pairs={{16,6},{17,7},{18,0},{19,1},{20,2},{21,3},{22,4},{23,5},{24,14},{2... | collective-permute-start | bytes 294920 | tf_op jit(solution)/shard_map/ppermute | solution.py:254
  254.9 11.8 %collective-permute-start.24 = (bf16[384,128]{1,0:T(8,128)(2,1)S(1)}, bf16[384,128]{1,0:T(8,128)(2,1)S(1)}, u32[]{:S(2)}, u32[]{:S(2)}) collective-permute-start(bf16[384,128]{1,0:T(8,128)(2,1)S(1)} %get-tuple-element.67), channel_id=1, source_target_pairs={{16,8},{17,9},{18,10},{19,11},{20,12},{21,13},{22,14},{23,15},{24,... | collective-permute-start | bytes 294920 | tf_op jit(solution)/shard_map/ppermute | solution.py:254
  257.0 10.7 %collective-permute-start.25 = (bf16[384,128]{1,0:T(8,128)(2,1)S(1)}, bf16[384,128]{1,0:T(8,128)(2,1)S(1)}, u32[]{:S(2)}, u32[]{:S(2)}) collective-permute-start(bf16[384,128]{1,0:T(8,128)(2,1)S(1)} %get-tuple-element.68), channel_id=1, source_target_pairs={{16,10},{17,11},{18,12},{19,13},{20,14},{21,15},{22,8},{23,9},{24,... | collective-permute-start | bytes 294920 | tf_op jit(solution)/shard_map/ppermute | solution.py:254
  260.4 11.0 %collective-permute-start.26 = (bf16[384,128]{1,0:T(8,128)(2,1)S(1)}, bf16[384,128]{1,0:T(8,128)(2,1)S(1)}, u32[]{:S(2)}, u32[]{:S(2)}) collective-permute-start(bf16[384,128]{1,0:T(8,128)(2,1)S(1)} %get-tuple-element.69), channel_id=1, source_target_pairs={{16,12},{17,13},{18,14},{19,15},{20,8},{21,9},{22,10},{23,11},{24,... | collective-permute-start | bytes 294920 | tf_op jit(solution)/shard_map/ppermute | solution.py:254
  262.6 10.8 %collective-permute-start.27 = (bf16[384,128]{1,0:T(8,128)(2,1)S(1)}, bf16[384,128]{1,0:T(8,128)(2,1)S(1)}, u32[]{:S(2)}, u32[]{:S(2)}) collective-permute-start(bf16[384,128]{1,0:T(8,128)(2,1)S(1)} %get-tuple-element.70), channel_id=1, source_target_pairs={{16,14},{17,15},{18,8},{19,9},{20,10},{21,11},{22,12},{23,13},{24,... | collective-permute-start | bytes 294920 | tf_op jit(solution)/shard_map/ppermute | solution.py:254

commit v2 on v1

v2 whole, which is shorter than its diff:
```python
import functools

import jax
import jax.numpy as jnp
from jax import lax
from jax.experimental import pallas as pl
from jax.experimental.pallas import tpu as pltpu
from jax.sharding import PartitionSpec as P

HD = 128
CHIPS = 8
CORES = 2
HEADS_CHIP = 3
TOK = 384
POOL = 96
ROW = 192
WIDE = HEADS_CHIP * HD
KTILES = CHIPS * CORES
KEYS = KTILES * POOL
SCALE = 1.0 / HD**0.5
LOG2E = 1.4426950408889634
BLOCKED = -1e30
LINE = 4
KV_AT = 2 * TOK
BIAS_AT = KV_AT + 2 * POOL
BIAS_ROWS = KTILES * (TOK // HD)
NN = (((1,), (0,)), ((), ()))
NT = (((1,), (1,)), ((), ()))
TN = (((0,), (0,)), ((), ()))


def dot(a, b, dims):
    return lax.dot_general(a, b, dims, preferred_element_type=jnp.float32)


def pool_matrix(shape, token_dim):
    token = lax.broadcasted_iota(jnp.int32, shape, token_dim)
    pooled = lax.broadcasted_iota(jnp.int32, shape, 1 - token_dim)
    column = jnp.where(token >= ROW, token - ROW, token)
    return jnp.where(column // 2 == pooled, 1.0, 0.0).astype(jnp.bfloat16)


def pack_head(pool, out_ref, q, d, k, v):
    out_ref[0, :TOK] = q
    out_ref[0, TOK:KV_AT] = d
    out_ref[0, KV_AT : KV_AT + POOL] = (dot(pool, k, NN) * 0.25).astype(jnp.bfloat16)
    out_ref[0, KV_AT + POOL : BIAS_AT] = (dot(pool, v, NN) * 0.25).astype(jnp.bfloat16)


def pack_first_kernel(core_ref, mask_ref, q_ref, d_ref, k_ref, v_ref, out_ref, pool, bias):
    @pl.when(pl.program_id(0) == 0)
    def _():
        pool[...] = pool_matrix((POOL, TOK), 1)
        for block in range(TOK // HD):
            token = lax.broadcasted_iota(jnp.int32, (1, HD), 1) + block * HD
            for at in range(KTILES):
                tile = at % CHIPS * CORES + (at // CHIPS + core_ref[0]) % CORES
                upper = jnp.where(mask_ref[0, tile] > 0, 0.0, BLOCKED)
                lower = jnp.where(mask_ref[1, tile] > 0, 0.0, BLOCKED)
                row = block * KTILES + at
                bias[row : row + 1] = jnp.where(token < ROW, upper, lower)

    pack_head(pool[...], out_ref, q_ref[0], d_ref[0], k_ref[0], v_ref[0])
    out_ref[0, BIAS_AT:] = bias[...].astype(jnp.bfloat16)


def pack_first(core, tile_mask, arrays):
    rows = BIAS_AT + BIAS_ROWS
    scalars = pl.BlockSpec(memory_space=pltpu.SMEM)
    return pl.pallas_call(
        pack_first_kernel,
        grid=(CHIPS,),
        in_specs=[scalars, scalars] + [pl.BlockSpec((1, TOK, HD), lambda j: (0, 0, HEADS_CHIP * j))] * 4,
        out_specs=pl.BlockSpec((1, rows, HD), lambda j: (j, 0, 0)),
        out_shape=jax.ShapeDtypeStruct((CHIPS, rows, HD), jnp.bfloat16),
        scratch_shapes=[pltpu.VMEM((POOL, TOK), jnp.bfloat16), pltpu.VMEM((BIAS_ROWS, HD), jnp.float32)],
        name="pack_first",
    )(core, tile_mask, *arrays)


def pack_rest_kernel(q_ref, d_ref, k_ref, v_ref, *rest):
    out_refs, pool = rest[:-1], rest[-1]

    @pl.when(pl.program_id(0) == 0)
    def _():
        pool[...] = pool_matrix((POOL, TOK), 1)

    for head, out_ref in enumerate(out_refs, 1):
        columns = slice(head * HD, (head + 1) * HD)
        pack_head(pool[...], out_ref, *[r[0, :, columns] for r in (q_ref, d_ref, k_ref, v_ref)])


def pack_rest(arrays):
    late = HEADS_CHIP - 1
    return pl.pallas_call(
        pack_rest_kernel,
        grid=(CHIPS,),
        in_specs=[pl.BlockSpec((1, TOK, WIDE), lambda j: (0, 0, j))] * 4,
        out_specs=[pl.BlockSpec((1, BIAS_AT, HD), lambda j: (j, 0, 0))] * late,
        out_shape=[jax.ShapeDtypeStruct((CHIPS, BIAS_AT, HD), jnp.bfloat16)] * late,
        scratch_shapes=[pltpu.VMEM((POOL, TOK), jnp.bfloat16)],
        name="pack_rest",
    )(*arrays)


def attend_kernel(order_ref, q_ref, d_ref, own_ref, other_ref, bias_ref, *rest):
    dq_refs, dkv_refs = rest[:-8], rest[-8:-6]
    keys, values, dkeys, dvalues, expo, dprob = rest[-6:]
    step = pl.program_id(0)

    @pl.when(step == 0)
    def _():
        for s in range(CHIPS):
            for half, ref in enumerate((own_ref, other_ref)):
                at = (half * CHIPS + s) * POOL
                keys[at : at + POOL] = ref[s, :POOL]
                values[at : at + POOL] = ref[s, POOL:]
        dkeys[...] = jnp.zeros_like(dkeys)
        dvalues[...] = jnp.zeros_like(dvalues)

    q = q_ref[0]
    d = d_ref[0]
    blocks = [bias_ref[0, at : at + KTILES].astype(jnp.float32) for at in range(0, BIAS_ROWS, KTILES)]
    bias = jnp.concatenate(blocks, axis=1)
    part = 4 * POOL
    top = jnp.full((8, TOK), -3e38, jnp.float32)
    for at in range(0, KEYS, part):
        scores = dot(keys[at : at + part], q, NT)
        for tile in range(part // POOL):
            row = at // POOL + tile
            one = scores[tile * POOL : (tile + 1) * POOL] + bias[row : row + 1]
            expo[at + tile * POOL : at + (tile + 1) * POOL] = one
            top = jnp.maximum(top, jnp.max(one.reshape(POOL // 8, 8, TOK), axis=0))
    top = jnp.max(top, axis=0, keepdims=True)
    total = jnp.zeros((8, TOK), jnp.float32)
    weighted = jnp.zeros((8, TOK), jnp.float32)
    for at in range(0, KEYS, part):
        grad = dot(values[at : at + part], d, NT)
        e = jnp.exp2((expo[at : at + part] - top) * (SCALE * LOG2E))
        expo[at : at + part] = e
        dprob[at : at + part] = grad
        total = total + jnp.sum(e.reshape(part // 8, 8, TOK), axis=0)
        weighted = weighted + jnp.sum((e * grad).reshape(part // 8, 8, TOK), axis=0)
    inverse = 1.0 / jnp.sum(total, axis=0, keepdims=True)
    delta = jnp.sum(weighted, axis=0, keepdims=True) * inverse
    scaled = inverse * SCALE
    dq = jnp.zeros((TOK, HD), jnp.float32)
    for at in range(0, KEYS, part):
        e = expo[at : at + part]
        probs = (e * inverse).astype(jnp.bfloat16)
        sgrad = ((e * scaled) * (dprob[at : at + part] - delta)).astype(jnp.bfloat16)
        dvalues[at : at + part] += dot(probs, d, NN)
        dkeys[at : at + part] += dot(sgrad, q, NN)
        dq = dq + dot(sgrad, keys[at : at + part], TN)
    each = CHIPS // len(dq_refs)
    for k, ref in enumerate(dq_refs):

        @pl.when(step // each == k)
        def _():
            ref[0] = dq.astype(jnp.bfloat16)

    @pl.when(step == CHIPS - 1)
    def _():
        for half, ref in enumerate(dkv_refs):
            for s in range(CHIPS):
                at = (half * CHIPS + s) * POOL
                ref[s, :POOL] = dkeys[at : at + POOL].astype(ref.dtype)
                ref[s, POOL:] = dvalues[at : at + POOL].astype(ref.dtype)


def attend(order, data, first, kv_other, parts):
    each = CHIPS // parts
    terms = pl.BlockSpec((CHIPS, 2 * POOL, HD), lambda k, order: (0, 0, 0))
    return pl.pallas_call(
        attend_kernel,
        grid_spec=pltpu.PrefetchScalarGridSpec(
            num_scalar_prefetch=1,
            grid=(CHIPS,),
            in_specs=[
                pl.BlockSpec((1, TOK, HD), lambda k, order: (order[k], 0, 0)),
                pl.BlockSpec((1, TOK, HD), lambda k, order: (order[k], 1, 0)),
                pl.BlockSpec((CHIPS, 2 * POOL, HD), lambda k, order: (0, KV_AT // (2 * POOL), 0)),
                terms,
                pl.BlockSpec((1, BIAS_ROWS, HD), lambda k, order: (order[k], BIAS_AT // BIAS_ROWS, 0)),
            ],
            out_specs=[
                pl.BlockSpec((1, TOK, HD), lambda k, order, at=at: (jnp.clip(k - at, 0, each - 1), 0, 0))
                for at in range(0, CHIPS, each)
            ]
            + [terms, terms],
            scratch_shapes=[
                pltpu.VMEM((KEYS, HD), jnp.bfloat16),
                pltpu.VMEM((KEYS, HD), jnp.bfloat16),
                pltpu.VMEM((KEYS, HD), jnp.float32),
                pltpu.VMEM((KEYS, HD), jnp.float32),
                pltpu.VMEM((KEYS, TOK), jnp.float32),
                pltpu.VMEM((KEYS, TOK), jnp.float32),
            ],
        ),
        out_shape=[jax.ShapeDtypeStruct((each, TOK, HD), jnp.bfloat16)] * parts
        + [jax.ShapeDtypeStruct((CHIPS, 2 * POOL, HD), t) for t in (jnp.float32, jnp.bfloat16)],
        compiler_params=pltpu.CompilerParams(vmem_limit_bytes=60 * 2**20),
        cost_estimate=pl.CostEstimate(
            flops=40 * CHIPS * TOK * KEYS * HD,
            bytes_accessed=6 * 2**20,
            transcendentals=CHIPS * TOK * KEYS,
        ),
        name="attend",
    )(order, data, data, data, kv_other, first)


def unpool_kernel(*refs):
    dkv_refs, (dk_ref, dv_ref, spread) = refs[:-3], refs[-3:]

    @pl.when(pl.program_id(0) == 0)
    def _():
        spread[...] = pool_matrix((TOK, POOL), 0)

    for head, ref in enumerate(dkv_refs):
        columns = slice(head * HD, (head + 1) * HD)
        part = ref[0] * jnp.bfloat16(0.25)
        dk_ref[0, :, columns] = dot(spread[...], part[:POOL], NN).astype(jnp.bfloat16)
        dv_ref[0, :, columns] = dot(spread[...], part[POOL:], NN).astype(jnp.bfloat16)


def unpool(pieces):
    column = pl.BlockSpec((1, TOK, WIDE), lambda s: (0, 0, s))
    whole = jax.ShapeDtypeStruct((1, TOK, CHIPS * WIDE), jnp.bfloat16)
    return pl.pallas_call(
        unpool_kernel,
        grid=(CHIPS,),
        in_specs=[pl.BlockSpec((1, 2 * POOL, HD), lambda s, at=at // (2 * POOL): (s, at, 0)) for _, at in pieces],
        out_specs=[column, column],
        out_shape=[whole, whole],
        scratch_shapes=[pltpu.VMEM((TOK, POOL), jnp.bfloat16)],
        name="unpool",
    )(*[piece for piece, _ in pieces])


def place_kernel(side_ref, *refs):
    for head, ref in enumerate(refs[:-1]):
        refs[-1][0, :, head * HD : (head + 1) * HD] = ref[0]


def place(side, pieces):
    by_chip = pl.BlockSpec((1, TOK, HD), lambda s, side: (s, 0, 0))
    by_line = pl.BlockSpec((1, TOK, HD), lambda s, side: (s % LINE, (s // LINE + side[0]) % 2, 0))
    return pl.pallas_call(
        place_kernel,
        grid_spec=pltpu.PrefetchScalarGridSpec(
            num_scalar_prefetch=1,
            grid=(CHIPS,),
            in_specs=[by_chip] * (len(pieces) - 1) + [by_line],
            out_specs=pl.BlockSpec((1, TOK, WIDE), lambda s, side: (0, 0, s)),
        ),
        out_shape=jax.ShapeDtypeStruct((1, TOK, CHIPS * WIDE), jnp.bfloat16),
        name="place",
    )(side, *pieces)


def after(value, *others):
    return lax.optimization_barrier((value, *others))[0]


def shards(query, key, value, out_grad, tile_mask, sections):
    here = lax.axis_index("ctx")
    core, side = here % CORES, here // (CORES * LINE)
    members = range(CHIPS * CORES)
    groups = [[i for i in members if i % CORES == c] for c in range(CORES)]

    lines = [group[at : at + LINE] for group in groups for at in (0, LINE)]

    def trade(data, among=groups):
        return lax.all_to_all(data, "ctx", 0, 0, axis_index_groups=among, tiled=True)

    def swap(data):
        return lax.ppermute(data, "ctx", [(i, i ^ 1) for i in members])

    def to_previous(data, across=0):
        pairs = [
            (section * KTILES + i, (section - 1) * KTILES + (i + across * LINE * CORES) % KTILES)
            for section in range(1, sections)
            for i in members
        ]
        return lax.ppermute(data, ("section", "ctx"), pairs)

    def kv_of(data):
        return swap(data[:, KV_AT:BIAS_AT])

    def summed(own, foreign):
        return (own + foreign.astype(jnp.float32)).astype(jnp.bfloat16)

    arrays = (query, out_grad, key, value)
    sent = [pack_first(core.reshape(1), tile_mask, arrays), *pack_rest(arrays)]
    first = after(trade(sent[0]), sent[1])

    natural = jnp.arange(CHIPS, dtype=jnp.int32)
    near_first = (natural // LINE + side) % 2 * LINE + natural % LINE
    dq, own, foreign = attend(natural, first, first, kv_of(first), 1)
    moved, terms = [to_previous(dq)], [(own, swap(foreign))]
    data = after(trade(after(sent[1], first)), dq)
    dq, own, foreign = attend(natural, data, first, kv_of(data), 1)
    moved.append(to_previous(dq))
    terms.append((own, swap(foreign)))
    data = after(trade(after(sent[2], data)), dq)
    joined = jnp.concatenate([moved[0], summed(*terms[0]), summed(*terms[1])], axis=1)
    near, far, own, foreign = attend(near_first, after(data, joined), first, kv_of(data), 2)
    early = after(trade(after(joined, data)), near)
    near, far = to_previous(after(near, moved[1])), to_previous(after(far, moved[1]), 1)
    terms.append((own, swap(foreign)))
    middle = trade(after(jnp.concatenate([moved[1], summed(*terms[2])], axis=1), early))
    late = trade(after(jnp.concatenate([near, far], axis=1), middle), lines)
    key_grad, value_grad = unpool([(early, TOK), (early, TOK + 2 * POOL), (middle, TOK)])
    upstream = place(side.reshape(1), [early, middle, late])
    return key_grad, value_grad, upstream


def solution(mesh):
    spec = P("section", "ctx", None)
    return jax.shard_map(
        functools.partial(shards, sections=mesh.shape["section"]),
        mesh=mesh,
        in_specs=(spec, spec, spec, spec, P("ctx", None)),
        out_specs=(spec, spec, spec),
        check_vma=False,
    )
```

time: 290 us -> 223 us (0.77); the launches traced: 284 us -> 221 us
  starting transfers between devices: 108 us -> 51.3 us
  blocking collectives: 24 us -> 0 us
  Pallas kernels: 84.8 us -> 98.2 us
  other arithmetic: 1.43 us -> 8.17 us
  waiting for transfers between devices: 62.7 us -> 57.6 us
  local copies, waits for them, and re-layouts: 2.05 us -> 5.23 us
    ppermute x28 -> x10, starting transfers between devices: 79.6 us -> 10.2 us  [the longest x4 9.53 us: to_previous(): return lax.ppermute(data, ('section', 'ctx'), pairs)]
    all_to_all x1 -> x0, blocking collectives: 24 us -> none  [shards(): kv_own = trade(kv)]
    all_to_all x2 -> x6, waiting for transfers between devices: 49.9 us -> 29.6 us  [trade(): lax.all_to_all(data, 'ctx', 0, 0, axis_index_groups=among, tiled=True)]
    ppermute x28 -> x10, waiting for transfers between devices: 12.8 us -> 28 us  [the longest x4 26.1 us: to_previous(): return lax.ppermute(data, ('section', 'ctx'), pairs)]
    all_to_all x2 -> x6, starting transfers between devices: 28.1 us -> 41.2 us  [trade(): lax.all_to_all(data, 'ctx', 0, 0, axis_index_groups=among, tiled=True)]
    pallas_call x1 -> x2, Pallas kernels: 8.95 us -> 15.1 us  [the longest x1 8.22 us: pack_rest(): pl.pallas_call(pack_rest_kernel, grid=(CHIPS,), in_specs=[pl.BlockSpec((1...]
    pallas_call x3, Pallas kernels: 65.2 us -> 70.3 us  [attend(): pl.pallas_call(attend_kernel, grid_spec=pltpu.PrefetchScalarGridSpec(num_...]
    concatenate x1 -> x3, other arithmetic: 1.17 us -> 4.43 us  [the longest x1 2.39 us: shards(): jnp.concatenate([moved[0], summed(*terms[0]), summed(*terms[1])], axis=1)]
  transfers between devices with their start and end apart: 30 -> 16, of which waited for: 9 -> 5; matrix products, arithmetic and copies ran while one was open for 0% -> 4% of each run, Pallas kernels for 17% -> 39%
where the time goes in v2:
time: 223 us; the launch traced here: 221 us
  Pallas kernels  98.2 us (44%)
  waiting for transfers between devices  57.6 us (26%)
  starting transfers between devices  51.3 us (23%)
  other arithmetic  8.17 us (4%)
  local copies, waits for them, and re-layouts  5.23 us (2%)
    pallas_call x3, Pallas kernels, attend(): pl.pallas_call(attend_kernel, grid_spec=pltpu.PrefetchScalarGridSpec(num_...  70.3 us
    all_to_all x6, starting transfers between devices, trade(): lax.all_to_all(data, 'ctx', 0, 0, axis_index_groups=among, tiled=True)  41.2 us
    all_to_all x6, waiting for transfers between devices, trade(): lax.all_to_all(data, 'ctx', 0, 0, axis_index_groups=among, tiled=True)  29.6 us
    ppermute x4, waiting for transfers between devices, to_previous(): return lax.ppermute(data, ('section', 'ctx'), pairs)  26.1 us
    ppermute x4, starting transfers between devices, to_previous(): return lax.ppermute(data, ('section', 'ctx'), pairs)  9.53 us
    pallas_call x1, Pallas kernels, pack_rest(): pl.pallas_call(pack_rest_kernel, grid=(CHIPS,), in_specs=[pl.BlockSpec((1...  8.22 us
    pallas_call x1, Pallas kernels, pack_first(): pl.pallas_call(pack_first_kernel, grid=(CHIPS,), in_specs=[scalars, scala...  6.87 us
    pallas_call x1, Pallas kernels, unpool(): pl.pallas_call(unpool_kernel, grid=(CHIPS,), in_specs=[pl.BlockSpec((1, 2...  6.74 us
  transfers between devices with their start and end apart: 16, of which 5 were waited for; matrix products, arithmetic and copies ran while one was open for 4% of the time, Pallas kernels for 39%

profile of v2, /device:TPU:56, one launch (start us, length us, event | category | flops | bytes accessed | tf_op | source)
XLA Modules:
  0.0 221.3 jit_solution(6493963459277375537)
XLA Ops:
  0.6 6.9 %pack_first.1 = bf16[8,1008,128]{2,1,0:T(8,128)(2,1)} custom-call(s32[1]{0:T(128)} %bitcast.core_ref, s32[2,16]{1,0:T(2,128)} %mask_ref.1, bf16[1,384,3072]{2,1,0:T(8,128)(2,1)} %q_ref.3, bf16[1,384,3072]{2,1,0:T(8,128)(2,1)} %d_ref.3, bf16[1,384,3072]{2,1,0:T(8,128)(2,1)} %k_ref.3, bf16[1,384,3072]{2,1,0:T(8,128)(2,1)} %v_ref.3), custom_call_target="tpu_custom_call" | custom-call | tf_op jit(solution)/shard_map/pack_first/pallas_call | solution.py:70
  7.5 7.3 %all-to-all-start = ((bf16[8,1008,128]{2,1,0:T(8,128)(2,1)}), bf16[8,1008,128]{2,1,0:T(8,128)(2,1)S(1)}, u32[]{:S(2)}, u32[]{:S(2)}) async-start(bf16[8,1008,128]{2,1,0:T(8,128)(2,1)} %pack_first.1), calls=%async_computation | async-start | bytes 4128768 | tf_op jit(solution)/shard_map/all_to_all | solution.py:274
  14.8 8.2 %pack_rest.1 = (bf16[8,960,128]{2,1,0:T(8,128)(2,1)}, bf16[8,960,128]{2,1,0:T(8,128)(2,1)}) custom-call(bf16[1,384,3072]{2,1,0:T(8,128)(2,1)} %q_ref.3, bf16[1,384,3072]{2,1,0:T(8,128)(2,1)} %d_ref.3, bf16[1,384,3072]{2,1,0:T(8,128)(2,1)} %k_ref.3, bf16[1,384,3072]{2,1,0:T(8,128)(2,1)} %v_ref.3), custom_call_target="tpu_custom_call" | custom-call | tf_op jit(solution)/shard_map/pack_rest/pallas_call | solution.py:95
  23.0 16.9 %all-to-all-done.q_ref.d_ref.own_ref.bias_ref = bf16[8,1008,128]{2,1,0:T(8,128)(2,1)S(1)} async-done(((bf16[8,1008,128]{2,1,0:T(8,128)(2,1)}), bf16[8,1008,128]{2,1,0:T(8,128)(2,1)S(1)}, u32[]{:S(2)}, u32[]{:S(2)}) %all-to-all-start) | async-done | bytes 2064416 | tf_op jit(solution)/shard_map/all_to_all | solution.py:274
  39.9 0.0 copy-start.3
  39.9 0.1 collective-permute-start
  40.0 1.2 copy-done.3
  41.2 8.6 %all-to-all-start.1 = ((bf16[8,960,128]{2,1,0:T(8,128)(2,1)}), bf16[8,960,128]{2,1,0:T(8,128)(2,1)}, u32[]{:S(2)}, u32[]{:S(2)}) async-start(bf16[8,960,128]{2,1,0:T(8,128)(2,1)} %get-tuple-element.34), calls=%async_computation.1 | async-start | bytes 3932160 | tf_op jit(solution)/shard_map/all_to_all | solution.py:274
  49.8 0.0 collective-permute-done.other_ref
  49.8 0.0 copy-start.8
  49.8 0.5 iota.9.order_ref
  50.3 0.2 copy-done.8
  50.5 23.3 %attend.3 = (bf16[8,384,128]{2,1,0:T(8,128)(2,1)}, f32[8,192,128]{2,1,0:T(8,128)}, bf16[8,192,128]{2,1,0:T(8,128)(2,1)}) custom-call(s32[8]{0:T(128)} %iota.9.order_ref, bf16[8,1008,128]{2,1,0:T(8,128)(2,1)} %copy-done.3, bf16[8,1008,128]{2,1,0:T(8,128)(2,1)} %copy-done.3, bf16[8,1008,128]{2,1,0:T(8,128)(2,1)} %copy-done.3, bf16[8,192,128]{2,1,0:T(8,128)(2,1)} %copy-done.8, ...), custom_call_target="tpu_custom_call" | custom-call | flops 24159191040 | bytes 6291456 | tf_op jit(solution)/shard_map/attend/pallas_call | solution.py:174
  73.8 0.0 all-to-all-done.1.q_ref.d_ref.own_ref
  73.9 1.0 slice.10
  74.9 0.1 collective-permute-start.3
  75.0 2.7 %collective-permute-start.1 = (bf16[8,384,128]{2,1,0:T(8,128)(2,1)}, bf16[8,384,128]{2,1,0:T(8,128)(2,1)}, u32[]{:S(2)}, u32[]{:S(2)}) collective-permute-start(bf16[8,384,128]{2,1,0:T(8,128)(2,1)} %get-tuple-element.31), channel_id=1, source_target_pairs={{16,0},{17,1},{18,2},{19,3},{20,4},{21,5},{22,6},{23,7},{24,8},{25... | collective-permute-start | bytes 2359304 | tf_op jit(solution)/shard_map/ppermute | solution.py:285
  77.6 0.3 collective-permute-start.2
  77.9 7.2 %all-to-all-start.2 = ((bf16[8,960,128]{2,1,0:T(8,128)(2,1)}), bf16[8,960,128]{2,1,0:T(8,128)(2,1)S(1)}, u32[]{:S(2)}, u32[]{:S(2)}) async-start(bf16[8,960,128]{2,1,0:T(8,128)(2,1)} %get-tuple-element.39), calls=%async_computation.2 | async-start | bytes 3932160 | tf_op jit(solution)/shard_map/all_to_all | solution.py:274
  85.1 0.0 collective-permute-done.3.other_ref
  85.1 0.0 copy-start.7
  85.1 0.7 copy-done.7
  85.9 0.6 iota.10.order_ref
  86.5 0.0 copy-start.5
  86.5 23.5 %attend.4 = (bf16[8,384,128]{2,1,0:T(8,128)(2,1)}, f32[8,192,128]{2,1,0:T(8,128)}, bf16[8,192,128]{2,1,0:T(8,128)(2,1)}) custom-call(s32[8]{0:T(128)} %iota.10.order_ref, bf16[8,960,128]{2,1,0:T(8,128)(2,1)} %all-to-all-done.1.q_ref.d_ref.own_ref, bf16[8,960,128]{2,1,0:T(8,128)(2,1)} %all-to-all-done.1.q_ref.d_ref.own_ref, ...), custom_call_target="tpu_custom_call" | custom-call | flops 24159191040 | bytes 6291456 | tf_op jit(solution)/shard_map/attend/pallas_call | solution.py:174
  109.9 0.0 collective-permute-start.4
  109.9 0.6 fusion.order_ref
  110.5 0.0 collective-permute-done.2
  110.5 0.0 copy-done.5
  110.5 0.1 add_convert_fusion.2
  110.6 2.8 %collective-permute-start.6 = (bf16[8,384,128]{2,1,0:T(8,128)(2,1)}, bf16[8,384,128]{2,1,0:T(8,128)(2,1)S(1)}, u32[]{:S(2)}, u32[]{:S(2)}) collective-permute-start(bf16[8,384,128]{2,1,0:T(8,128)(2,1)} %get-tuple-element.40), channel_id=1, source_target_pairs={{16,0},{17,1},{18,2},{19,3},{20,4},{21,5},{22,6},{23,7},{24,8},{25... | collective-permute-start | bytes 2359304 | tf_op jit(solution)/shard_map/ppermute | solution.py:285
  113.4 7.0 %all-to-all-done.2.q_ref.d_ref.own_ref = bf16[8,960,128]{2,1,0:T(8,128)(2,1)S(1)} async-done(((bf16[8,960,128]{2,1,0:T(8,128)(2,1)}), bf16[8,960,128]{2,1,0:T(8,128)(2,1)S(1)}, u32[]{:S(2)}, u32[]{:S(2)}) %all-to-all-start.2) | async-done | bytes 1966112 | tf_op jit(solution)/shard_map/all_to_all | solution.py:274
  120.4 0.0 copy-start.4
  120.4 0.1 collective-permute-start.5
  120.5 0.0 collective-permute-done.4
  120.5 1.9 add_convert_fusion.1
  122.4 0.0 collective-permute-done.1
  122.4 2.4 %pad_maximum_fusion = bf16[8,768,128]{2,1,0:T(8,128)(2,1)} fusion(bf16[8,192,128]{2,1,0:T(8,128)(2,1)S(1)} %add_convert_fusion.1, bf16[8,192,128]{2,1,0:T(8,128)(2,1)S(1)} %add_convert_fusion.2, bf16[8,384,128]{2,1,0:T(8,128)(2,1)} %collective-permute-done.1), kind=kLoop, calls=%fused_computation | loop fusion | flops 4718592 | bytes 3145728 | tf_op jit(solution)/shard_map/concatenate | solution.py:306
  124.8 0.0 copy-done.4
  124.8 5.2 %all-to-all-start.3 = ((bf16[8,768,128]{2,1,0:T(8,128)(2,1)}), bf16[8,768,128]{2,1,0:T(8,128)(2,1)S(1)}, u32[]{:S(2)}, u32[]{:S(2)}) async-start(bf16[8,768,128]{2,1,0:T(8,128)(2,1)} %pad_maximum_fusion), calls=%async_computation.3 | async-start | bytes 3145728 | tf_op jit(solution)/shard_map/all_to_all | solution.py:274
  130.0 0.0 collective-permute-done.5.other_ref
  130.0 23.5 %attend.5 = (bf16[4,384,128]{2,1,0:T(8,128)(2,1)}, bf16[4,384,128]{2,1,0:T(8,128)(2,1)}, f32[8,192,128]{2,1,0:T(8,128)}, bf16[8,192,128]{2,1,0:T(8,128)(2,1)}) custom-call(s32[8]{0:T(128)} %fusion.order_ref, bf16[8,960,128]{2,1,0:T(8,128)(2,1)} %copy-done.4, bf16[8,960,128]{2,1,0:T(8,128)(2,1)} %copy-done.4, bf16[8,960,128]{2,1,0:T(8,128)(2,1)} %copy-done.4, ...), custom_call_target="tpu_custom_call" | custom-call | flops 24159191040 | bytes 6291456 | tf_op jit(solution)/shard_map/attend/pallas_call | solution.py:174
  153.6 0.1 collective-permute-start.7
  153.7 1.9 collective-permute-done.7
  155.6 1.2 add_convert_fusion
  156.8 0.0 copy-start.6
  156.8 0.0 collective-permute-done.6
  156.8 1.1 pad_maximum_fusion.1
  157.9 0.0 all-to-all-done.3.refs_0_.refs_1_
  157.9 7.2 %all-to-all-start.4 = ((bf16[8,576,128]{2,1,0:T(8,128)(2,1)}), bf16[8,576,128]{2,1,0:T(8,128)(2,1)S(1)}, u32[]{:S(2)}, u32[]{:S(2)}) async-start(bf16[8,576,128]{2,1,0:T(8,128)(2,1)} %pad_maximum_fusion.1), calls=%async_computation.4 | async-start | bytes 2359296 | tf_op jit(solution)/shard_map/all_to_all | solution.py:274
  165.1 2.2 collective-permute-start.8
  167.3 0.0 copy-done.6
  167.3 1.9 collective-permute-start.9
  169.2 26.1 %collective-permute-done.8 = bf16[4,384,128]{2,1,0:T(8,128)(2,1)S(1)} collective-permute-done((bf16[4,384,128]{2,1,0:T(8,128)(2,1)}, bf16[4,384,128]{2,1,0:T(8,128)(2,1)S(1)}, u32[]{:S(2)}, u32[]{:S(2)}) %collective-permute-start.8) | collective-permute-done | bytes 393248 | tf_op jit(solution)/shard_map/ppermute | solution.py:285
  195.3 0.0 collective-permute-done.9
  195.3 0.9 pad_maximum_fusion.2
  196.3 0.0 copy-done
  196.3 0.0 all-to-all-done.4.refs_2_.refs_1_
  196.3 5.7 %all-to-all-start.5 = ((bf16[4,768,128]{2,1,0:T(8,128)(2,1)}), bf16[4,768,128]{2,1,0:T(8,128)(2,1)S(1)}, u32[]{:S(2)}, u32[]{:S(2)}) async-start(bf16[4,768,128]{2,1,0:T(8,128)(2,1)} %pad_maximum_fusion.2), calls=%async_computation.5 | async-start | bytes 1572864 | tf_op jit(solution)/shard_map/all_to_all | solution.py:274
  202.0 0.0 copy-done.1
  202.0 6.7 %unpool.1 = (bf16[1,384,3072]{2,1,0:T(8,128)(2,1)}, bf16[1,384,3072]{2,1,0:T(8,128)(2,1)}) custom-call(bf16[8,768,128]{2,1,0:T(8,128)(2,1)} %copy-done, bf16[8,768,128]{2,1,0:T(8,128)(2,1)} %copy-done, bf16[8,576,128]{2,1,0:T(8,128)(2,1)} %copy-done.1), custom_call_target="tpu_custom_call" | custom-call | tf_op jit(solution)/shard_map/unpool/pallas_call | solution.py:229
  208.7 5.7 %all-to-all-done.5.refs_2_ = bf16[4,768,128]{2,1,0:T(8,128)(2,1)S(1)} async-done(((bf16[4,768,128]{2,1,0:T(8,128)(2,1)}), bf16[4,768,128]{2,1,0:T(8,128)(2,1)S(1)}, u32[]{:S(2)}, u32[]{:S(2)}) %all-to-all-start.5) | async-done | bytes 786464 | tf_op jit(solution)/shard_map/all_to_all | solution.py:274
  214.4 0.9 copy-done.2
  215.3 6.0 %place.1 = bf16[1,384,3072]{2,1,0:T(8,128)(2,1)} custom-call(s32[1]{0:T(128)} %bitcast.1.side_ref, bf16[8,768,128]{2,1,0:T(8,128)(2,1)} %copy-done, bf16[8,576,128]{2,1,0:T(8,128)(2,1)} %copy-done.1, bf16[4,768,128]{2,1,0:T(8,128)(2,1)} %copy-done.2), custom_call_target="tpu_custom_call" | custom-call | tf_op jit(solution)/shard_map/place/pallas_call | solution.py:248
  (5 shorter events, 0.1 us)
Async XLA Ops:
  7.5 32.4 %all-to-all-start = ((bf16[8,1008,128]{2,1,0:T(8,128)(2,1)}), bf16[8,1008,128]{2,1,0:T(8,128)(2,1)S(1)}, u32[]{:S(2)}, u32[]{:S(2)}) async-start(bf16[8,1008,128]{2,1,0:T(8,128)(2,1)} %pack_first.1), calls=%async_computation | async-start | bytes 4128768 | tf_op jit(solution)/shard_map/all_to_all | solution.py:274
  39.9 1.3 copy-start.3
  39.9 9.9 %collective-permute-start = (bf16[8,192,128]{2,1,0:T(8,128)(2,1)S(1)}, bf16[8,192,128]{2,1,0:T(8,128)(2,1)S(1)}, u32[]{:S(2)}, u32[]{:S(2)}) collective-permute-start(bf16[8,192,128]{2,1,0:T(8,128)(2,1)S(1)} %slice.9), channel_id=1, source_target_pairs={{0,1},{1,0},{2,3},{3,2},{4,5},{5,4},{6,7},{7,6},{8,9},{9,8},{10,11... | collective-permute-start | bytes 1179656 | tf_op jit(solution)/shard_map/ppermute | solution.py:277
  41.2 32.6 %all-to-all-start.1 = ((bf16[8,960,128]{2,1,0:T(8,128)(2,1)}), bf16[8,960,128]{2,1,0:T(8,128)(2,1)}, u32[]{:S(2)}, u32[]{:S(2)}) async-start(bf16[8,960,128]{2,1,0:T(8,128)(2,1)} %get-tuple-element.34), calls=%async_computation.1 | async-start | bytes 3932160 | tf_op jit(solution)/shard_map/all_to_all | solution.py:274
  49.8 0.7 copy-start.8
  74.9 10.2 %collective-permute-start.3 = (bf16[8,192,128]{2,1,0:T(8,128)(2,1)S(1)}, bf16[8,192,128]{2,1,0:T(8,128)(2,1)S(1)}, u32[]{:S(2)}, u32[]{:S(2)}) collective-permute-start(bf16[8,192,128]{2,1,0:T(8,128)(2,1)S(1)} %slice.10), channel_id=1, source_target_pairs={{0,1},{1,0},{2,3},{3,2},{4,5},{5,4},{6,7},{7,6},{8,9},{9,8},{10,11... | collective-permute-start | bytes 1179656 | tf_op jit(solution)/shard_map/ppermute | solution.py:277
  75.0 47.4 %collective-permute-start.1 = (bf16[8,384,128]{2,1,0:T(8,128)(2,1)}, bf16[8,384,128]{2,1,0:T(8,128)(2,1)}, u32[]{:S(2)}, u32[]{:S(2)}) collective-permute-start(bf16[8,384,128]{2,1,0:T(8,128)(2,1)} %get-tuple-element.31), channel_id=1, source_target_pairs={{16,0},{17,1},{18,2},{19,3},{20,4},{21,5},{22,6},{23,7},{24,8},{25... | collective-permute-start | bytes 2359304 | tf_op jit(solution)/shard_map/ppermute | solution.py:285
  77.6 32.9 %collective-permute-start.2 = (bf16[8,192,128]{2,1,0:T(8,128)(2,1)}, bf16[8,192,128]{2,1,0:T(8,128)(2,1)S(1)}, u32[]{:S(2)}, u32[]{:S(2)}) collective-permute-start(bf16[8,192,128]{2,1,0:T(8,128)(2,1)} %get-tuple-element.33), channel_id=1, source_target_pairs={{0,1},{1,0},{2,3},{3,2},{4,5},{5,4},{6,7},{7,6},{8,9},{9,8},{10,11... | collective-permute-start | bytes 1179656 | tf_op jit(solution)/shard_map/ppermute | solution.py:277
  77.9 42.4 %all-to-all-start.2 = ((bf16[8,960,128]{2,1,0:T(8,128)(2,1)}), bf16[8,960,128]{2,1,0:T(8,128)(2,1)S(1)}, u32[]{:S(2)}, u32[]{:S(2)}) async-start(bf16[8,960,128]{2,1,0:T(8,128)(2,1)} %get-tuple-element.39), calls=%async_computation.2 | async-start | bytes 3932160 | tf_op jit(solution)/shard_map/all_to_all | solution.py:274
  85.1 0.7 copy-start.7
  86.5 24.0 %copy-start.5 = (f32[8,192,128]{2,1,0:T(8,128)S(1)}, f32[8,192,128]{2,1,0:T(8,128)}, u32[]{:S(2)}) copy-start(f32[8,192,128]{2,1,0:T(8,128)} %get-tuple-element.32) | copy-start | bytes 2359300
  109.9 10.6 %collective-permute-start.4 = (bf16[8,192,128]{2,1,0:T(8,128)(2,1)}, bf16[8,192,128]{2,1,0:T(8,128)(2,1)}, u32[]{:S(2)}, u32[]{:S(2)}) collective-permute-start(bf16[8,192,128]{2,1,0:T(8,128)(2,1)} %get-tuple-element.37), channel_id=1, source_target_pairs={{0,1},{1,0},{2,3},{3,2},{4,5},{5,4},{6,7},{7,6},{8,9},{9,8},{10,11... | collective-permute-start | bytes 1179656 | tf_op jit(solution)/shard_map/ppermute | solution.py:277
  110.6 46.2 %collective-permute-start.6 = (bf16[8,384,128]{2,1,0:T(8,128)(2,1)}, bf16[8,384,128]{2,1,0:T(8,128)(2,1)S(1)}, u32[]{:S(2)}, u32[]{:S(2)}) collective-permute-start(bf16[8,384,128]{2,1,0:T(8,128)(2,1)} %get-tuple-element.40), channel_id=1, source_target_pairs={{16,0},{17,1},{18,2},{19,3},{20,4},{21,5},{22,6},{23,7},{24,8},{25... | collective-permute-start | bytes 2359304 | tf_op jit(solution)/shard_map/ppermute | solution.py:285
  120.4 4.4 %copy-start.4 = (bf16[8,960,128]{2,1,0:T(8,128)(2,1)}, bf16[8,960,128]{2,1,0:T(8,128)(2,1)S(1)}, u32[]{:S(2)}) copy-start(bf16[8,960,128]{2,1,0:T(8,128)(2,1)S(1)} %all-to-all-done.2.q_ref.d_ref.own_ref) | copy-start | bytes 5898244
  120.4 9.6 %collective-permute-start.5 = (bf16[8,192,128]{2,1,0:T(8,128)(2,1)S(1)}, bf16[8,192,128]{2,1,0:T(8,128)(2,1)}, u32[]{:S(2)}, u32[]{:S(2)}) collective-permute-start(bf16[8,192,128]{2,1,0:T(8,128)(2,1)S(1)} %slice.11), channel_id=1, source_target_pairs={{0,1},{1,0},{2,3},{3,2},{4,5},{5,4},{6,7},{7,6},{8,9},{9,8},{10,11... | collective-permute-start | bytes 1179656 | tf_op jit(solution)/shard_map/ppermute | solution.py:277
  124.8 33.1 %all-to-all-start.3 = ((bf16[8,768,128]{2,1,0:T(8,128)(2,1)}), bf16[8,768,128]{2,1,0:T(8,128)(2,1)S(1)}, u32[]{:S(2)}, u32[]{:S(2)}) async-start(bf16[8,768,128]{2,1,0:T(8,128)(2,1)} %pad_maximum_fusion), calls=%async_computation.3 | async-start | bytes 3145728 | tf_op jit(solution)/shard_map/all_to_all | solution.py:274
  153.6 2.0 collective-permute-start.7
  156.8 10.5 %copy-start.6 = (bf16[4,384,128]{2,1,0:T(8,128)(2,1)S(1)}, bf16[4,384,128]{2,1,0:T(8,128)(2,1)}, u32[]{:S(2)}) copy-start(bf16[4,384,128]{2,1,0:T(8,128)(2,1)} %get-tuple-element.53) | copy-start | bytes 1179652
  157.9 38.4 %copy-start = (bf16[8,768,128]{2,1,0:T(8,128)(2,1)}, bf16[8,768,128]{2,1,0:T(8,128)(2,1)S(1)}, u32[]{:S(2)}) copy-start(bf16[8,768,128]{2,1,0:T(8,128)(2,1)S(1)} %all-to-all-done.3.refs_0_.refs_1_) | copy-start | bytes 4718596
  157.9 38.4 %all-to-all-start.4 = ((bf16[8,576,128]{2,1,0:T(8,128)(2,1)}), bf16[8,576,128]{2,1,0:T(8,128)(2,1)S(1)}, u32[]{:S(2)}, u32[]{:S(2)}) async-start(bf16[8,576,128]{2,1,0:T(8,128)(2,1)} %pad_maximum_fusion.1), calls=%async_computation.4 | async-start | bytes 2359296 | tf_op jit(solution)/shard_map/all_to_all | solution.py:274
  165.1 30.2 %collective-permute-start.8 = (bf16[4,384,128]{2,1,0:T(8,128)(2,1)}, bf16[4,384,128]{2,1,0:T(8,128)(2,1)S(1)}, u32[]{:S(2)}, u32[]{:S(2)}) collective-permute-start(bf16[4,384,128]{2,1,0:T(8,128)(2,1)} %get-tuple-element.51), channel_id=1, source_target_pairs={{16,0},{17,1},{18,2},{19,3},{20,4},{21,5},{22,6},{23,7},{24,8},{25... | collective-permute-start | bytes 1179656 | tf_op jit(solution)/shard_map/ppermute | solution.py:285
  167.3 28.0 %collective-permute-start.9 = (bf16[4,384,128]{2,1,0:T(8,128)(2,1)S(1)}, bf16[4,384,128]{2,1,0:T(8,128)(2,1)S(1)}, u32[]{:S(2)}, u32[]{:S(2)}) collective-permute-start(bf16[4,384,128]{2,1,0:T(8,128)(2,1)S(1)} %copy-done.6), channel_id=1, source_target_pairs={{16,8},{17,9},{18,10},{19,11},{20,12},{21,13},{22,14},{23,15},{24,... | collective-permute-start | bytes 1179656 | tf_op jit(solution)/shard_map/ppermute | solution.py:285
  196.3 5.7 %copy-start.1 = (bf16[8,576,128]{2,1,0:T(8,128)(2,1)}, bf16[8,576,128]{2,1,0:T(8,128)(2,1)S(1)}, u32[]{:S(2)}) copy-start(bf16[8,576,128]{2,1,0:T(8,128)(2,1)S(1)} %all-to-all-done.4.refs_2_.refs_1_) | copy-start | bytes 3538948
  196.3 18.1 %all-to-all-start.5 = ((bf16[4,768,128]{2,1,0:T(8,128)(2,1)}), bf16[4,768,128]{2,1,0:T(8,128)(2,1)S(1)}, u32[]{:S(2)}, u32[]{:S(2)}) async-start(bf16[4,768,128]{2,1,0:T(8,128)(2,1)} %pad_maximum_fusion.2), calls=%async_computation.5 | async-start | bytes 1572864 | tf_op jit(solution)/shard_map/all_to_all | solution.py:274
  214.4 0.9 copy-start.2

commit v3 on v2

v3 whole, which is shorter than its diff:
```python
import functools

import jax
import jax.numpy as jnp
from jax import lax
from jax.experimental import pallas as pl
from jax.experimental.pallas import tpu as pltpu
from jax.sharding import PartitionSpec as P

HD = 128
CHIPS = 8
CORES = 2
HEADS_CHIP = 3
TOK = 384
POOL = 96
ROW = 192
WIDE = HEADS_CHIP * HD
KTILES = CHIPS * CORES
KEYS = KTILES * POOL
SCALE = 1.0 / HD**0.5
LOG2E = 1.4426950408889634
BLOCKED = -1e30
LINE = 4
PAIR = 2
WIDTH = PAIR * TOK
KV_AT = 2 * TOK
BIAS_AT = KV_AT + 2 * POOL
BIAS_ROWS = KTILES * (TOK // HD)
NN = (((1,), (0,)), ((), ()))
NT = (((1,), (1,)), ((), ()))
TN = (((0,), (0,)), ((), ()))


def dot(a, b, dims):
    return lax.dot_general(a, b, dims, preferred_element_type=jnp.float32)


def pool_matrix(shape, token_dim):
    token = lax.broadcasted_iota(jnp.int32, shape, token_dim)
    pooled = lax.broadcasted_iota(jnp.int32, shape, 1 - token_dim)
    column = jnp.where(token >= ROW, token - ROW, token)
    return jnp.where(column // 2 == pooled, 1.0, 0.0).astype(jnp.bfloat16)


def pack_head(pool, out_ref, q, d, k, v):
    out_ref[0, :TOK] = q
    out_ref[0, TOK:KV_AT] = d
    out_ref[0, KV_AT : KV_AT + POOL] = (dot(pool, k, NN) * 0.25).astype(jnp.bfloat16)
    out_ref[0, KV_AT + POOL : BIAS_AT] = (dot(pool, v, NN) * 0.25).astype(jnp.bfloat16)


def pack_first_kernel(core_ref, mask_ref, *rest):
    out_ref, pool, bias = rest[-3:]

    @pl.when(pl.program_id(0) == 0)
    def _():
        pool[...] = pool_matrix((POOL, TOK), 1)
        for block in range(TOK // HD):
            token = lax.broadcasted_iota(jnp.int32, (1, HD), 1) + block * HD
            for at in range(KTILES):
                tile = at % CHIPS * CORES + (at // CHIPS + core_ref[0]) % CORES
                upper = jnp.where(mask_ref[0, tile] > 0, 0.0, BLOCKED)
                lower = jnp.where(mask_ref[1, tile] > 0, 0.0, BLOCKED)
                row = block * KTILES + at
                bias[row : row + 1] = jnp.where(token < ROW, upper, lower)

    for chip in range(PAIR):
        pack_head(pool[...], out_ref.at[chip : chip + 1], *[r[0] for r in rest[4 * chip : 4 * chip + 4]])
        out_ref[chip, BIAS_AT:] = bias[...].astype(jnp.bfloat16)


def pack_first(core, tile_mask, arrays):
    rows = BIAS_AT + BIAS_ROWS
    scalars = pl.BlockSpec(memory_space=pltpu.SMEM)
    return pl.pallas_call(
        pack_first_kernel,
        grid=(CHIPS // PAIR,),
        in_specs=[scalars, scalars]
        + [
            pl.BlockSpec((1, TOK, HD), lambda j, chip=chip: (0, 0, HEADS_CHIP * (PAIR * j + chip)))
            for chip in range(PAIR)
            for _ in arrays
        ],
        out_specs=pl.BlockSpec((PAIR, rows, HD), lambda j: (j, 0, 0)),
        out_shape=jax.ShapeDtypeStruct((CHIPS, rows, HD), jnp.bfloat16),
        scratch_shapes=[pltpu.VMEM((POOL, TOK), jnp.bfloat16), pltpu.VMEM((BIAS_ROWS, HD), jnp.float32)],
        name="pack_first",
    )(core, tile_mask, *[*arrays] * PAIR)


def pack_rest_kernel(q_ref, d_ref, k_ref, v_ref, *rest):
    out_refs, pool = rest[:-1], rest[-1]

    @pl.when(pl.program_id(0) == 0)
    def _():
        pool[...] = pool_matrix((POOL, TOK), 1)

    for head, out_ref in enumerate(out_refs, 1):
        columns = slice(head * HD, (head + 1) * HD)
        pack_head(pool[...], out_ref, *[r[0, :, columns] for r in (q_ref, d_ref, k_ref, v_ref)])


def pack_rest(arrays):
    late = HEADS_CHIP - 1
    return pl.pallas_call(
        pack_rest_kernel,
        grid=(CHIPS,),
        in_specs=[pl.BlockSpec((1, TOK, WIDE), lambda j: (0, 0, j))] * 4,
        out_specs=[pl.BlockSpec((1, BIAS_AT, HD), lambda j: (j, 0, 0))] * late,
        out_shape=[jax.ShapeDtypeStruct((CHIPS, BIAS_AT, HD), jnp.bfloat16)] * late,
        scratch_shapes=[pltpu.VMEM((POOL, TOK), jnp.bfloat16)],
        name="pack_rest",
    )(*arrays)


def attend_kernel(side_ref, q_ref, d_ref, own_ref, other_ref, bias_ref, *rest):
    dq_refs, dkv_refs = rest[:-8], rest[-8:-6]
    keys, values, dkeys, dvalues, expo, dprob = rest[-6:]
    step = pl.program_id(0)

    @pl.when(step == 0)
    def _():
        for s in range(CHIPS):
            for half, ref in enumerate((own_ref, other_ref)):
                at = (half * CHIPS + s) * POOL
                keys[at : at + POOL] = ref[s, :POOL]
                values[at : at + POOL] = ref[s, POOL:]
        dkeys[...] = jnp.zeros_like(dkeys)
        dvalues[...] = jnp.zeros_like(dvalues)

    q = q_ref[...].reshape(WIDTH, HD)
    d = d_ref[...].reshape(WIDTH, HD)
    blocks = [
        bias_ref[owner, at : at + KTILES].astype(jnp.float32)
        for owner in range(PAIR)
        for at in range(0, BIAS_ROWS, KTILES)
    ]
    bias = jnp.concatenate(blocks, axis=1)
    part = 4 * POOL
    top = jnp.full((8, WIDTH), -3e38, jnp.float32)
    for at in range(0, KEYS, part):
        scores = dot(keys[at : at + part], q, NT)
        for tile in range(part // POOL):
            row = at // POOL + tile
            one = scores[tile * POOL : (tile + 1) * POOL] + bias[row : row + 1]
            expo[at + tile * POOL : at + (tile + 1) * POOL] = one
            top = jnp.maximum(top, jnp.max(one.reshape(POOL // 8, 8, WIDTH), axis=0))
    top = jnp.max(top, axis=0, keepdims=True)
    total = jnp.zeros((8, WIDTH), jnp.float32)
    weighted = jnp.zeros((8, WIDTH), jnp.float32)
    for at in range(0, KEYS, part):
        grad = dot(values[at : at + part], d, NT)
        e = jnp.exp2((expo[at : at + part] - top) * (SCALE * LOG2E))
        expo[at : at + part] = e
        dprob[at : at + part] = grad
        total = total + jnp.sum(e.reshape(part // 8, 8, WIDTH), axis=0)
        weighted = weighted + jnp.sum((e * grad).reshape(part // 8, 8, WIDTH), axis=0)
    inverse = 1.0 / jnp.sum(total, axis=0, keepdims=True)
    delta = jnp.sum(weighted, axis=0, keepdims=True) * inverse
    scaled = inverse * SCALE
    dq = jnp.zeros((WIDTH, HD), jnp.float32)
    for at in range(0, KEYS, part):
        e = expo[at : at + part]
        probs = (e * inverse).astype(jnp.bfloat16)
        sgrad = ((e * scaled) * (dprob[at : at + part] - delta)).astype(jnp.bfloat16)
        dvalues[at : at + part] += dot(probs, d, NN)
        dkeys[at : at + part] += dot(sgrad, q, NN)
        dq = dq + dot(sgrad, keys[at : at + part], TN)
    each = CHIPS // PAIR // len(dq_refs)
    for k, ref in enumerate(dq_refs):

        @pl.when(step // each == k)
        def _():
            ref[...] = dq.astype(jnp.bfloat16).reshape(PAIR, TOK, HD)

    @pl.when(step == CHIPS // PAIR - 1)
    def _():
        for half, ref in enumerate(dkv_refs):
            for s in range(CHIPS):
                at = (half * CHIPS + s) * POOL
                ref[s, :POOL] = dkeys[at : at + POOL].astype(ref.dtype)
                ref[s, POOL:] = dvalues[at : at + POOL].astype(ref.dtype)


def attend(side, data, first, kv_other, parts):
    each = CHIPS // PAIR // parts
    half = LINE // PAIR

    def owners(k, side):
        return (k // half + side[0]) % 2 * half + k % half

    terms = pl.BlockSpec((CHIPS, 2 * POOL, HD), lambda k, side: (0, 0, 0))
    return pl.pallas_call(
        attend_kernel,
        grid_spec=pltpu.PrefetchScalarGridSpec(
            num_scalar_prefetch=1,
            grid=(CHIPS // PAIR,),
            in_specs=[
                pl.BlockSpec((PAIR, TOK, HD), lambda k, side: (owners(k, side), 0, 0)),
                pl.BlockSpec((PAIR, TOK, HD), lambda k, side: (owners(k, side), 1, 0)),
                pl.BlockSpec((CHIPS, 2 * POOL, HD), lambda k, side: (0, KV_AT // (2 * POOL), 0)),
                terms,
                pl.BlockSpec((PAIR, BIAS_ROWS, HD), lambda k, side: (owners(k, side), BIAS_AT // BIAS_ROWS, 0)),
            ],
            out_specs=[
                pl.BlockSpec((PAIR, TOK, HD), lambda k, side, at=at: (jnp.clip(k - at, 0, each - 1), 0, 0))
                for at in range(0, CHIPS // PAIR, each)
            ]
            + [terms, terms],
            scratch_shapes=[
                pltpu.VMEM((KEYS, HD), jnp.bfloat16),
                pltpu.VMEM((KEYS, HD), jnp.bfloat16),
                pltpu.VMEM((KEYS, HD), jnp.float32),
                pltpu.VMEM((KEYS, HD), jnp.float32),
                pltpu.VMEM((KEYS, WIDTH), jnp.float32),
                pltpu.VMEM((KEYS, WIDTH), jnp.float32),
            ],
        ),
        out_shape=[jax.ShapeDtypeStruct((PAIR * each, TOK, HD), jnp.bfloat16)] * parts
        + [jax.ShapeDtypeStruct((CHIPS, 2 * POOL, HD), t) for t in (jnp.float32, jnp.bfloat16)],
        compiler_params=pltpu.CompilerParams(vmem_limit_bytes=60 * 2**20),
        cost_estimate=pl.CostEstimate(
            flops=40 * CHIPS * TOK * KEYS * HD,
            bytes_accessed=6 * 2**20,
            transcendentals=CHIPS * TOK * KEYS,
        ),
        name="attend",
    )(side, data, data, data, kv_other, first)


def unpool_kernel(*refs):
    dkv_refs, (dk_ref, dv_ref, spread) = refs[:-3], refs[-3:]

    @pl.when(pl.program_id(0) == 0)
    def _():
        spread[...] = pool_matrix((TOK, POOL), 0)

    for chip in range(PAIR):
        for head, ref in enumerate(dkv_refs):
            at = chip * WIDE + head * HD
            part = ref[chip] * jnp.bfloat16(0.25)
            dk_ref[0, :, at : at + HD] = dot(spread[...], part[:POOL], NN).astype(jnp.bfloat16)
            dv_ref[0, :, at : at + HD] = dot(spread[...], part[POOL:], NN).astype(jnp.bfloat16)


def unpool(pieces):
    column = pl.BlockSpec((1, TOK, PAIR * WIDE), lambda s: (0, 0, s))
    whole = jax.ShapeDtypeStruct((1, TOK, CHIPS * WIDE), jnp.bfloat16)
    return pl.pallas_call(
        unpool_kernel,
        grid=(CHIPS // PAIR,),
        in_specs=[
            pl.BlockSpec((PAIR, 2 * POOL, HD), lambda s, at=at // (2 * POOL): (s, at, 0)) for _, at in pieces
        ],
        out_specs=[column, column],
        out_shape=[whole, whole],
        scratch_shapes=[pltpu.VMEM((TOK, POOL), jnp.bfloat16)],
        name="unpool",
    )(*[piece for piece, _ in pieces])


def place_kernel(side_ref, *refs):
    for chip in range(PAIR):
        for head, ref in enumerate(refs[:-1]):
            at = chip * WIDE + head * HD
            refs[-1][0, :, at : at + HD] = ref[chip]


def place(side, by_chip, by_line):
    def line(head):
        per = LINE // PAIR
        return lambda s, side: (s % per, 2 * head + (s // per + side[0]) % 2, 0)

    return pl.pallas_call(
        place_kernel,
        grid_spec=pltpu.PrefetchScalarGridSpec(
            num_scalar_prefetch=1,
            grid=(CHIPS // PAIR,),
            in_specs=[pl.BlockSpec((PAIR, TOK, HD), lambda s, side: (s, 0, 0))]
            + [pl.BlockSpec((PAIR, TOK, HD), line(head)) for head in range(HEADS_CHIP - 1)],
            out_specs=pl.BlockSpec((1, TOK, PAIR * WIDE), lambda s, side: (0, 0, s)),
        ),
        out_shape=jax.ShapeDtypeStruct((1, TOK, CHIPS * WIDE), jnp.bfloat16),
        name="place",
    )(side, by_chip, by_line, by_line)


def after(value, *others):
    return lax.optimization_barrier((value, *others))[0]


def shards(query, key, value, out_grad, tile_mask, sections):
    here = lax.axis_index("ctx")
    core, side = here % CORES, here // (CORES * LINE)
    members = range(CHIPS * CORES)
    groups = [[i for i in members if i % CORES == c] for c in range(CORES)]

    lines = [group[at : at + LINE] for group in groups for at in (0, LINE)]

    def trade(data, among=groups):
        return lax.all_to_all(data, "ctx", 0, 0, axis_index_groups=among, tiled=True)

    def swap(data):
        return lax.ppermute(data, "ctx", [(i, i ^ 1) for i in members])

    def to_previous(data, across=0):
        pairs = [
            (section * KTILES + i, (section - 1) * KTILES + (i + across * LINE * CORES) % KTILES)
            for section in range(1, sections)
            for i in members
        ]
        return lax.ppermute(data, ("section", "ctx"), pairs)

    def kv_of(data):
        return swap(data[:, KV_AT:BIAS_AT])

    def summed(own, foreign):
        return (own + foreign.astype(jnp.float32)).astype(jnp.bfloat16)

    arrays = (query, out_grad, key, value)
    sent = [pack_first(core.reshape(1), tile_mask, arrays), *pack_rest(arrays)]
    first = after(trade(sent[0]), sent[1])

    side = side.reshape(1)
    dq, own, foreign = attend(jnp.zeros((1,), jnp.int32), first, first, kv_of(first), 1)
    moved, terms = [to_previous(dq)], [(own, swap(foreign))]
    data = after(trade(after(sent[1], first)), dq)
    near, far, own, foreign = attend(side, data, first, kv_of(data), 2)
    moved += [to_previous(near), to_previous(far, 1)]
    terms.append((own, swap(foreign)))
    data = after(trade(after(sent[2], data)), near)
    joined = jnp.concatenate([moved[0], summed(*terms[0]), summed(*terms[1])], axis=1)
    near, far, own, foreign = attend(side, after(data, joined), first, kv_of(data), 2)
    early = after(trade(after(joined, data)), near)
    moved += [to_previous(after(near, *moved[1:])), to_previous(after(far, *moved[1:]), 1)]
    middle = trade(after(summed(own, swap(foreign)), early))
    late = trade(after(jnp.concatenate(moved[1:], axis=1), middle), lines)
    key_grad, value_grad = unpool([(early, TOK), (early, TOK + 2 * POOL), (middle, 0)])
    upstream = place(side, early, late)
    return key_grad, value_grad, upstream


def solution(mesh):
    spec = P("section", "ctx", None)
    return jax.shard_map(
        functools.partial(shards, sections=mesh.shape["section"]),
        mesh=mesh,
        in_specs=(spec, spec, spec, spec, P("ctx", None)),
        out_specs=(spec, spec, spec),
        check_vma=False,
    )
```

time: 223 us -> 208 us (0.933)
  Pallas kernels: 98.2 us -> 87.9 us
  waiting for transfers between devices: 57.6 us -> 52.2 us
    ppermute x4 -> x5, waiting for transfers between devices: 26.1 us -> 10.1 us  [to_previous(): return lax.ppermute(data, ('section', 'ctx'), pairs)]
    all_to_all x6, waiting for transfers between devices: 29.6 us -> 42.1 us  [trade(): lax.all_to_all(data, 'ctx', 0, 0, axis_index_groups=among, tiled=True)]
    pallas_call x3, Pallas kernels: 70.3 us -> 66 us  [attend(): pl.pallas_call(attend_kernel, grid_spec=pltpu.PrefetchScalarGridSpec(num_...]
    pallas_call x2, Pallas kernels: 13.6 us -> 9.66 us  [the longest x1 4.98 us: unpool(): pl.pallas_call(unpool_kernel, grid=(CHIPS // PAIR,), in_specs=[pl.BlockSp...]
    ppermute x4 -> x5, starting transfers between devices: 9.53 us -> 10.4 us  [to_previous(): return lax.ppermute(data, ('section', 'ctx'), pairs)]
  transfers between devices with their start and end apart: 16 -> 17, of which waited for: 5 -> 6; matrix products, arithmetic and copies ran while one was open for 4% -> 4% of each run, Pallas kernels for 39% -> 38%
where the time goes in v3:
time: 208 us; the launch traced here: 206 us
  Pallas kernels  87.9 us (42%)
  starting transfers between devices  52.3 us (25%)
  waiting for transfers between devices  52.2 us (25%)
  other arithmetic  7.58 us (4%)
  local copies, waits for them, and re-layouts  4.91 us (2%)
    pallas_call x3, Pallas kernels, attend(): pl.pallas_call(attend_kernel, grid_spec=pltpu.PrefetchScalarGridSpec(num_...  66 us
    all_to_all x6, waiting for transfers between devices, trade(): lax.all_to_all(data, 'ctx', 0, 0, axis_index_groups=among, tiled=True)  42.1 us
    all_to_all x6, starting transfers between devices, trade(): lax.all_to_all(data, 'ctx', 0, 0, axis_index_groups=among, tiled=True)  41.2 us
    ppermute x5, starting transfers between devices, to_previous(): return lax.ppermute(data, ('section', 'ctx'), pairs)  10.4 us
    ppermute x5, waiting for transfers between devices, to_previous(): return lax.ppermute(data, ('section', 'ctx'), pairs)  10.1 us
    pallas_call x1, Pallas kernels, pack_rest(): pl.pallas_call(pack_rest_kernel, grid=(CHIPS,), in_specs=[pl.BlockSpec((1...  8.23 us
    pallas_call x1, Pallas kernels, unpool(): pl.pallas_call(unpool_kernel, grid=(CHIPS // PAIR,), in_specs=[pl.BlockSp...  4.98 us
    pallas_call x1, Pallas kernels, pack_first(): pl.pallas_call(pack_first_kernel, grid=(CHIPS // PAIR,), in_specs=[scalar...  4.68 us
  transfers between devices with their start and end apart: 17, of which 6 were waited for; matrix products, arithmetic and copies ran while one was open for 4% of the time, Pallas kernels for 38%

profile of v3, /device:TPU:56, one launch (start us, length us, event | category | flops | bytes accessed | tf_op | source)
XLA Modules:
  0.0 205.8 jit_solution(13308909158017687986)
XLA Ops:
  0.6 4.7 %pack_first.1 = bf16[8,1008,128]{2,1,0:T(8,128)(2,1)} custom-call(s32[1]{0:T(128)} %bitcast.core_ref, s32[2,16]{1,0:T(2,128)} %mask_ref.1, bf16[1,384,3072]{2,1,0:T(8,128)(2,1)} %q_ref.1, bf16[1,384,3072]{2,1,0:T(8,128)(2,1)} %d_ref.1, bf16[1,384,3072]{2,1,0:T(8,128)(2,1)} %k_ref.1, bf16[1,384,3072]{2,1,0:T(8,128)(2,1)} %v_ref.1, ...), custom_call_target="tpu_custom_call" | custom-call | tf_op jit(solution)/shard_map/pack_first/pallas_call | solution.py:75
  5.3 7.3 %all-to-all-start = ((bf16[8,1008,128]{2,1,0:T(8,128)(2,1)}), bf16[8,1008,128]{2,1,0:T(8,128)(2,1)S(1)}, u32[]{:S(2)}, u32[]{:S(2)}) async-start(bf16[8,1008,128]{2,1,0:T(8,128)(2,1)} %pack_first.1), calls=%async_computation | async-start | bytes 4128768 | tf_op jit(solution)/shard_map/all_to_all | solution.py:301
  12.6 8.2 %pack_rest.1 = (bf16[8,960,128]{2,1,0:T(8,128)(2,1)}, bf16[8,960,128]{2,1,0:T(8,128)(2,1)}) custom-call(bf16[1,384,3072]{2,1,0:T(8,128)(2,1)} %q_ref.1, bf16[1,384,3072]{2,1,0:T(8,128)(2,1)} %d_ref.1, bf16[1,384,3072]{2,1,0:T(8,128)(2,1)} %k_ref.1, bf16[1,384,3072]{2,1,0:T(8,128)(2,1)} %v_ref.1), custom_call_target="tpu_custom_call" | custom-call | tf_op jit(solution)/shard_map/pack_rest/pallas_call | solution.py:105
  20.8 16.9 %all-to-all-done.q_ref.d_ref.own_ref.bias_ref = bf16[8,1008,128]{2,1,0:T(8,128)(2,1)S(1)} async-done(((bf16[8,1008,128]{2,1,0:T(8,128)(2,1)}), bf16[8,1008,128]{2,1,0:T(8,128)(2,1)S(1)}, u32[]{:S(2)}, u32[]{:S(2)}) %all-to-all-start) | async-done | bytes 2064416 | tf_op jit(solution)/shard_map/all_to_all | solution.py:301
  37.7 0.0 copy-start.2
  37.7 0.1 collective-permute-start
  37.8 1.2 copy-done.2
  39.0 8.6 %all-to-all-start.1 = ((bf16[8,960,128]{2,1,0:T(8,128)(2,1)}), bf16[8,960,128]{2,1,0:T(8,128)(2,1)}, u32[]{:S(2)}, u32[]{:S(2)}) async-start(bf16[8,960,128]{2,1,0:T(8,128)(2,1)} %get-tuple-element.35), calls=%async_computation.1 | async-start | bytes 3932160 | tf_op jit(solution)/shard_map/all_to_all | solution.py:301
  47.7 0.0 collective-permute-done.other_ref
  47.7 0.0 copy-start.7
  47.7 0.7 copy-done.7
  48.4 21.8 %attend.3 = (bf16[8,384,128]{2,1,0:T(8,128)(2,1)}, f32[8,192,128]{2,1,0:T(8,128)}, bf16[8,192,128]{2,1,0:T(8,128)(2,1)}) custom-call(s32[1]{0:T(128)} %constant.25.clone.1.side_ref, bf16[8,1008,128]{2,1,0:T(8,128)(2,1)} %copy-done.2, bf16[8,1008,128]{2,1,0:T(8,128)(2,1)} %copy-done.2, bf16[8,1008,128]{2,1,0:T(8,128)(2,1)} %copy-done.2, ...), custom_call_target="tpu_custom_call" | custom-call | flops 24159191040 | bytes 6291456 | tf_op jit(solution)/shard_map/attend/pallas_call | solution.py:193
  70.2 1.1 all-to-all-done.1.q_ref.d_ref.own_ref
  71.3 1.0 slice.10
  72.3 0.1 collective-permute-start.3
  72.5 2.7 %collective-permute-start.1 = (bf16[8,384,128]{2,1,0:T(8,128)(2,1)}, bf16[8,384,128]{2,1,0:T(8,128)(2,1)}, u32[]{:S(2)}, u32[]{:S(2)}) collective-permute-start(bf16[8,384,128]{2,1,0:T(8,128)(2,1)} %get-tuple-element.32), channel_id=1, source_target_pairs={{16,0},{17,1},{18,2},{19,3},{20,4},{21,5},{22,6},{23,7},{24,8},{25... | collective-permute-start | bytes 2359304 | tf_op jit(solution)/shard_map/ppermute | solution.py:312
  75.1 0.3 collective-permute-start.2
  75.4 7.1 %all-to-all-start.2 = ((bf16[8,960,128]{2,1,0:T(8,128)(2,1)}), bf16[8,960,128]{2,1,0:T(8,128)(2,1)S(1)}, u32[]{:S(2)}, u32[]{:S(2)}) async-start(bf16[8,960,128]{2,1,0:T(8,128)(2,1)} %get-tuple-element.40), calls=%async_computation.2 | async-start | bytes 3932160 | tf_op jit(solution)/shard_map/all_to_all | solution.py:301
  82.5 0.0 collective-permute-done.3.other_ref
  82.5 0.0 copy-start.6
  82.5 0.7 copy-done.6
  83.2 0.0 copy-start.5
  83.2 22.1 %attend.4 = (bf16[4,384,128]{2,1,0:T(8,128)(2,1)}, bf16[4,384,128]{2,1,0:T(8,128)(2,1)}, f32[8,192,128]{2,1,0:T(8,128)}, bf16[8,192,128]{2,1,0:T(8,128)(2,1)}) custom-call(s32[1]{0:T(128)} %bitcast.1.side_ref, bf16[8,960,128]{2,1,0:T(8,128)(2,1)} %all-to-all-done.1.q_ref.d_ref.own_ref, bf16[8,960,128]{2,1,0:T(8,128)(2,1)} %all-to-all-done.1.q_ref.d_ref.own_ref, ...), custom_call_target="tpu_custom_call" | custom-call | flops 24159191040 | bytes 6291456 | tf_op jit(solution)/shard_map/attend/pallas_call | solution.py:193
  105.4 0.1 collective-permute-start.4
  105.5 0.0 collective-permute-done.2
  105.5 0.0 copy-done.5
  105.5 0.1 add_convert_fusion.2
  105.6 1.9 collective-permute-start.8
  107.5 1.9 collective-permute-start.7
  109.5 8.8 %all-to-all-done.2.q_ref.d_ref.own_ref = bf16[8,960,128]{2,1,0:T(8,128)(2,1)S(1)} async-done(((bf16[8,960,128]{2,1,0:T(8,128)(2,1)}), bf16[8,960,128]{2,1,0:T(8,128)(2,1)S(1)}, u32[]{:S(2)}, u32[]{:S(2)}) %all-to-all-start.2) | async-done | bytes 1966112 | tf_op jit(solution)/shard_map/all_to_all | solution.py:301
  118.3 0.0 copy-start.3
  118.3 0.1 collective-permute-start.5
  118.4 0.0 collective-permute-done.4
  118.4 1.9 add_convert_fusion.1
  120.3 0.0 collective-permute-done.1
  120.3 2.4 %pad_maximum_fusion = bf16[8,768,128]{2,1,0:T(8,128)(2,1)} fusion(bf16[8,192,128]{2,1,0:T(8,128)(2,1)S(1)} %add_convert_fusion.1, bf16[8,192,128]{2,1,0:T(8,128)(2,1)S(1)} %add_convert_fusion.2, bf16[8,384,128]{2,1,0:T(8,128)(2,1)} %collective-permute-done.1), kind=kLoop, calls=%fused_computation | loop fusion | flops 4718592 | bytes 3145728 | tf_op jit(solution)/shard_map/concatenate | solution.py:332
  122.7 0.0 copy-done.3
  122.7 5.1 %all-to-all-start.3 = ((bf16[8,768,128]{2,1,0:T(8,128)(2,1)}), bf16[8,768,128]{2,1,0:T(8,128)(2,1)S(1)}, u32[]{:S(2)}, u32[]{:S(2)}) async-start(bf16[8,768,128]{2,1,0:T(8,128)(2,1)} %pad_maximum_fusion), calls=%async_computation.3 | async-start | bytes 3145728 | tf_op jit(solution)/shard_map/all_to_all | solution.py:301
  127.8 0.0 collective-permute-done.5.other_ref
  127.8 22.0 %attend.5 = (bf16[4,384,128]{2,1,0:T(8,128)(2,1)}, bf16[4,384,128]{2,1,0:T(8,128)(2,1)}, f32[8,192,128]{2,1,0:T(8,128)}, bf16[8,192,128]{2,1,0:T(8,128)(2,1)}) custom-call(s32[1]{0:T(128)} %bitcast.1.side_ref, bf16[8,960,128]{2,1,0:T(8,128)(2,1)} %copy-done.3, bf16[8,960,128]{2,1,0:T(8,128)(2,1)} %copy-done.3, bf16[8,960,128]{2,1,0:T(8,128)(2,1)} %copy-done.3, ...), custom_call_target="tpu_custom_call" | custom-call | flops 24159191040 | bytes 6291456 | tf_op jit(solution)/shard_map/attend/pallas_call | solution.py:193
  149.9 0.1 collective-permute-start.6
  150.0 0.0 collective-permute-done.8
  150.0 0.0 collective-permute-done.7
  150.0 1.9 collective-permute-start.9
  151.9 1.9 collective-permute-start.10
  153.9 0.0 collective-permute-done.6
  153.9 2.0 add_convert_fusion
  155.8 0.0 all-to-all-done.3.refs_0_.refs_1_
  155.9 0.0 copy-start
  155.9 7.8 %all-to-all-start.4 = ((bf16[8,192,128]{2,1,0:T(8,128)(2,1)}), bf16[8,192,128]{2,1,0:T(8,128)(2,1)S(1)}, u32[]{:S(2)}, u32[]{:S(2)}) async-start(bf16[8,192,128]{2,1,0:T(8,128)(2,1)} %add_convert_fusion), calls=%async_computation.4 | async-start | bytes 786432 | tf_op jit(solution)/shard_map/all_to_all | solution.py:301
  163.6 7.9 %collective-permute-done.9 = bf16[4,384,128]{2,1,0:T(8,128)(2,1)S(1)} collective-permute-done((bf16[4,384,128]{2,1,0:T(8,128)(2,1)}, bf16[4,384,128]{2,1,0:T(8,128)(2,1)S(1)}, u32[]{:S(2)}, u32[]{:S(2)}) %collective-permute-start.9) | collective-permute-done | bytes 393248 | tf_op jit(solution)/shard_map/ppermute | solution.py:312
  171.5 2.2 %collective-permute-done.10 = bf16[4,384,128]{2,1,0:T(8,128)(2,1)S(1)} collective-permute-done((bf16[4,384,128]{2,1,0:T(8,128)(2,1)}, bf16[4,384,128]{2,1,0:T(8,128)(2,1)S(1)}, u32[]{:S(2)}, u32[]{:S(2)}) %collective-permute-start.10) | collective-permute-done | bytes 393248 | tf_op jit(solution)/shard_map/ppermute | solution.py:312
  173.7 1.2 pad_maximum_fusion.1
  174.9 0.0 all-to-all-done.4.refs_2_
  174.9 0.0 copy-start.4
  174.9 0.0 copy-done
  174.9 5.4 %all-to-all-start.5 = ((bf16[4,1536,128]{2,1,0:T(8,128)(2,1)}), bf16[4,1536,128]{2,1,0:T(8,128)(2,1)S(1)}, u32[]{:S(2)}, u32[]{:S(2)}) async-start(bf16[4,1536,128]{2,1,0:T(8,128)(2,1)} %pad_maximum_fusion.1), calls=%async_computation.5 | async-start | bytes 3145728 | tf_op jit(solution)/shard_map/all_to_all | solution.py:301
  180.3 0.0 copy-done.4
  180.3 5.0 %unpool.1 = (bf16[1,384,3072]{2,1,0:T(8,128)(2,1)}, bf16[1,384,3072]{2,1,0:T(8,128)(2,1)}) custom-call(bf16[8,768,128]{2,1,0:T(8,128)(2,1)} %copy-done, bf16[8,768,128]{2,1,0:T(8,128)(2,1)} %copy-done, bf16[8,192,128]{2,1,0:T(8,128)(2,1)} %copy-done.4), custom_call_target="tpu_custom_call" | custom-call | tf_op jit(solution)/shard_map/unpool/pallas_call | solution.py:249
  185.3 15.3 %all-to-all-done.5.refs_1_.refs_2_ = bf16[4,1536,128]{2,1,0:T(8,128)(2,1)S(1)} async-done(((bf16[4,1536,128]{2,1,0:T(8,128)(2,1)}), bf16[4,1536,128]{2,1,0:T(8,128)(2,1)S(1)}, u32[]{:S(2)}, u32[]{:S(2)}) %all-to-all-start.5) | async-done | bytes 1572896 | tf_op jit(solution)/shard_map/all_to_all | solution.py:301
  200.6 0.0 copy-start.1
  200.6 1.1 copy-done.1
  201.7 4.0 %place.1 = bf16[1,384,3072]{2,1,0:T(8,128)(2,1)} custom-call(s32[1]{0:T(128)} %bitcast.1.side_ref, bf16[8,768,128]{2,1,0:T(8,128)(2,1)} %copy-done, bf16[4,1536,128]{2,1,0:T(8,128)(2,1)} %copy-done.1, bf16[4,1536,128]{2,1,0:T(8,128)(2,1)} %copy-done.1), custom_call_target="tpu_custom_call" | custom-call | tf_op jit(solution)/shard_map/place/pallas_call | solution.py:274
  (2 shorter events, 0.1 us)
Async XLA Ops:
  5.3 32.4 %all-to-all-start = ((bf16[8,1008,128]{2,1,0:T(8,128)(2,1)}), bf16[8,1008,128]{2,1,0:T(8,128)(2,1)S(1)}, u32[]{:S(2)}, u32[]{:S(2)}) async-start(bf16[8,1008,128]{2,1,0:T(8,128)(2,1)} %pack_first.1), calls=%async_computation | async-start | bytes 4128768 | tf_op jit(solution)/shard_map/all_to_all | solution.py:301
  37.7 1.3 copy-start.2
  37.7 9.9 %collective-permute-start = (bf16[8,192,128]{2,1,0:T(8,128)(2,1)S(1)}, bf16[8,192,128]{2,1,0:T(8,128)(2,1)S(1)}, u32[]{:S(2)}, u32[]{:S(2)}) collective-permute-start(bf16[8,192,128]{2,1,0:T(8,128)(2,1)S(1)} %slice.9), channel_id=1, source_target_pairs={{0,1},{1,0},{2,3},{3,2},{4,5},{5,4},{6,7},{7,6},{8,9},{9,8},{10,11... | collective-permute-start | bytes 1179656 | tf_op jit(solution)/shard_map/ppermute | solution.py:304
  39.0 32.3 %all-to-all-start.1 = ((bf16[8,960,128]{2,1,0:T(8,128)(2,1)}), bf16[8,960,128]{2,1,0:T(8,128)(2,1)}, u32[]{:S(2)}, u32[]{:S(2)}) async-start(bf16[8,960,128]{2,1,0:T(8,128)(2,1)} %get-tuple-element.35), calls=%async_computation.1 | async-start | bytes 3932160 | tf_op jit(solution)/shard_map/all_to_all | solution.py:301
  47.7 0.7 copy-start.7
  72.3 10.1 %collective-permute-start.3 = (bf16[8,192,128]{2,1,0:T(8,128)(2,1)S(1)}, bf16[8,192,128]{2,1,0:T(8,128)(2,1)S(1)}, u32[]{:S(2)}, u32[]{:S(2)}) collective-permute-start(bf16[8,192,128]{2,1,0:T(8,128)(2,1)S(1)} %slice.10), channel_id=1, source_target_pairs={{0,1},{1,0},{2,3},{3,2},{4,5},{5,4},{6,7},{7,6},{8,9},{9,8},{10,11... | collective-permute-start | bytes 1179656 | tf_op jit(solution)/shard_map/ppermute | solution.py:304
  72.5 47.9 %collective-permute-start.1 = (bf16[8,384,128]{2,1,0:T(8,128)(2,1)}, bf16[8,384,128]{2,1,0:T(8,128)(2,1)}, u32[]{:S(2)}, u32[]{:S(2)}) collective-permute-start(bf16[8,384,128]{2,1,0:T(8,128)(2,1)} %get-tuple-element.32), channel_id=1, source_target_pairs={{16,0},{17,1},{18,2},{19,3},{20,4},{21,5},{22,6},{23,7},{24,8},{25... | collective-permute-start | bytes 2359304 | tf_op jit(solution)/shard_map/ppermute | solution.py:312
  75.1 30.4 %collective-permute-start.2 = (bf16[8,192,128]{2,1,0:T(8,128)(2,1)}, bf16[8,192,128]{2,1,0:T(8,128)(2,1)S(1)}, u32[]{:S(2)}, u32[]{:S(2)}) collective-permute-start(bf16[8,192,128]{2,1,0:T(8,128)(2,1)} %get-tuple-element.34), channel_id=1, source_target_pairs={{0,1},{1,0},{2,3},{3,2},{4,5},{5,4},{6,7},{7,6},{8,9},{9,8},{10,11... | collective-permute-start | bytes 1179656 | tf_op jit(solution)/shard_map/ppermute | solution.py:304
  75.4 42.9 %all-to-all-start.2 = ((bf16[8,960,128]{2,1,0:T(8,128)(2,1)}), bf16[8,960,128]{2,1,0:T(8,128)(2,1)S(1)}, u32[]{:S(2)}, u32[]{:S(2)}) async-start(bf16[8,960,128]{2,1,0:T(8,128)(2,1)} %get-tuple-element.40), calls=%async_computation.2 | async-start | bytes 3932160 | tf_op jit(solution)/shard_map/all_to_all | solution.py:301
  82.5 0.7 copy-start.6
  83.2 22.3 %copy-start.5 = (f32[8,192,128]{2,1,0:T(8,128)S(1)}, f32[8,192,128]{2,1,0:T(8,128)}, u32[]{:S(2)}) copy-start(f32[8,192,128]{2,1,0:T(8,128)} %get-tuple-element.33) | copy-start | bytes 2359300
  105.4 13.1 %collective-permute-start.4 = (bf16[8,192,128]{2,1,0:T(8,128)(2,1)}, bf16[8,192,128]{2,1,0:T(8,128)(2,1)}, u32[]{:S(2)}, u32[]{:S(2)}) collective-permute-start(bf16[8,192,128]{2,1,0:T(8,128)(2,1)} %get-tuple-element.38), channel_id=1, source_target_pairs={{0,1},{1,0},{2,3},{3,2},{4,5},{5,4},{6,7},{7,6},{8,9},{9,8},{10,11... | collective-permute-start | bytes 1179656 | tf_op jit(solution)/shard_map/ppermute | solution.py:304
  105.6 44.4 %collective-permute-start.8 = (bf16[4,384,128]{2,1,0:T(8,128)(2,1)}, bf16[4,384,128]{2,1,0:T(8,128)(2,1)S(1)}, u32[]{:S(2)}, u32[]{:S(2)}) collective-permute-start(bf16[4,384,128]{2,1,0:T(8,128)(2,1)} %get-tuple-element.52), channel_id=1, source_target_pairs={{16,8},{17,9},{18,10},{19,11},{20,12},{21,13},{22,14},{23,15},{24,... | collective-permute-start | bytes 1179656 | tf_op jit(solution)/shard_map/ppermute | solution.py:312
  107.5 42.5 %collective-permute-start.7 = (bf16[4,384,128]{2,1,0:T(8,128)(2,1)}, bf16[4,384,128]{2,1,0:T(8,128)(2,1)S(1)}, u32[]{:S(2)}, u32[]{:S(2)}) collective-permute-start(bf16[4,384,128]{2,1,0:T(8,128)(2,1)} %get-tuple-element.41), channel_id=1, source_target_pairs={{16,0},{17,1},{18,2},{19,3},{20,4},{21,5},{22,6},{23,7},{24,8},{25... | collective-permute-start | bytes 1179656 | tf_op jit(solution)/shard_map/ppermute | solution.py:312
  118.3 4.4 %copy-start.3 = (bf16[8,960,128]{2,1,0:T(8,128)(2,1)}, bf16[8,960,128]{2,1,0:T(8,128)(2,1)S(1)}, u32[]{:S(2)}) copy-start(bf16[8,960,128]{2,1,0:T(8,128)(2,1)S(1)} %all-to-all-done.2.q_ref.d_ref.own_ref) | copy-start | bytes 5898244
  118.3 9.5 %collective-permute-start.5 = (bf16[8,192,128]{2,1,0:T(8,128)(2,1)S(1)}, bf16[8,192,128]{2,1,0:T(8,128)(2,1)}, u32[]{:S(2)}, u32[]{:S(2)}) collective-permute-start(bf16[8,192,128]{2,1,0:T(8,128)(2,1)S(1)} %slice.11), channel_id=1, source_target_pairs={{0,1},{1,0},{2,3},{3,2},{4,5},{5,4},{6,7},{7,6},{8,9},{9,8},{10,11... | collective-permute-start | bytes 1179656 | tf_op jit(solution)/shard_map/ppermute | solution.py:304
  122.7 33.1 %all-to-all-start.3 = ((bf16[8,768,128]{2,1,0:T(8,128)(2,1)}), bf16[8,768,128]{2,1,0:T(8,128)(2,1)S(1)}, u32[]{:S(2)}, u32[]{:S(2)}) async-start(bf16[8,768,128]{2,1,0:T(8,128)(2,1)} %pad_maximum_fusion), calls=%async_computation.3 | async-start | bytes 3145728 | tf_op jit(solution)/shard_map/all_to_all | solution.py:301
  149.9 4.0 %collective-permute-start.6 = (bf16[8,192,128]{2,1,0:T(8,128)(2,1)}, bf16[8,192,128]{2,1,0:T(8,128)(2,1)S(1)}, u32[]{:S(2)}, u32[]{:S(2)}) collective-permute-start(bf16[8,192,128]{2,1,0:T(8,128)(2,1)} %get-tuple-element.48), channel_id=1, source_target_pairs={{0,1},{1,0},{2,3},{3,2},{4,5},{5,4},{6,7},{7,6},{8,9},{9,8},{10,11... | collective-permute-start | bytes 1179656 | tf_op jit(solution)/shard_map/ppermute | solution.py:304
  150.0 21.5 %collective-permute-start.9 = (bf16[4,384,128]{2,1,0:T(8,128)(2,1)}, bf16[4,384,128]{2,1,0:T(8,128)(2,1)S(1)}, u32[]{:S(2)}, u32[]{:S(2)}) collective-permute-start(bf16[4,384,128]{2,1,0:T(8,128)(2,1)} %get-tuple-element.53), channel_id=1, source_target_pairs={{16,0},{17,1},{18,2},{19,3},{20,4},{21,5},{22,6},{23,7},{24,8},{25... | collective-permute-start | bytes 1179656 | tf_op jit(solution)/shard_map/ppermute | solution.py:312
  151.9 21.8 %collective-permute-start.10 = (bf16[4,384,128]{2,1,0:T(8,128)(2,1)}, bf16[4,384,128]{2,1,0:T(8,128)(2,1)S(1)}, u32[]{:S(2)}, u32[]{:S(2)}) collective-permute-start(bf16[4,384,128]{2,1,0:T(8,128)(2,1)} %get-tuple-element.55), channel_id=1, source_target_pairs={{16,8},{17,9},{18,10},{19,11},{20,12},{21,13},{22,14},{23,15},{24,... | collective-permute-start | bytes 1179656 | tf_op jit(solution)/shard_map/ppermute | solution.py:312
  155.9 19.1 %copy-start = (bf16[8,768,128]{2,1,0:T(8,128)(2,1)}, bf16[8,768,128]{2,1,0:T(8,128)(2,1)S(1)}, u32[]{:S(2)}) copy-start(bf16[8,768,128]{2,1,0:T(8,128)(2,1)S(1)} %all-to-all-done.3.refs_0_.refs_1_) | copy-start | bytes 4718596
  155.9 19.1 %all-to-all-start.4 = ((bf16[8,192,128]{2,1,0:T(8,128)(2,1)}), bf16[8,192,128]{2,1,0:T(8,128)(2,1)S(1)}, u32[]{:S(2)}, u32[]{:S(2)}) async-start(bf16[8,192,128]{2,1,0:T(8,128)(2,1)} %add_convert_fusion), calls=%async_computation.4 | async-start | bytes 786432 | tf_op jit(solution)/shard_map/all_to_all | solution.py:301
  174.9 5.4 %copy-start.4 = (bf16[8,192,128]{2,1,0:T(8,128)(2,1)}, bf16[8,192,128]{2,1,0:T(8,128)(2,1)S(1)}, u32[]{:S(2)}) copy-start(bf16[8,192,128]{2,1,0:T(8,128)(2,1)S(1)} %all-to-all-done.4.refs_2_) | copy-start | bytes 1179652
  174.9 25.6 %all-to-all-start.5 = ((bf16[4,1536,128]{2,1,0:T(8,128)(2,1)}), bf16[4,1536,128]{2,1,0:T(8,128)(2,1)S(1)}, u32[]{:S(2)}, u32[]{:S(2)}) async-start(bf16[4,1536,128]{2,1,0:T(8,128)(2,1)} %pad_maximum_fusion.1), calls=%async_computation.5 | async-start | bytes 3145728 | tf_op jit(solution)/shard_map/all_to_all | solution.py:301
  200.6 1.1 copy-start.1

commit v4 on v3

--- a/solution.py
+++ b/solution.py
@@ -25,7 +25,7 @@
 WIDTH = PAIR * TOK
 KV_AT = 2 * TOK
 BIAS_AT = KV_AT + 2 * POOL
-BIAS_ROWS = KTILES * (TOK // HD)
+BIAS_ROWS = KTILES
 NN = (((1,), (0,)), ((), ()))
 NT = (((1,), (1,)), ((), ()))
 TN = (((0,), (0,)), ((), ()))
@@ -55,14 +55,12 @@
     @pl.when(pl.program_id(0) == 0)
     def _():
         pool[...] = pool_matrix((POOL, TOK), 1)
-        for block in range(TOK // HD):
-            token = lax.broadcasted_iota(jnp.int32, (1, HD), 1) + block * HD
-            for at in range(KTILES):
-                tile = at % CHIPS * CORES + (at // CHIPS + core_ref[0]) % CORES
-                upper = jnp.where(mask_ref[0, tile] > 0, 0.0, BLOCKED)
-                lower = jnp.where(mask_ref[1, tile] > 0, 0.0, BLOCKED)
-                row = block * KTILES + at
-                bias[row : row + 1] = jnp.where(token < ROW, upper, lower)
+        first = lax.broadcasted_iota(jnp.int32, (1, HD), 1) < HD // 2
+        for at in range(KTILES):
+            tile = at % CHIPS * CORES + (at // CHIPS + core_ref[0]) % CORES
+            upper = jnp.where(mask_ref[0, tile] > 0, 0.0, BLOCKED)
+            lower = jnp.where(mask_ref[1, tile] > 0, 0.0, BLOCKED)
+            bias[at : at + 1] = jnp.where(first, upper, lower)
 
     for chip in range(PAIR):
         pack_head(pool[...], out_ref.at[chip : chip + 1], *[r[0] for r in rest[4 * chip : 4 * chip + 4]])
@@ -130,11 +128,11 @@
 
     q = q_ref[...].reshape(WIDTH, HD)
     d = d_ref[...].reshape(WIDTH, HD)
-    blocks = [
-        bias_ref[owner, at : at + KTILES].astype(jnp.float32)
-        for owner in range(PAIR)
-        for at in range(0, BIAS_ROWS, KTILES)
-    ]
+    upper = lax.broadcasted_iota(jnp.int32, (KTILES, TOK), 1) < ROW
+    blocks = []
+    for owner in range(PAIR):
+        rows = bias_ref[owner].astype(jnp.float32)
+        blocks.append(jnp.where(upper, rows[:, :1], rows[:, HD - 1 :]))
     bias = jnp.concatenate(blocks, axis=1)
     part = 4 * POOL
     top = jnp.full((8, WIDTH), -3e38, jnp.float32)
@@ -217,7 +215,7 @@
             ],
         ),
         out_shape=[jax.ShapeDtypeStruct((PAIR * each, TOK, HD), jnp.bfloat16)] * parts
-        + [jax.ShapeDtypeStruct((CHIPS, 2 * POOL, HD), t) for t in (jnp.float32, jnp.bfloat16)],
+        + [jax.ShapeDtypeStruct((CHIPS, 2 * POOL, HD), t) for t in (jnp.bfloat16, jnp.bfloat16)],
         compiler_params=pltpu.CompilerParams(vmem_limit_bytes=60 * 2**20),
         cost_estimate=pl.CostEstimate(
             flops=40 * CHIPS * TOK * KEYS * HD,
@@ -255,6 +253,7 @@
         out_specs=[column, column],
         out_shape=[whole, whole],
         scratch_shapes=[pltpu.VMEM((TOK, POOL), jnp.bfloat16)],
+        compiler_params=pltpu.CompilerParams(vmem_limit_bytes=60 * 2**20),
         name="unpool",
     )(*[piece for piece, _ in pieces])
 
@@ -281,6 +280,7 @@
             out_specs=pl.BlockSpec((1, TOK, PAIR * WIDE), lambda s, side: (0, 0, s)),
         ),
         out_shape=jax.ShapeDtypeStruct((1, TOK, CHIPS * WIDE), jnp.bfloat16),
+        compiler_params=pltpu.CompilerParams(vmem_limit_bytes=60 * 2**20),
         name="place",
     )(side, by_chip, by_line, by_line)
 
@@ -315,7 +315,7 @@
         return swap(data[:, KV_AT:BIAS_AT])
 
     def summed(own, foreign):
-        return (own + foreign.astype(jnp.float32)).astype(jnp.bfloat16)
+        return (own.astype(jnp.float32) + foreign.astype(jnp.float32)).astype(jnp.bfloat16)
 
     arrays = (query, out_grad, key, value)
     sent = [pack_first(core.reshape(1), tile_mask, arrays), *pack_rest(arrays)]

time: 208 us -> 207 us (level)
  transfers between devices with their start and end apart: 17 -> 17, of which waited for: 6 -> 6; matrix products, arithmetic and copies ran while one was open for 4% -> 4% of each run, Pallas kernels for 38% -> 39%
where the time goes in v4:
time: 207 us; the launch traced here: 204 us
  Pallas kernels  87.3 us (42%)
  waiting for transfers between devices  52.4 us (25%)
  starting transfers between devices  51.8 us (25%)
  other arithmetic  6.79 us (3%)
  local copies, waits for them, and re-layouts  4.96 us (2%)
    pallas_call x3, Pallas kernels, attend(): pl.pallas_call(attend_kernel, grid_spec=pltpu.PrefetchScalarGridSpec(num_...  65.5 us
    all_to_all x6, waiting for transfers between devices, trade(): lax.all_to_all(data, 'ctx', 0, 0, axis_index_groups=among, tiled=True)  42.2 us
    all_to_all x6, starting transfers between devices, trade(): lax.all_to_all(data, 'ctx', 0, 0, axis_index_groups=among, tiled=True)  40.4 us
    ppermute x5, starting transfers between devices, to_previous(): return lax.ppermute(data, ('section', 'ctx'), pairs)  10.8 us
    ppermute x5, waiting for transfers between devices, to_previous(): return lax.ppermute(data, ('section', 'ctx'), pairs)  10.2 us
    pallas_call x1, Pallas kernels, pack_rest(): pl.pallas_call(pack_rest_kernel, grid=(CHIPS,), in_specs=[pl.BlockSpec((1...  8.22 us
    pallas_call x1, Pallas kernels, unpool(): pl.pallas_call(unpool_kernel, grid=(CHIPS // PAIR,), in_specs=[pl.BlockSp...  4.98 us
    pallas_call x1, Pallas kernels, pack_first(): pl.pallas_call(pack_first_kernel, grid=(CHIPS // PAIR,), in_specs=[scalar...  4.61 us
  transfers between devices with their start and end apart: 17, of which 6 were waited for; matrix products, arithmetic and copies ran while one was open for 4% of the time, Pallas kernels for 39%

profile of v4, /device:TPU:56, one launch (start us, length us, event | category | flops | bytes accessed | tf_op | source)
XLA Modules:
  0.0 204.1 jit_solution(2311737963780927148)
XLA Ops:
  0.6 4.6 %pack_first.1 = bf16[8,976,128]{2,1,0:T(8,128)(2,1)} custom-call(s32[1]{0:T(128)} %bitcast.core_ref, s32[2,16]{1,0:T(2,128)} %mask_ref.1, bf16[1,384,3072]{2,1,0:T(8,128)(2,1)} %q_ref.1, bf16[1,384,3072]{2,1,0:T(8,128)(2,1)} %d_ref.1, bf16[1,384,3072]{2,1,0:T(8,128)(2,1)} %k_ref.1, bf16[1,384,3072]{2,1,0:T(8,128)(2,1)} %v_ref.1, ...), custom_call_target="tpu_custom_call" | custom-call | tf_op jit(solution)/shard_map/pack_first/pallas_call | solution.py:73
  5.2 7.3 %all-to-all-start = ((bf16[8,976,128]{2,1,0:T(8,128)(2,1)}), bf16[8,976,128]{2,1,0:T(8,128)(2,1)S(1)}, u32[]{:S(2)}, u32[]{:S(2)}) async-start(bf16[8,976,128]{2,1,0:T(8,128)(2,1)} %pack_first.1), calls=%async_computation | async-start | bytes 3997696 | tf_op jit(solution)/shard_map/all_to_all | solution.py:301
  12.5 8.2 %pack_rest.1 = (bf16[8,960,128]{2,1,0:T(8,128)(2,1)}, bf16[8,960,128]{2,1,0:T(8,128)(2,1)}) custom-call(bf16[1,384,3072]{2,1,0:T(8,128)(2,1)} %q_ref.1, bf16[1,384,3072]{2,1,0:T(8,128)(2,1)} %d_ref.1, bf16[1,384,3072]{2,1,0:T(8,128)(2,1)} %k_ref.1, bf16[1,384,3072]{2,1,0:T(8,128)(2,1)} %v_ref.1), custom_call_target="tpu_custom_call" | custom-call | tf_op jit(solution)/shard_map/pack_rest/pallas_call | solution.py:103
  20.7 16.2 %all-to-all-done.q_ref.d_ref.own_ref.bias_ref = bf16[8,976,128]{2,1,0:T(8,128)(2,1)S(1)} async-done(((bf16[8,976,128]{2,1,0:T(8,128)(2,1)}), bf16[8,976,128]{2,1,0:T(8,128)(2,1)S(1)}, u32[]{:S(2)}, u32[]{:S(2)}) %all-to-all-start) | async-done | bytes 1998880 | tf_op jit(solution)/shard_map/all_to_all | solution.py:301
  36.9 0.0 copy-start.2
  37.0 0.1 collective-permute-start
  37.1 1.2 copy-done.2
  38.2 8.2 %all-to-all-start.1 = ((bf16[8,960,128]{2,1,0:T(8,128)(2,1)}), bf16[8,960,128]{2,1,0:T(8,128)(2,1)}, u32[]{:S(2)}, u32[]{:S(2)}) async-start(bf16[8,960,128]{2,1,0:T(8,128)(2,1)} %get-tuple-element.35), calls=%async_computation.1 | async-start | bytes 3932160 | tf_op jit(solution)/shard_map/all_to_all | solution.py:301
  46.4 0.0 collective-permute-done.other_ref
  46.4 0.0 copy-start.7
  46.4 0.7 copy-done.7
  47.2 21.6 %attend.3 = (bf16[8,384,128]{2,1,0:T(8,128)(2,1)}, bf16[8,192,128]{2,1,0:T(8,128)(2,1)}, bf16[8,192,128]{2,1,0:T(8,128)(2,1)}) custom-call(s32[1]{0:T(128)} %constant.25.clone.1.side_ref, bf16[8,976,128]{2,1,0:T(8,128)(2,1)} %copy-done.2, bf16[8,976,128]{2,1,0:T(8,128)(2,1)} %copy-done.2, bf16[8,976,128]{2,1,0:T(8,128)(2,1)} %copy-done.2, ...), custom_call_target="tpu_custom_call" | custom-call | flops 24159191040 | bytes 6291456 | tf_op jit(solution)/shard_map/attend/pallas_call | solution.py:191
  68.8 1.3 all-to-all-done.1.q_ref.d_ref.own_ref
  70.1 1.0 slice.10
  71.1 0.1 collective-permute-start.3
  71.2 2.7 %collective-permute-start.1 = (bf16[8,384,128]{2,1,0:T(8,128)(2,1)}, bf16[8,384,128]{2,1,0:T(8,128)(2,1)S(1)}, u32[]{:S(2)}, u32[]{:S(2)}) collective-permute-start(bf16[8,384,128]{2,1,0:T(8,128)(2,1)} %get-tuple-element.32), channel_id=1, source_target_pairs={{16,0},{17,1},{18,2},{19,3},{20,4},{21,5},{22,6},{23,7},{24,8},{25... | collective-permute-start | bytes 2359304 | tf_op jit(solution)/shard_map/ppermute | solution.py:312
  73.9 0.3 collective-permute-start.2
  74.2 7.1 %all-to-all-start.2 = ((bf16[8,960,128]{2,1,0:T(8,128)(2,1)}), bf16[8,960,128]{2,1,0:T(8,128)(2,1)S(1)}, u32[]{:S(2)}, u32[]{:S(2)}) async-start(bf16[8,960,128]{2,1,0:T(8,128)(2,1)} %get-tuple-element.40), calls=%async_computation.2 | async-start | bytes 3932160 | tf_op jit(solution)/shard_map/all_to_all | solution.py:301
  81.3 0.0 collective-permute-done.3.other_ref
  81.3 0.0 copy-start.6
  81.3 22.0 %attend.4 = (bf16[4,384,128]{2,1,0:T(8,128)(2,1)}, bf16[4,384,128]{2,1,0:T(8,128)(2,1)}, bf16[8,192,128]{2,1,0:T(8,128)(2,1)}, bf16[8,192,128]{2,1,0:T(8,128)(2,1)}) custom-call(s32[1]{0:T(128)} %bitcast.1.side_ref, bf16[8,960,128]{2,1,0:T(8,128)(2,1)} %all-to-all-done.1.q_ref.d_ref.own_ref, bf16[8,960,128]{2,1,0:T(8,128)(2,1)} %all-to-all-done.1.q_ref.d_ref.own_ref, ...), custom_call_target="tpu_custom_call" | custom-call | flops 24159191040 | bytes 6291456 | tf_op jit(solution)/shard_map/attend/pallas_call | solution.py:191
  103.2 0.1 collective-permute-start.4
  103.3 0.0 collective-permute-done.2
  103.4 0.0 copy-done.6
  103.4 0.1 add_convert_fusion.2
  103.5 1.9 collective-permute-start.8
  105.4 2.0 collective-permute-start.7
  107.4 9.7 %all-to-all-done.2.q_ref.d_ref.own_ref = bf16[8,960,128]{2,1,0:T(8,128)(2,1)S(1)} async-done(((bf16[8,960,128]{2,1,0:T(8,128)(2,1)}), bf16[8,960,128]{2,1,0:T(8,128)(2,1)S(1)}, u32[]{:S(2)}, u32[]{:S(2)}) %all-to-all-start.2) | async-done | bytes 1966112 | tf_op jit(solution)/shard_map/all_to_all | solution.py:301
  117.1 0.0 copy-start.3
  117.1 0.8 slice.11
  117.9 0.0 collective-permute-start.5
  117.9 0.0 collective-permute-done.4
  117.9 1.2 add_convert_fusion.1
  119.2 0.0 collective-permute-done.1
  119.2 1.2 pad_maximum_fusion
  120.4 0.0 copy-done.3
  120.4 5.1 %all-to-all-start.3 = ((bf16[8,768,128]{2,1,0:T(8,128)(2,1)}), bf16[8,768,128]{2,1,0:T(8,128)(2,1)S(1)}, u32[]{:S(2)}, u32[]{:S(2)}) async-start(bf16[8,768,128]{2,1,0:T(8,128)(2,1)} %pad_maximum_fusion), calls=%async_computation.3 | async-start | bytes 3145728 | tf_op jit(solution)/shard_map/all_to_all | solution.py:301
  125.5 0.0 collective-permute-done.5.other_ref
  125.5 21.9 %attend.5 = (bf16[4,384,128]{2,1,0:T(8,128)(2,1)}, bf16[4,384,128]{2,1,0:T(8,128)(2,1)}, bf16[8,192,128]{2,1,0:T(8,128)(2,1)}, bf16[8,192,128]{2,1,0:T(8,128)(2,1)}) custom-call(s32[1]{0:T(128)} %bitcast.1.side_ref, bf16[8,960,128]{2,1,0:T(8,128)(2,1)} %copy-done.3, bf16[8,960,128]{2,1,0:T(8,128)(2,1)} %copy-done.3, bf16[8,960,128]{2,1,0:T(8,128)(2,1)} %copy-done.3, ...), custom_call_target="tpu_custom_call" | custom-call | flops 24159191040 | bytes 6291456 | tf_op jit(solution)/shard_map/attend/pallas_call | solution.py:191
  147.4 0.1 collective-permute-start.6
  147.5 0.0 collective-permute-done.8
  147.5 0.0 copy-start.5
  147.5 0.0 collective-permute-done.7
  147.5 2.3 %collective-permute-start.9 = (bf16[4,384,128]{2,1,0:T(8,128)(2,1)}, bf16[4,384,128]{2,1,0:T(8,128)(2,1)S(1)}, u32[]{:S(2)}, u32[]{:S(2)}) collective-permute-start(bf16[4,384,128]{2,1,0:T(8,128)(2,1)} %get-tuple-element.53), channel_id=1, source_target_pairs={{16,0},{17,1},{18,2},{19,3},{20,4},{21,5},{22,6},{23,7},{24,8},{25... | collective-permute-start | bytes 1179656 | tf_op jit(solution)/shard_map/ppermute | solution.py:312
  149.8 1.9 collective-permute-start.10
  151.8 0.0 collective-permute-done.6
  151.8 1.8 add_convert_fusion
  153.6 0.0 all-to-all-done.3.refs_0_.refs_1_
  153.6 0.0 copy-start
  153.6 0.0 copy-done.5
  153.6 7.4 %all-to-all-start.4 = ((bf16[8,192,128]{2,1,0:T(8,128)(2,1)}), bf16[8,192,128]{2,1,0:T(8,128)(2,1)S(1)}, u32[]{:S(2)}, u32[]{:S(2)}) async-start(bf16[8,192,128]{2,1,0:T(8,128)(2,1)} %add_convert_fusion), calls=%async_computation.4 | async-start | bytes 786432 | tf_op jit(solution)/shard_map/all_to_all | solution.py:301
  161.1 7.8 %collective-permute-done.9 = bf16[4,384,128]{2,1,0:T(8,128)(2,1)S(1)} collective-permute-done((bf16[4,384,128]{2,1,0:T(8,128)(2,1)}, bf16[4,384,128]{2,1,0:T(8,128)(2,1)S(1)}, u32[]{:S(2)}, u32[]{:S(2)}) %collective-permute-start.9) | collective-permute-done | bytes 393248 | tf_op jit(solution)/shard_map/ppermute | solution.py:312
  168.9 2.3 %collective-permute-done.10 = bf16[4,384,128]{2,1,0:T(8,128)(2,1)S(1)} collective-permute-done((bf16[4,384,128]{2,1,0:T(8,128)(2,1)}, bf16[4,384,128]{2,1,0:T(8,128)(2,1)S(1)}, u32[]{:S(2)}, u32[]{:S(2)}) %collective-permute-start.10) | collective-permute-done | bytes 393248 | tf_op jit(solution)/shard_map/ppermute | solution.py:312
  171.2 2.4 %pad_maximum_fusion.1 = bf16[4,1536,128]{2,1,0:T(8,128)(2,1)} fusion(bf16[4,384,128]{2,1,0:T(8,128)(2,1)S(1)} %collective-permute-done.10, bf16[4,384,128]{2,1,0:T(8,128)(2,1)S(1)} %collective-permute-done.9, bf16[4,384,128]{2,1,0:T(8,128)(2,1)} %copy-done.5, bf16[4,384,128]{2,1,0:T(8,128)(2,1)} %collective-permute-done.7), kind=kLoop, calls=%fused_computation.1 | loop fusion | flops 6291456 | bytes 3145728 | tf_op jit(solution)/shard_map/concatenate | solution.py:337
  173.6 0.0 all-to-all-done.4.refs_2_
  173.6 0.0 copy-start.4
  173.6 0.0 copy-done
  173.6 5.4 %all-to-all-start.5 = ((bf16[4,1536,128]{2,1,0:T(8,128)(2,1)}), bf16[4,1536,128]{2,1,0:T(8,128)(2,1)S(1)}, u32[]{:S(2)}, u32[]{:S(2)}) async-start(bf16[4,1536,128]{2,1,0:T(8,128)(2,1)} %pad_maximum_fusion.1), calls=%async_computation.5 | async-start | bytes 3145728 | tf_op jit(solution)/shard_map/all_to_all | solution.py:301
  179.0 0.0 copy-done.4
  179.0 5.0 %unpool.1 = (bf16[1,384,3072]{2,1,0:T(8,128)(2,1)}, bf16[1,384,3072]{2,1,0:T(8,128)(2,1)}) custom-call(bf16[8,768,128]{2,1,0:T(8,128)(2,1)} %copy-done, bf16[8,768,128]{2,1,0:T(8,128)(2,1)} %copy-done, bf16[8,192,128]{2,1,0:T(8,128)(2,1)} %copy-done.4), custom_call_target="tpu_custom_call" | custom-call | tf_op jit(solution)/shard_map/unpool/pallas_call | solution.py:247
  184.0 15.0 %all-to-all-done.5.refs_1_.refs_2_ = bf16[4,1536,128]{2,1,0:T(8,128)(2,1)S(1)} async-done(((bf16[4,1536,128]{2,1,0:T(8,128)(2,1)}), bf16[4,1536,128]{2,1,0:T(8,128)(2,1)S(1)}, u32[]{:S(2)}, u32[]{:S(2)}) %all-to-all-start.5) | async-done | bytes 1572896 | tf_op jit(solution)/shard_map/all_to_all | solution.py:301
  198.9 0.0 copy-start.1
  198.9 1.1 copy-done.1
  200.1 4.0 %place.1 = bf16[1,384,3072]{2,1,0:T(8,128)(2,1)} custom-call(s32[1]{0:T(128)} %bitcast.1.side_ref, bf16[8,768,128]{2,1,0:T(8,128)(2,1)} %copy-done, bf16[4,1536,128]{2,1,0:T(8,128)(2,1)} %copy-done.1, bf16[4,1536,128]{2,1,0:T(8,128)(2,1)} %copy-done.1), custom_call_target="tpu_custom_call" | custom-call | tf_op jit(solution)/shard_map/place/pallas_call | solution.py:273
  (1 shorter events, 0.0 us)
Async XLA Ops:
  5.2 31.7 %all-to-all-start = ((bf16[8,976,128]{2,1,0:T(8,128)(2,1)}), bf16[8,976,128]{2,1,0:T(8,128)(2,1)S(1)}, u32[]{:S(2)}, u32[]{:S(2)}) async-start(bf16[8,976,128]{2,1,0:T(8,128)(2,1)} %pack_first.1), calls=%async_computation | async-start | bytes 3997696 | tf_op jit(solution)/shard_map/all_to_all | solution.py:301
  36.9 1.3 copy-start.2
  37.0 9.5 %collective-permute-start = (bf16[8,192,128]{2,1,0:T(8,128)(2,1)S(1)}, bf16[8,192,128]{2,1,0:T(8,128)(2,1)S(1)}, u32[]{:S(2)}, u32[]{:S(2)}) collective-permute-start(bf16[8,192,128]{2,1,0:T(8,128)(2,1)S(1)} %slice.9), channel_id=1, source_target_pairs={{0,1},{1,0},{2,3},{3,2},{4,5},{5,4},{6,7},{7,6},{8,9},{9,8},{10,11... | collective-permute-start | bytes 1179656 | tf_op jit(solution)/shard_map/ppermute | solution.py:304
  38.2 31.9 %all-to-all-start.1 = ((bf16[8,960,128]{2,1,0:T(8,128)(2,1)}), bf16[8,960,128]{2,1,0:T(8,128)(2,1)}, u32[]{:S(2)}, u32[]{:S(2)}) async-start(bf16[8,960,128]{2,1,0:T(8,128)(2,1)} %get-tuple-element.35), calls=%async_computation.1 | async-start | bytes 3932160 | tf_op jit(solution)/shard_map/all_to_all | solution.py:301
  46.4 0.7 copy-start.7
  71.1 10.1 %collective-permute-start.3 = (bf16[8,192,128]{2,1,0:T(8,128)(2,1)S(1)}, bf16[8,192,128]{2,1,0:T(8,128)(2,1)}, u32[]{:S(2)}, u32[]{:S(2)}) collective-permute-start(bf16[8,192,128]{2,1,0:T(8,128)(2,1)S(1)} %slice.10), channel_id=1, source_target_pairs={{0,1},{1,0},{2,3},{3,2},{4,5},{5,4},{6,7},{7,6},{8,9},{9,8},{10,11... | collective-permute-start | bytes 1179656 | tf_op jit(solution)/shard_map/ppermute | solution.py:304
  71.2 47.9 %collective-permute-start.1 = (bf16[8,384,128]{2,1,0:T(8,128)(2,1)}, bf16[8,384,128]{2,1,0:T(8,128)(2,1)S(1)}, u32[]{:S(2)}, u32[]{:S(2)}) collective-permute-start(bf16[8,384,128]{2,1,0:T(8,128)(2,1)} %get-tuple-element.32), channel_id=1, source_target_pairs={{16,0},{17,1},{18,2},{19,3},{20,4},{21,5},{22,6},{23,7},{24,8},{25... | collective-permute-start | bytes 2359304 | tf_op jit(solution)/shard_map/ppermute | solution.py:312
  73.9 29.5 %collective-permute-start.2 = (bf16[8,192,128]{2,1,0:T(8,128)(2,1)}, bf16[8,192,128]{2,1,0:T(8,128)(2,1)S(1)}, u32[]{:S(2)}, u32[]{:S(2)}) collective-permute-start(bf16[8,192,128]{2,1,0:T(8,128)(2,1)} %get-tuple-element.34), channel_id=1, source_target_pairs={{0,1},{1,0},{2,3},{3,2},{4,5},{5,4},{6,7},{7,6},{8,9},{9,8},{10,11... | collective-permute-start | bytes 1179656 | tf_op jit(solution)/shard_map/ppermute | solution.py:304
  74.2 42.9 %all-to-all-start.2 = ((bf16[8,960,128]{2,1,0:T(8,128)(2,1)}), bf16[8,960,128]{2,1,0:T(8,128)(2,1)S(1)}, u32[]{:S(2)}, u32[]{:S(2)}) async-start(bf16[8,960,128]{2,1,0:T(8,128)(2,1)} %get-tuple-element.40), calls=%async_computation.2 | async-start | bytes 3932160 | tf_op jit(solution)/shard_map/all_to_all | solution.py:301
  81.3 22.1 %copy-start.6 = (bf16[8,192,128]{2,1,0:T(8,128)(2,1)S(1)}, bf16[8,192,128]{2,1,0:T(8,128)(2,1)}, u32[]{:S(2)}) copy-start(bf16[8,192,128]{2,1,0:T(8,128)(2,1)} %get-tuple-element.33) | copy-start | bytes 1179652
  103.2 14.7 %collective-permute-start.4 = (bf16[8,192,128]{2,1,0:T(8,128)(2,1)}, bf16[8,192,128]{2,1,0:T(8,128)(2,1)}, u32[]{:S(2)}, u32[]{:S(2)}) collective-permute-start(bf16[8,192,128]{2,1,0:T(8,128)(2,1)} %get-tuple-element.38), channel_id=1, source_target_pairs={{0,1},{1,0},{2,3},{3,2},{4,5},{5,4},{6,7},{7,6},{8,9},{9,8},{10,11... | collective-permute-start | bytes 1179656 | tf_op jit(solution)/shard_map/ppermute | solution.py:304
  103.5 44.0 %collective-permute-start.8 = (bf16[4,384,128]{2,1,0:T(8,128)(2,1)}, bf16[4,384,128]{2,1,0:T(8,128)(2,1)S(1)}, u32[]{:S(2)}, u32[]{:S(2)}) collective-permute-start(bf16[4,384,128]{2,1,0:T(8,128)(2,1)} %get-tuple-element.52), channel_id=1, source_target_pairs={{16,8},{17,9},{18,10},{19,11},{20,12},{21,13},{22,14},{23,15},{24,... | collective-permute-start | bytes 1179656 | tf_op jit(solution)/shard_map/ppermute | solution.py:312
  105.4 42.1 %collective-permute-start.7 = (bf16[4,384,128]{2,1,0:T(8,128)(2,1)}, bf16[4,384,128]{2,1,0:T(8,128)(2,1)}, u32[]{:S(2)}, u32[]{:S(2)}) collective-permute-start(bf16[4,384,128]{2,1,0:T(8,128)(2,1)} %get-tuple-element.41), channel_id=1, source_target_pairs={{16,0},{17,1},{18,2},{19,3},{20,4},{21,5},{22,6},{23,7},{24,8},{25... | collective-permute-start | bytes 1179656 | tf_op jit(solution)/shard_map/ppermute | solution.py:312
  117.1 3.3 %copy-start.3 = (bf16[8,960,128]{2,1,0:T(8,128)(2,1)}, bf16[8,960,128]{2,1,0:T(8,128)(2,1)S(1)}, u32[]{:S(2)}) copy-start(bf16[8,960,128]{2,1,0:T(8,128)(2,1)S(1)} %all-to-all-done.2.q_ref.d_ref.own_ref) | copy-start | bytes 5898244
  117.9 7.6 %collective-permute-start.5 = (bf16[8,192,128]{2,1,0:T(8,128)(2,1)}, bf16[8,192,128]{2,1,0:T(8,128)(2,1)}, u32[]{:S(2)}, u32[]{:S(2)}) collective-permute-start(bf16[8,192,128]{2,1,0:T(8,128)(2,1)} %slice.11), channel_id=1, source_target_pairs={{0,1},{1,0},{2,3},{3,2},{4,5},{5,4},{6,7},{7,6},{8,9},{9,8},{10,11... | collective-permute-start | bytes 1179656 | tf_op jit(solution)/shard_map/ppermute | solution.py:304
  120.4 33.2 %all-to-all-start.3 = ((bf16[8,768,128]{2,1,0:T(8,128)(2,1)}), bf16[8,768,128]{2,1,0:T(8,128)(2,1)S(1)}, u32[]{:S(2)}, u32[]{:S(2)}) async-start(bf16[8,768,128]{2,1,0:T(8,128)(2,1)} %pad_maximum_fusion), calls=%async_computation.3 | async-start | bytes 3145728 | tf_op jit(solution)/shard_map/all_to_all | solution.py:301
  147.4 4.4 %collective-permute-start.6 = (bf16[8,192,128]{2,1,0:T(8,128)(2,1)}, bf16[8,192,128]{2,1,0:T(8,128)(2,1)S(1)}, u32[]{:S(2)}, u32[]{:S(2)}) collective-permute-start(bf16[8,192,128]{2,1,0:T(8,128)(2,1)} %get-tuple-element.48), channel_id=1, source_target_pairs={{0,1},{1,0},{2,3},{3,2},{4,5},{5,4},{6,7},{7,6},{8,9},{9,8},{10,11... | collective-permute-start | bytes 1179656 | tf_op jit(solution)/shard_map/ppermute | solution.py:304
  147.5 6.1 %copy-start.5 = (bf16[4,384,128]{2,1,0:T(8,128)(2,1)}, bf16[4,384,128]{2,1,0:T(8,128)(2,1)S(1)}, u32[]{:S(2)}) copy-start(bf16[4,384,128]{2,1,0:T(8,128)(2,1)S(1)} %collective-permute-done.8) | copy-start | bytes 1179652
  147.5 21.4 %collective-permute-start.9 = (bf16[4,384,128]{2,1,0:T(8,128)(2,1)}, bf16[4,384,128]{2,1,0:T(8,128)(2,1)S(1)}, u32[]{:S(2)}, u32[]{:S(2)}) collective-permute-start(bf16[4,384,128]{2,1,0:T(8,128)(2,1)} %get-tuple-element.53), channel_id=1, source_target_pairs={{16,0},{17,1},{18,2},{19,3},{20,4},{21,5},{22,6},{23,7},{24,8},{25... | collective-permute-start | bytes 1179656 | tf_op jit(solution)/shard_map/ppermute | solution.py:312
  149.8 21.4 %collective-permute-start.10 = (bf16[4,384,128]{2,1,0:T(8,128)(2,1)}, bf16[4,384,128]{2,1,0:T(8,128)(2,1)S(1)}, u32[]{:S(2)}, u32[]{:S(2)}) collective-permute-start(bf16[4,384,128]{2,1,0:T(8,128)(2,1)} %get-tuple-element.55), channel_id=1, source_target_pairs={{16,8},{17,9},{18,10},{19,11},{20,12},{21,13},{22,14},{23,15},{24,... | collective-permute-start | bytes 1179656 | tf_op jit(solution)/shard_map/ppermute | solution.py:312
  153.6 20.0 %copy-start = (bf16[8,768,128]{2,1,0:T(8,128)(2,1)}, bf16[8,768,128]{2,1,0:T(8,128)(2,1)S(1)}, u32[]{:S(2)}) copy-start(bf16[8,768,128]{2,1,0:T(8,128)(2,1)S(1)} %all-to-all-done.3.refs_0_.refs_1_) | copy-start | bytes 4718596
  153.6 20.0 %all-to-all-start.4 = ((bf16[8,192,128]{2,1,0:T(8,128)(2,1)}), bf16[8,192,128]{2,1,0:T(8,128)(2,1)S(1)}, u32[]{:S(2)}, u32[]{:S(2)}) async-start(bf16[8,192,128]{2,1,0:T(8,128)(2,1)} %add_convert_fusion), calls=%async_computation.4 | async-start | bytes 786432 | tf_op jit(solution)/shard_map/all_to_all | solution.py:301
  173.6 5.4 %copy-start.4 = (bf16[8,192,128]{2,1,0:T(8,128)(2,1)}, bf16[8,192,128]{2,1,0:T(8,128)(2,1)S(1)}, u32[]{:S(2)}) copy-start(bf16[8,192,128]{2,1,0:T(8,128)(2,1)S(1)} %all-to-all-done.4.refs_2_) | copy-start | bytes 1179652
  173.6 25.3 %all-to-all-start.5 = ((bf16[4,1536,128]{2,1,0:T(8,128)(2,1)}), bf16[4,1536,128]{2,1,0:T(8,128)(2,1)S(1)}, u32[]{:S(2)}, u32[]{:S(2)}) async-start(bf16[4,1536,128]{2,1,0:T(8,128)(2,1)} %pad_maximum_fusion.1), calls=%async_computation.5 | async-start | bytes 3145728 | tf_op jit(solution)/shard_map/all_to_all | solution.py:301
  198.9 1.1 copy-start.1

commit v5 on v4

--- a/solution.py
+++ b/solution.py
@@ -323,20 +323,23 @@
 
     side = side.reshape(1)
     dq, own, foreign = attend(jnp.zeros((1,), jnp.int32), first, first, kv_of(first), 1)
-    moved, terms = [to_previous(dq)], [(own, swap(foreign))]
+    terms = [(own, swap(foreign))]
     data = after(trade(after(sent[1], first)), dq)
-    near, far, own, foreign = attend(side, data, first, kv_of(data), 2)
+    other = kv_of(data)
+    moved = [to_previous(after(dq, other))]
+    near, far, own, foreign = attend(side, data, first, other, 2)
     moved += [to_previous(near), to_previous(far, 1)]
     terms.append((own, swap(foreign)))
     data = after(trade(after(sent[2], data)), near)
-    joined = jnp.concatenate([moved[0], summed(*terms[0]), summed(*terms[1])], axis=1)
+    joined = jnp.concatenate([summed(*terms[0]), summed(*terms[1])], axis=1)
     near, far, own, foreign = attend(side, after(data, joined), first, kv_of(data), 2)
+    foreign = after(foreign, *moved)
     early = after(trade(after(joined, data)), near)
-    moved += [to_previous(after(near, *moved[1:])), to_previous(after(far, *moved[1:]), 1)]
-    middle = trade(after(summed(own, swap(foreign)), early))
+    moved += [to_previous(after(near, *moved)), to_previous(after(far, *moved), 1)]
+    middle = trade(after(jnp.concatenate([moved[0], summed(own, swap(foreign))], axis=1), early))
     late = trade(after(jnp.concatenate(moved[1:], axis=1), middle), lines)
-    key_grad, value_grad = unpool([(early, TOK), (early, TOK + 2 * POOL), (middle, 0)])
-    upstream = place(side, early, late)
+    key_grad, value_grad = unpool([(early, 0), (early, 2 * POOL), (middle, TOK)])
+    upstream = place(side, middle, late)
     return key_grad, value_grad, upstream
 
 

time: 207 us -> 224 us (1.082)
  waiting for transfers between devices: 52.4 us -> 66.1 us
  starting transfers between devices: 51.8 us -> 57.5 us
    ppermute x5, waiting for transfers between devices: 10.2 us -> 29 us  [to_previous(): return lax.ppermute(data, ('section', 'ctx'), pairs)]
    all_to_all x6, waiting for transfers between devices: 42.2 us -> 35.2 us  [trade(): lax.all_to_all(data, 'ctx', 0, 0, axis_index_groups=among, tiled=True)]
    all_to_all x6, starting transfers between devices: 40.4 us -> 43.3 us  [trade(): lax.all_to_all(data, 'ctx', 0, 0, axis_index_groups=among, tiled=True)]
    ppermute x5, starting transfers between devices: 10.8 us -> 13.5 us  [to_previous(): return lax.ppermute(data, ('section', 'ctx'), pairs)]
  transfers between devices with their start and end apart: 17 -> 17, of which waited for: 6 -> 8; matrix products, arithmetic and copies ran while one was open for 4% -> 2% of each run, Pallas kernels for 39% -> 35%
where the time goes in v5:
time: 224 us; the launch traced here: 223 us
  Pallas kernels  87.3 us (39%)
  waiting for transfers between devices  66.1 us (30%)
  starting transfers between devices  57.5 us (26%)
  local copies, waits for them, and re-layouts  5.68 us (3%)
  other arithmetic  5.58 us (2%)
    pallas_call x3, Pallas kernels, attend(): pl.pallas_call(attend_kernel, grid_spec=pltpu.PrefetchScalarGridSpec(num_...  65.5 us
    all_to_all x6, starting transfers between devices, trade(): lax.all_to_all(data, 'ctx', 0, 0, axis_index_groups=among, tiled=True)  43.3 us
    all_to_all x6, waiting for transfers between devices, trade(): lax.all_to_all(data, 'ctx', 0, 0, axis_index_groups=among, tiled=True)  35.2 us
    ppermute x5, waiting for transfers between devices, to_previous(): return lax.ppermute(data, ('section', 'ctx'), pairs)  29 us
    ppermute x5, starting transfers between devices, to_previous(): return lax.ppermute(data, ('section', 'ctx'), pairs)  13.5 us
    pallas_call x1, Pallas kernels, pack_rest(): pl.pallas_call(pack_rest_kernel, grid=(CHIPS,), in_specs=[pl.BlockSpec((1...  8.22 us
    pallas_call x1, Pallas kernels, unpool(): pl.pallas_call(unpool_kernel, grid=(CHIPS // PAIR,), in_specs=[pl.BlockSp...  4.98 us
    pallas_call x1, Pallas kernels, pack_first(): pl.pallas_call(pack_first_kernel, grid=(CHIPS // PAIR,), in_specs=[scalar...  4.61 us
  transfers between devices with their start and end apart: 17, of which 8 were waited for; matrix products, arithmetic and copies ran while one was open for 2% of the time, Pallas kernels for 35%

profile of v5, /device:TPU:56, one launch (start us, length us, event | category | flops | bytes accessed | tf_op | source)
XLA Modules:
  0.0 223.0 jit_solution(15913391669131498109)
XLA Ops:
  0.6 4.6 %pack_first.1 = bf16[8,976,128]{2,1,0:T(8,128)(2,1)} custom-call(s32[1]{0:T(128)} %bitcast.core_ref, s32[2,16]{1,0:T(2,128)} %mask_ref.1, bf16[1,384,3072]{2,1,0:T(8,128)(2,1)} %q_ref.1, bf16[1,384,3072]{2,1,0:T(8,128)(2,1)} %d_ref.1, bf16[1,384,3072]{2,1,0:T(8,128)(2,1)} %k_ref.1, bf16[1,384,3072]{2,1,0:T(8,128)(2,1)} %v_ref.1, ...), custom_call_target="tpu_custom_call" | custom-call | tf_op jit(solution)/shard_map/pack_first/pallas_call | solution.py:73
  5.2 7.3 %all-to-all-start = ((bf16[8,976,128]{2,1,0:T(8,128)(2,1)}), bf16[8,976,128]{2,1,0:T(8,128)(2,1)S(1)}, u32[]{:S(2)}, u32[]{:S(2)}) async-start(bf16[8,976,128]{2,1,0:T(8,128)(2,1)} %pack_first.1), calls=%async_computation | async-start | bytes 3997696 | tf_op jit(solution)/shard_map/all_to_all | solution.py:301
  12.5 8.2 %pack_rest.1 = (bf16[8,960,128]{2,1,0:T(8,128)(2,1)}, bf16[8,960,128]{2,1,0:T(8,128)(2,1)}) custom-call(bf16[1,384,3072]{2,1,0:T(8,128)(2,1)} %q_ref.1, bf16[1,384,3072]{2,1,0:T(8,128)(2,1)} %d_ref.1, bf16[1,384,3072]{2,1,0:T(8,128)(2,1)} %k_ref.1, bf16[1,384,3072]{2,1,0:T(8,128)(2,1)} %v_ref.1), custom_call_target="tpu_custom_call" | custom-call | tf_op jit(solution)/shard_map/pack_rest/pallas_call | solution.py:103
  20.7 16.2 %all-to-all-done.q_ref.d_ref.own_ref.bias_ref = bf16[8,976,128]{2,1,0:T(8,128)(2,1)S(1)} async-done(((bf16[8,976,128]{2,1,0:T(8,128)(2,1)}), bf16[8,976,128]{2,1,0:T(8,128)(2,1)S(1)}, u32[]{:S(2)}, u32[]{:S(2)}) %all-to-all-start) | async-done | bytes 1998880 | tf_op jit(solution)/shard_map/all_to_all | solution.py:301
  36.9 0.0 copy-start.3
  37.0 0.1 collective-permute-start
  37.1 1.2 copy-done.3
  38.2 8.2 %all-to-all-start.1 = ((bf16[8,960,128]{2,1,0:T(8,128)(2,1)}), bf16[8,960,128]{2,1,0:T(8,128)(2,1)}, u32[]{:S(2)}, u32[]{:S(2)}) async-start(bf16[8,960,128]{2,1,0:T(8,128)(2,1)} %get-tuple-element.36), calls=%async_computation.1 | async-start | bytes 3932160 | tf_op jit(solution)/shard_map/all_to_all | solution.py:301
  46.4 0.0 collective-permute-done.other_ref
  46.4 0.0 copy-start.8
  46.4 0.7 copy-done.8
  47.2 21.6 %attend.3 = (bf16[8,384,128]{2,1,0:T(8,128)(2,1)}, bf16[8,192,128]{2,1,0:T(8,128)(2,1)}, bf16[8,192,128]{2,1,0:T(8,128)(2,1)}) custom-call(s32[1]{0:T(128)} %constant.25.clone.1.side_ref, bf16[8,976,128]{2,1,0:T(8,128)(2,1)} %copy-done.3, bf16[8,976,128]{2,1,0:T(8,128)(2,1)} %copy-done.3, bf16[8,976,128]{2,1,0:T(8,128)(2,1)} %copy-done.3, ...), custom_call_target="tpu_custom_call" | custom-call | flops 24159191040 | bytes 6291456 | tf_op jit(solution)/shard_map/attend/pallas_call | solution.py:191
  68.8 1.3 all-to-all-done.1.q_ref.d_ref.own_ref
  70.1 1.0 slice.10
  71.1 0.1 collective-permute-start.2
  71.2 0.5 collective-permute-start.1
  71.7 6.5 %all-to-all-start.2 = ((bf16[8,960,128]{2,1,0:T(8,128)(2,1)}), bf16[8,960,128]{2,1,0:T(8,128)(2,1)S(1)}, u32[]{:S(2)}, u32[]{:S(2)}) async-start(bf16[8,960,128]{2,1,0:T(8,128)(2,1)} %get-tuple-element.42), calls=%async_computation.2 | async-start | bytes 3932160 | tf_op jit(solution)/shard_map/all_to_all | solution.py:301
  78.2 0.0 collective-permute-done.2.other_ref
  78.2 0.0 copy-start.7
  78.2 0.7 copy-done.7
  79.0 0.0 copy-start.5
  79.0 21.9 %attend.4 = (bf16[4,384,128]{2,1,0:T(8,128)(2,1)}, bf16[4,384,128]{2,1,0:T(8,128)(2,1)}, bf16[8,192,128]{2,1,0:T(8,128)(2,1)}, bf16[8,192,128]{2,1,0:T(8,128)(2,1)}) custom-call(s32[1]{0:T(128)} %bitcast.1.side_ref, bf16[8,960,128]{2,1,0:T(8,128)(2,1)} %all-to-all-done.1.q_ref.d_ref.own_ref, bf16[8,960,128]{2,1,0:T(8,128)(2,1)} %all-to-all-done.1.q_ref.d_ref.own_ref, ...), custom_call_target="tpu_custom_call" | custom-call | flops 24159191040 | bytes 6291456 | tf_op jit(solution)/shard_map/attend/pallas_call | solution.py:191
  100.9 0.1 collective-permute-start.3
  101.0 1.8 all-to-all-done.2.q_ref.d_ref.own_ref
  102.8 0.0 copy-start.4
  102.8 0.0 copy-start.6
  102.8 0.8 slice.11
  103.6 0.0 collective-permute-start.4
  103.6 0.0 collective-permute-done.1
  103.6 0.0 copy-done.5
  103.6 0.1 add_convert_fusion.2
  103.8 2.7 %collective-permute-start.6 = (bf16[4,384,128]{2,1,0:T(8,128)(2,1)}, bf16[4,384,128]{2,1,0:T(8,128)(2,1)S(1)}, u32[]{:S(2)}, u32[]{:S(2)}) collective-permute-start(bf16[4,384,128]{2,1,0:T(8,128)(2,1)} %get-tuple-element.43), channel_id=1, source_target_pairs={{16,0},{17,1},{18,2},{19,3},{20,4},{21,5},{22,6},{23,7},{24,8},{25... | collective-permute-start | bytes 1179656 | tf_op jit(solution)/shard_map/ppermute | solution.py:312
  106.4 4.3 %collective-permute-start.7 = (bf16[4,384,128]{2,1,0:T(8,128)(2,1)}, bf16[4,384,128]{2,1,0:T(8,128)(2,1)S(1)}, u32[]{:S(2)}, u32[]{:S(2)}) collective-permute-start(bf16[4,384,128]{2,1,0:T(8,128)(2,1)} %get-tuple-element.52), channel_id=1, source_target_pairs={{16,8},{17,9},{18,10},{19,11},{20,12},{21,13},{22,14},{23,15},{24,... | collective-permute-start | bytes 1179656 | tf_op jit(solution)/shard_map/ppermute | solution.py:312
  110.7 2.7 %collective-permute-start.5 = (bf16[8,384,128]{2,1,0:T(8,128)(2,1)}, bf16[8,384,128]{2,1,0:T(8,128)(2,1)S(1)}, u32[]{:S(2)}, u32[]{:S(2)}) collective-permute-start(bf16[8,384,128]{2,1,0:T(8,128)(2,1)} %get-tuple-element.49), channel_id=1, source_target_pairs={{16,0},{17,1},{18,2},{19,3},{20,4},{21,5},{22,6},{23,7},{24,8},{25... | collective-permute-start | bytes 2359304 | tf_op jit(solution)/shard_map/ppermute | solution.py:312
  113.3 0.0 collective-permute-done.3
  113.4 0.0 copy-done.6
  113.4 1.1 add_convert_fusion.1
  114.5 0.9 pad_maximum_fusion.2
  115.4 0.0 copy-done.4
  115.4 8.6 %all-to-all-start.3 = ((bf16[8,384,128]{2,1,0:T(8,128)(2,1)}), bf16[8,384,128]{2,1,0:T(8,128)(2,1)S(1)}, u32[]{:S(2)}, u32[]{:S(2)}) async-start(bf16[8,384,128]{2,1,0:T(8,128)(2,1)} %pad_maximum_fusion.2), calls=%async_computation.3 | async-start | bytes 1572864 | tf_op jit(solution)/shard_map/all_to_all | solution.py:301
  124.0 0.0 collective-permute-done.4.other_ref
  124.0 21.9 %attend.5 = (bf16[4,384,128]{2,1,0:T(8,128)(2,1)}, bf16[4,384,128]{2,1,0:T(8,128)(2,1)}, bf16[8,192,128]{2,1,0:T(8,128)(2,1)}, bf16[8,192,128]{2,1,0:T(8,128)(2,1)}) custom-call(s32[1]{0:T(128)} %bitcast.1.side_ref, bf16[8,960,128]{2,1,0:T(8,128)(2,1)} %copy-done.4, bf16[8,960,128]{2,1,0:T(8,128)(2,1)} %copy-done.4, bf16[8,960,128]{2,1,0:T(8,128)(2,1)} %copy-done.4, ...), custom_call_target="tpu_custom_call" | custom-call | flops 24159191040 | bytes 6291456 | tf_op jit(solution)/shard_map/attend/pallas_call | solution.py:191
  145.9 0.0 collective-permute-done.7
  145.9 0.0 collective-permute-done.6
  145.9 4.0 %collective-permute-done.5 = bf16[8,384,128]{2,1,0:T(8,128)(2,1)S(1)} collective-permute-done((bf16[8,384,128]{2,1,0:T(8,128)(2,1)}, bf16[8,384,128]{2,1,0:T(8,128)(2,1)S(1)}, u32[]{:S(2)}, u32[]{:S(2)}) %collective-permute-start.5) | collective-permute-done | bytes 786464 | tf_op jit(solution)/shard_map/ppermute | solution.py:312
  149.9 0.0 collective-permute-start.8
  149.9 0.0 all-to-all-done.3.refs_0_.refs_1_
  149.9 1.9 collective-permute-done.8
  151.8 1.1 add_convert_fusion
  153.0 1.1 pad_maximum_fusion.1
  154.0 0.0 copy-done.2
  154.0 7.1 %all-to-all-start.4 = ((bf16[8,576,128]{2,1,0:T(8,128)(2,1)}), bf16[8,576,128]{2,1,0:T(8,128)(2,1)S(1)}, u32[]{:S(2)}, u32[]{:S(2)}) async-start(bf16[8,576,128]{2,1,0:T(8,128)(2,1)} %pad_maximum_fusion.1), calls=%async_computation.4 | async-start | bytes 2359296 | tf_op jit(solution)/shard_map/all_to_all | solution.py:301
  161.2 1.9 collective-permute-start.9
  163.1 2.0 collective-permute-start.10
  165.1 24.7 %collective-permute-done.9 = bf16[4,384,128]{2,1,0:T(8,128)(2,1)S(1)} collective-permute-done((bf16[4,384,128]{2,1,0:T(8,128)(2,1)}, bf16[4,384,128]{2,1,0:T(8,128)(2,1)S(1)}, u32[]{:S(2)}, u32[]{:S(2)}) %collective-permute-start.9) | collective-permute-done | bytes 393248 | tf_op jit(solution)/shard_map/ppermute | solution.py:312
  189.9 0.3 collective-permute-done.10
  190.1 1.2 pad_maximum_fusion
  191.4 0.0 all-to-all-done.4.refs_2_.refs_0_
  191.4 5.6 %all-to-all-start.5 = ((bf16[4,1536,128]{2,1,0:T(8,128)(2,1)}), bf16[4,1536,128]{2,1,0:T(8,128)(2,1)S(1)}, u32[]{:S(2)}, u32[]{:S(2)}) async-start(bf16[4,1536,128]{2,1,0:T(8,128)(2,1)} %pad_maximum_fusion), calls=%async_computation.5 | async-start | bytes 3145728 | tf_op jit(solution)/shard_map/all_to_all | solution.py:301
  197.0 0.0 copy-done.1
  197.0 5.0 %unpool.1 = (bf16[1,384,3072]{2,1,0:T(8,128)(2,1)}, bf16[1,384,3072]{2,1,0:T(8,128)(2,1)}) custom-call(bf16[8,384,128]{2,1,0:T(8,128)(2,1)} %copy-done.2, bf16[8,384,128]{2,1,0:T(8,128)(2,1)} %copy-done.2, bf16[8,576,128]{2,1,0:T(8,128)(2,1)} %copy-done.1), custom_call_target="tpu_custom_call" | custom-call | tf_op jit(solution)/shard_map/unpool/pallas_call | solution.py:247
  201.9 15.9 %all-to-all-done.5.refs_1_.refs_2_ = bf16[4,1536,128]{2,1,0:T(8,128)(2,1)S(1)} async-done(((bf16[4,1536,128]{2,1,0:T(8,128)(2,1)}), bf16[4,1536,128]{2,1,0:T(8,128)(2,1)S(1)}, u32[]{:S(2)}, u32[]{:S(2)}) %all-to-all-start.5) | async-done | bytes 1572896 | tf_op jit(solution)/shard_map/all_to_all | solution.py:301
  217.8 1.2 copy-done
  219.0 4.0 %place.1 = bf16[1,384,3072]{2,1,0:T(8,128)(2,1)} custom-call(s32[1]{0:T(128)} %bitcast.1.side_ref, bf16[8,576,128]{2,1,0:T(8,128)(2,1)} %copy-done.1, bf16[4,1536,128]{2,1,0:T(8,128)(2,1)} %copy-done, bf16[4,1536,128]{2,1,0:T(8,128)(2,1)} %copy-done), custom_call_target="tpu_custom_call" | custom-call | tf_op jit(solution)/shard_map/place/pallas_call | solution.py:273
  (4 shorter events, 0.0 us)
Async XLA Ops:
  5.2 31.7 %all-to-all-start = ((bf16[8,976,128]{2,1,0:T(8,128)(2,1)}), bf16[8,976,128]{2,1,0:T(8,128)(2,1)S(1)}, u32[]{:S(2)}, u32[]{:S(2)}) async-start(bf16[8,976,128]{2,1,0:T(8,128)(2,1)} %pack_first.1), calls=%async_computation | async-start | bytes 3997696 | tf_op jit(solution)/shard_map/all_to_all | solution.py:301
  36.9 1.3 copy-start.3
  37.0 9.5 %collective-permute-start = (bf16[8,192,128]{2,1,0:T(8,128)(2,1)S(1)}, bf16[8,192,128]{2,1,0:T(8,128)(2,1)S(1)}, u32[]{:S(2)}, u32[]{:S(2)}) collective-permute-start(bf16[8,192,128]{2,1,0:T(8,128)(2,1)S(1)} %slice.9), channel_id=1, source_target_pairs={{0,1},{1,0},{2,3},{3,2},{4,5},{5,4},{6,7},{7,6},{8,9},{9,8},{10,11... | collective-permute-start | bytes 1179656 | tf_op jit(solution)/shard_map/ppermute | solution.py:304
  38.2 31.9 %all-to-all-start.1 = ((bf16[8,960,128]{2,1,0:T(8,128)(2,1)}), bf16[8,960,128]{2,1,0:T(8,128)(2,1)}, u32[]{:S(2)}, u32[]{:S(2)}) async-start(bf16[8,960,128]{2,1,0:T(8,128)(2,1)} %get-tuple-element.36), calls=%async_computation.1 | async-start | bytes 3932160 | tf_op jit(solution)/shard_map/all_to_all | solution.py:301
  46.4 0.7 copy-start.8
  71.1 7.1 %collective-permute-start.2 = (bf16[8,192,128]{2,1,0:T(8,128)(2,1)S(1)}, bf16[8,192,128]{2,1,0:T(8,128)(2,1)S(1)}, u32[]{:S(2)}, u32[]{:S(2)}) collective-permute-start(bf16[8,192,128]{2,1,0:T(8,128)(2,1)S(1)} %slice.10), channel_id=1, source_target_pairs={{0,1},{1,0},{2,3},{3,2},{4,5},{5,4},{6,7},{7,6},{8,9},{9,8},{10,11... | collective-permute-start | bytes 1179656 | tf_op jit(solution)/shard_map/ppermute | solution.py:304
  71.2 32.4 %collective-permute-start.1 = (bf16[8,192,128]{2,1,0:T(8,128)(2,1)}, bf16[8,192,128]{2,1,0:T(8,128)(2,1)S(1)}, u32[]{:S(2)}, u32[]{:S(2)}) collective-permute-start(bf16[8,192,128]{2,1,0:T(8,128)(2,1)} %get-tuple-element.35), channel_id=1, source_target_pairs={{0,1},{1,0},{2,3},{3,2},{4,5},{5,4},{6,7},{7,6},{8,9},{9,8},{10,11... | collective-permute-start | bytes 1179656 | tf_op jit(solution)/shard_map/ppermute | solution.py:304
  71.7 31.1 %all-to-all-start.2 = ((bf16[8,960,128]{2,1,0:T(8,128)(2,1)}), bf16[8,960,128]{2,1,0:T(8,128)(2,1)S(1)}, u32[]{:S(2)}, u32[]{:S(2)}) async-start(bf16[8,960,128]{2,1,0:T(8,128)(2,1)} %get-tuple-element.42), calls=%async_computation.2 | async-start | bytes 3932160 | tf_op jit(solution)/shard_map/all_to_all | solution.py:301
  78.2 0.7 copy-start.7
  79.0 24.7 %copy-start.5 = (bf16[8,192,128]{2,1,0:T(8,128)(2,1)S(1)}, bf16[8,192,128]{2,1,0:T(8,128)(2,1)}, u32[]{:S(2)}) copy-start(bf16[8,192,128]{2,1,0:T(8,128)(2,1)} %get-tuple-element.34) | copy-start | bytes 1179652
  100.9 12.4 %collective-permute-start.3 = (bf16[8,192,128]{2,1,0:T(8,128)(2,1)}, bf16[8,192,128]{2,1,0:T(8,128)(2,1)}, u32[]{:S(2)}, u32[]{:S(2)}) collective-permute-start(bf16[8,192,128]{2,1,0:T(8,128)(2,1)} %get-tuple-element.40), channel_id=1, source_target_pairs={{0,1},{1,0},{2,3},{3,2},{4,5},{5,4},{6,7},{7,6},{8,9},{9,8},{10,11... | collective-permute-start | bytes 1179656 | tf_op jit(solution)/shard_map/ppermute | solution.py:304
  102.8 12.6 %copy-start.4 = (bf16[8,960,128]{2,1,0:T(8,128)(2,1)}, bf16[8,960,128]{2,1,0:T(8,128)(2,1)S(1)}, u32[]{:S(2)}) copy-start(bf16[8,960,128]{2,1,0:T(8,128)(2,1)S(1)} %all-to-all-done.2.q_ref.d_ref.own_ref) | copy-start | bytes 5898244
  102.8 10.5 %copy-start.6 = (bf16[8,192,128]{2,1,0:T(8,128)(2,1)S(1)}, bf16[8,192,128]{2,1,0:T(8,128)(2,1)}, u32[]{:S(2)}) copy-start(bf16[8,192,128]{2,1,0:T(8,128)(2,1)} %get-tuple-element.39) | copy-start | bytes 1179652
  103.6 20.4 %collective-permute-start.4 = (bf16[8,192,128]{2,1,0:T(8,128)(2,1)}, bf16[8,192,128]{2,1,0:T(8,128)(2,1)}, u32[]{:S(2)}, u32[]{:S(2)}) collective-permute-start(bf16[8,192,128]{2,1,0:T(8,128)(2,1)} %slice.11), channel_id=1, source_target_pairs={{0,1},{1,0},{2,3},{3,2},{4,5},{5,4},{6,7},{7,6},{8,9},{9,8},{10,11... | collective-permute-start | bytes 1179656 | tf_op jit(solution)/shard_map/ppermute | solution.py:304
  103.8 42.2 %collective-permute-start.6 = (bf16[4,384,128]{2,1,0:T(8,128)(2,1)}, bf16[4,384,128]{2,1,0:T(8,128)(2,1)S(1)}, u32[]{:S(2)}, u32[]{:S(2)}) collective-permute-start(bf16[4,384,128]{2,1,0:T(8,128)(2,1)} %get-tuple-element.43), channel_id=1, source_target_pairs={{16,0},{17,1},{18,2},{19,3},{20,4},{21,5},{22,6},{23,7},{24,8},{25... | collective-permute-start | bytes 1179656 | tf_op jit(solution)/shard_map/ppermute | solution.py:312
  106.4 39.5 %collective-permute-start.7 = (bf16[4,384,128]{2,1,0:T(8,128)(2,1)}, bf16[4,384,128]{2,1,0:T(8,128)(2,1)S(1)}, u32[]{:S(2)}, u32[]{:S(2)}) collective-permute-start(bf16[4,384,128]{2,1,0:T(8,128)(2,1)} %get-tuple-element.52), channel_id=1, source_target_pairs={{16,8},{17,9},{18,10},{19,11},{20,12},{21,13},{22,14},{23,15},{24,... | collective-permute-start | bytes 1179656 | tf_op jit(solution)/shard_map/ppermute | solution.py:312
  110.7 39.2 %collective-permute-start.5 = (bf16[8,384,128]{2,1,0:T(8,128)(2,1)}, bf16[8,384,128]{2,1,0:T(8,128)(2,1)S(1)}, u32[]{:S(2)}, u32[]{:S(2)}) collective-permute-start(bf16[8,384,128]{2,1,0:T(8,128)(2,1)} %get-tuple-element.49), channel_id=1, source_target_pairs={{16,0},{17,1},{18,2},{19,3},{20,4},{21,5},{22,6},{23,7},{24,8},{25... | collective-permute-start | bytes 2359304 | tf_op jit(solution)/shard_map/ppermute | solution.py:312
  115.4 34.5 %all-to-all-start.3 = ((bf16[8,384,128]{2,1,0:T(8,128)(2,1)}), bf16[8,384,128]{2,1,0:T(8,128)(2,1)S(1)}, u32[]{:S(2)}, u32[]{:S(2)}) async-start(bf16[8,384,128]{2,1,0:T(8,128)(2,1)} %pad_maximum_fusion.2), calls=%async_computation.3 | async-start | bytes 1572864 | tf_op jit(solution)/shard_map/all_to_all | solution.py:301
  149.9 1.9 collective-permute-start.8
  149.9 4.1 %copy-start.2 = (bf16[8,384,128]{2,1,0:T(8,128)(2,1)}, bf16[8,384,128]{2,1,0:T(8,128)(2,1)S(1)}, u32[]{:S(2)}) copy-start(bf16[8,384,128]{2,1,0:T(8,128)(2,1)S(1)} %all-to-all-done.3.refs_0_.refs_1_) | copy-start | bytes 2359300
  154.0 37.3 %all-to-all-start.4 = ((bf16[8,576,128]{2,1,0:T(8,128)(2,1)}), bf16[8,576,128]{2,1,0:T(8,128)(2,1)S(1)}, u32[]{:S(2)}, u32[]{:S(2)}) async-start(bf16[8,576,128]{2,1,0:T(8,128)(2,1)} %pad_maximum_fusion.1), calls=%async_computation.4 | async-start | bytes 2359296 | tf_op jit(solution)/shard_map/all_to_all | solution.py:301
  161.2 28.7 %collective-permute-start.9 = (bf16[4,384,128]{2,1,0:T(8,128)(2,1)}, bf16[4,384,128]{2,1,0:T(8,128)(2,1)S(1)}, u32[]{:S(2)}, u32[]{:S(2)}) collective-permute-start(bf16[4,384,128]{2,1,0:T(8,128)(2,1)} %get-tuple-element.57), channel_id=1, source_target_pairs={{16,0},{17,1},{18,2},{19,3},{20,4},{21,5},{22,6},{23,7},{24,8},{25... | collective-permute-start | bytes 1179656 | tf_op jit(solution)/shard_map/ppermute | solution.py:312
  163.1 27.0 %collective-permute-start.10 = (bf16[4,384,128]{2,1,0:T(8,128)(2,1)}, bf16[4,384,128]{2,1,0:T(8,128)(2,1)S(1)}, u32[]{:S(2)}, u32[]{:S(2)}) collective-permute-start(bf16[4,384,128]{2,1,0:T(8,128)(2,1)} %get-tuple-element.59), channel_id=1, source_target_pairs={{16,8},{17,9},{18,10},{19,11},{20,12},{21,13},{22,14},{23,15},{24,... | collective-permute-start | bytes 1179656 | tf_op jit(solution)/shard_map/ppermute | solution.py:312
  191.4 5.6 %copy-start.1 = (bf16[8,576,128]{2,1,0:T(8,128)(2,1)}, bf16[8,576,128]{2,1,0:T(8,128)(2,1)S(1)}, u32[]{:S(2)}) copy-start(bf16[8,576,128]{2,1,0:T(8,128)(2,1)S(1)} %all-to-all-done.4.refs_2_.refs_0_) | copy-start | bytes 3538948
  191.4 26.4 %all-to-all-start.5 = ((bf16[4,1536,128]{2,1,0:T(8,128)(2,1)}), bf16[4,1536,128]{2,1,0:T(8,128)(2,1)S(1)}, u32[]{:S(2)}, u32[]{:S(2)}) async-start(bf16[4,1536,128]{2,1,0:T(8,128)(2,1)} %pad_maximum_fusion), calls=%async_computation.5 | async-start | bytes 3145728 | tf_op jit(solution)/shard_map/all_to_all | solution.py:301
  217.8 1.2 copy-start
